TPU v7x, 32 devices: a whole 2x2x4 slice. The times are simulated.
32 devices in a mesh: gx: 4 (over y, x), gy: 2 (over core), gz: 4 (over z).
Axes of the slice: x: 2, y: 2, z: 4, core: 2. Of those that a mesh axis runs over, the one named last changes fastest.
Arguments:
- density: float32 [96, 128, 512], P('gx', 'gy', 'gz'), may hold values from 0.8 to 1.25
- momentum: float32 [3, 96, 128, 512], P(None, 'gx', 'gy', 'gz'), may hold values from -1.5 to 1.5
- energy: float32 [96, 128, 512], P('gx', 'gy', 'gz'), may hold values from 2 to 3
- increment: float32 [5, 96, 128, 512], P(None, 'gx', 'gy', 'gz'), may hold values from -1.8 to 1.8
Outputs:
- new_state: float32 [5, 96, 128, 512], P(None, 'gx', 'gy', 'gz')
- new_increment: float32 [5, 96, 128, 512], P(None, 'gx', 'gy', 'gz')
All inputs are finite; a program needn't handle non-finite values.
Results may differ from a plain program's by a relative error of at most 0.0003.
Values sent between devices are 32-bit elements; how exact they have to be, the bound alone decides.
No kernel may reach another device: no remote copies, remote signals or barrier semaphores. Data moves between devices by JAX's collectives and lax.ppermute only.
A program may use at most 128 MiB of HBM per device.

v0:
```python
import functools
import math

import jax
import jax.numpy as jnp
import numpy as np
from jax import lax
from jax.experimental import pallas as pl
from jax.experimental.pallas import tpu as pltpu
from jax.sharding import PartitionSpec as P

deriv_alpha = 1.0 / 3.0
filter_alpha = 0.4999
gas_gamma = 1.4
time_step = 0.2
section_a = -5.0 / 9.0
section_b = 15.0 / 16.0
explicit_weights = (0.75, -0.15, 1.0 / 60.0)
f32 = jnp.float32


def root_of(coupling):
    return (-1.0 + math.sqrt(1.0 - 4.0 * coupling * coupling)) / (2.0 * coupling)


def laurent(poly, times_s):
    size = len(poly) + 1
    total = np.zeros(2 * size + 1)
    for power, value in enumerate(poly):
        term = np.array([1.0])
        for _ in range(power):
            term = np.convolve(term, [1.0, 0.0, 1.0])
        if times_s:
            term = np.convolve(term, [-1.0, 0.0, 1.0])
        half = len(term) // 2
        total[size - half : size + half + 1] += value * term
    return [float(v) for v in total[size:]]


def x_constants():
    ad, af = deriv_alpha, filter_alpha
    kappa = (1.0 / 36.0) / ad
    beta = 7.0 / 9.0 - kappa
    poly = np.polynomial.polynomial
    p_of_c = (1.0 - 2.0 * af) / 256.0 * poly.polypow([2.0, -1.0], 4)
    q_of_c, rest = poly.polydiv(p_of_c, [1.0, af])
    rho = float(rest[0])
    both = poly.polymul([1.0, af], [1.0, ad])
    q2_of_c, _ = poly.polydiv(p_of_c, both)
    mu_f = float(poly.polyval(-1.0 / af, p_of_c)) / (1.0 - ad / af)
    mu_d = float(poly.polyval(-1.0 / ad, p_of_c)) / (1.0 - af / ad)
    b_of_c = poly.polyadd(kappa * q_of_c, beta * q2_of_c)
    g = 1.0 / math.sqrt(1.0 - 4.0 * af * af)
    sigma = -section_b * time_step
    return dict(
        kappa=kappa,
        deriv=beta / ad,
        band_q=laurent(q_of_c, False)[:4],
        band_f=[sigma * v for v in laurent(b_of_c, True)[:5]],
        own=rho * g,
        pair=sigma * (kappa * rho + beta * mu_f) / af,
        slow=sigma * beta * mu_d / ad,
    )


X = x_constants()
ROOT_D = root_of(deriv_alpha)
ROOT_F = root_of(filter_alpha)


def primitives(cells):
    density, m0, m1, m2, energy = cells
    inverse = 1.0 / density
    squared = m0 * m0 + m1 * m1 + m2 * m2
    pressure = (gas_gamma - 1.0) * (energy - 0.5 * squared * inverse)
    return inverse, pressure


def flux(cells, inverse, pressure, axis_k):
    momentum = cells[1:4]
    velocity = momentum[axis_k] * inverse
    parts = [
        momentum[axis_k],
        momentum[0] * velocity,
        momentum[1] * velocity,
        momentum[2] * velocity,
        (cells[4] + pressure) * velocity,
    ]
    parts[axis_k + 1] = parts[axis_k + 1] + pressure
    return parts


def lanes(shape):
    return lax.broadcasted_iota(jnp.int32, shape, len(shape) - 1)


def roll(value, amount):
    size = value.shape[-1]
    if isinstance(amount, int):
        amount = amount % size
        if amount == 0:
            return value
    return pltpu.roll(value, amount, value.ndim - 1)


def cells_at(rho, mom, ene, x, at):
    return [rho[x, at], mom[0, x, at], mom[1, x, at], mom[2, x, at], ene[x, at]]


class Blocks:
    def __init__(self, sources, targets, sems, dims, size, begin=0):
        self.copies = []
        for k in range(targets[0].shape[dims[0]] // size):
            piece = []
            for n, (source, target, dim) in enumerate(zip(sources, targets, dims)):
                lead = (slice(None),) * dim
                there = source.at[(*lead, pl.ds(begin + k * size, size))]
                here = target.at[(*lead, pl.ds(k * size, size))]
                piece.append(pltpu.make_async_copy(there, here, sems.at[n, k]))
            self.copies.append(piece)
        for piece in self.copies:
            for copy in piece:
                copy.start()

    def wait(self, k):
        for copy in self.copies[k]:
            copy.wait()


def cells_at(rho, mom, ene, x, at):
    return [rho[x, at], mom[0, x, at], mom[1, x, at], mom[2, x, at], ene[x, at]]


def face_kernel(
    rho_hbm, mom_hbm, ene_hbm,
    up, down, own, g_rows, h_rows, z_up, z_down, z_own, y_edge, token,
    rho, mom, ene, sems,
):
    nx, ny, nz = rho.shape
    lane = lanes((8, nz))
    slot = lane // 8
    first_half = lane % 8 < 4
    row = lax.broadcasted_iota(jnp.int32, (8, nz), 0)
    stored = {x: r for r, x in enumerate((0, 1, 2, nx - 3, nx - 2, nx - 1))}
    rows = 16
    blocks = Blocks((rho_hbm, mom_hbm, ene_hbm), (rho, mom, ene), sems, (1, 2, 1), rows)
    token[...] = jnp.zeros_like(token)

    def tile(t, _):
        at = pl.ds(pl.multiple_of(8 * t, 8), 8)
        keep = (row < 4) & (t > 0)
        packed = [[None] * 5, [None] * 5]
        totals = lower = upper = None
        for x in range(nx):
            cells = cells_at(rho, mom, ene, x, at)
            inverse, pressure = primitives(cells)
            f = flux(cells, inverse, pressure, 0)
            g = flux(cells, inverse, pressure, 1)
            h = flux(cells, inverse, pressure, 2)
            group, place = x // 16, x % 16
            for v in range(5):
                y_edge[v, x] = jnp.where(keep, y_edge[v, x], g[v])
                moved = roll(cells[v], 8 * place + 3)
                if place:
                    moved = jnp.where(slot == place, moved, packed[group][v])
                packed[group][v] = moved
                if x in stored:
                    g_rows[stored[x], v, at] = g[v]
                    h_rows[stored[x], v, at] = h[v]
                if x == 0:
                    down[0, v, at] = f[v]
                if x == nx - 1:
                    up[0, v, at] = f[v]
            if x == 0:
                totals, lower, upper = [g, h, g, h], f, f
            else:
                lower = [ROOT_D * a + b for a, b in zip(lower, f)]
                upper = [a + ROOT_D**x * b for a, b in zip(upper, f)]
                factor = ROOT_F**x
                totals = [
                    [ROOT_F * a + b if k < 2 else a + factor * b for a, b in zip(total, term)]
                    for k, (total, term) in enumerate(zip(totals, (g, h, g, h)))
                ]
        h = [flux(packed[group], *primitives(packed[group]), 2) for group in range(2)]
        for v in range(5):
            up[1, v, at] = own[0, v, at] = lower[v]
            down[1, v, at] = own[1, v, at] = upper[v]
            for k in range(2):
                g_rows[6 + k, v, at] = totals[2 * k][v]
                h_rows[6 + k, v, at] = totals[2 * k + 1][v]
                y_edge[v, nx + k] = jnp.where(keep, y_edge[v, nx + k], totals[2 * k][v])
                group, place = (nx + k) // 16, (nx + k) % 16
                moved = roll(totals[2 * k + 1][v], 8 * place + 3)
                h[group][v] = jnp.where(slot == place, moved, h[group][v])
            for group in range(2):
                z_own[group, v, at] = h[group][v]
            z_up[v, at] = jnp.where(first_half, h[0][v], roll(h[1][v], 4))
            z_down[v, at] = jnp.where(first_half, roll(h[0][v], -3), roll(h[1][v], 1))
        return 0

    for k in range(ny // rows):
        blocks.wait(k)
        lax.fori_loop(k * rows // 8, (k + 1) * rows // 8, tile, 0)


def base_kernel(rho_hbm, mom_hbm, ene_hbm, inc_hbm, after, base, w_up, w_down, rho, mom, ene, inc, sems):
    nx, ny, nz = rho.shape
    rows = 16
    blocks = Blocks((rho_hbm, mom_hbm, ene_hbm, inc_hbm), (rho, mom, ene, inc), sems, (1, 2, 1, 2), rows)

    def tile(t, _):
        at = pl.ds(pl.multiple_of(8 * t, 8), 8)
        totals = None
        ends = {1.0: [[None] * 5 for _ in range(3)], -1.0: [[None] * 5 for _ in range(3)]}
        for x in range(nx):
            cells = cells_at(rho, mom, ene, x, at)
            f = flux(cells, *primitives(cells), 0)
            q = [cells[v] + (section_a * section_b) * inc[v, x, at] for v in range(5)]
            own = [X["own"] * q[v] for v in range(5)]
            pair = [X["pair"] * f[v] for v in range(5)]
            plus = [a + b for a, b in zip(own, pair)]
            minus = [a - b for a, b in zip(own, pair)]
            if x == 0:
                totals = [plus, minus]
            else:
                totals[0] = [ROOT_F * a + b for a, b in zip(totals[0], plus)]
                totals[1] = [a + ROOT_F**x * b for a, b in zip(totals[1], minus)]
            for sign, j in ((1.0, x + 1), (-1.0, nx - x)):
                for k in range(3):
                    n = k + j
                    if n > 4:
                        continue
                    for v in range(5):
                        term = (sign * X["band_f"][n]) * f[v]
                        if n <= 3:
                            term = term + X["band_q"][n] * q[v]
                        so_far = ends[sign][k][v]
                        ends[sign][k][v] = term if so_far is None else so_far + term
            if x == 3:
                for k in range(3):
                    for v in range(5):
                        w_down[k, v, at] = ends[1.0][k][v]
        for v in range(5):
            base[0, v, at] = totals[0][v]
            base[1, v, at] = totals[1][v]
            for k in range(3):
                w_up[k, v, at] = ends[-1.0][k][v]
        return 0

    for k in range(ny // rows):
        blocks.wait(k)
        lax.fori_loop(k * rows // 8, (k + 1) * rows // 8, tile, 0)


def fix_table(nz):
    weight = {1: 45.0, 2: -9.0, 3: 1.0}
    table = np.zeros((4 * nz, 2 * nz))
    for group in range(2):
        for place in range(nz // 8):
            into = group * nz + 8 * place
            came = 8 * place + 4 * group
            kept = (2 + group) * nz + 8 * place
            for j in range(3):
                for n, w in weight.items():
                    if j + n >= 3:
                        table[nz + came + j + n - 3, into + j] += w
                        table[kept + 3 + j + n - 3, into + j] -= w
                    if n > j:
                        table[came + 3 + j - n, into + 3 + j] -= w
                        table[kept + 3 + j - n, into + 3 + j] += w
    return table


def split(value):
    high = value.astype(jnp.bfloat16)
    return high, (value - high.astype(f32)).astype(jnp.bfloat16)


def around(at):
    return 45.0 * (at(1) - at(-1)) - 9.0 * (at(2) - at(-2)) + (at(3) - at(-3))


def turn_of(x, nz):
    if isinstance(x, int):
        return (2 * nz - 3 - 8 * (x % 16)) % nz
    return lax.rem(2 * nz - 3 - 8 * lax.rem(x, 16), nz)


def end_kernel(
    base, w_up0, w_down0, g_rows, h_rows, y_halo, z_low, z_high, z_own, table,
    sums, own_sums, w_up, w_down, fix, pad, dz_all,
):
    ny, nz = base.shape[2:]
    nx = y_halo.shape[1] - 2
    lane = lanes((8, nz))
    edge_lane = (lane < 3) | (lane >= nz - 3)
    parts = [z_low[...], z_high[...], z_own[0], z_own[1]]
    halves = [split(p.reshape(5 * ny, nz)) for p in parts]
    fixed = sum(
        jnp.dot(jnp.concatenate([h[k] for h in halves], axis=1), table[...], preferred_element_type=f32)
        for k in range(2)
    )
    for group in range(2):
        fix[group] = fixed[:, group * nz : group * nz + nz].reshape(5, ny, nz)
    rows = [0, 1, 2, nx - 3, nx - 2, nx - 1, nx, nx + 1]
    for r, x in enumerate(rows):
        for v in range(5):
            pad[r, v, 0:8] = y_halo[v, x]
            pad[r, v, ny + 8 : ny + 16] = y_halo[v, x]

    def first(t, _):
        at = pl.ds(pl.multiple_of(8 * t, 8), 8)
        inside = pl.ds(pl.multiple_of(8 * t + 8, 8), 8)
        for r, x in enumerate(rows):
            for v in range(5):
                h = h_rows[r, v, at]
                pad[r, v, inside] = g_rows[r, v, at]
                moved = roll(fix[x // 16, v, at], turn_of(x, nz))
                dz_all[r, v, at] = around(lambda n: roll(h, -n)) + jnp.where(edge_lane, moved, 0.0)
        return 0

    lax.fori_loop(0, ny // 8, first, 0)
    scale = -time_step * section_b / 60.0

    for t in range(ny // 8):
        at = slice(8 * t, 8 * t + 8)

        def cross(r, v, t=t):
            dy = around(lambda n: pad[r, v, 8 + 8 * t + n : 16 + 8 * t + n])
            return scale * (dy + dz_all[r, v, slice(8 * t, 8 * t + 8)])

        for v in range(5):
            for k in range(2):
                sums[k, v, at] = own_sums[k, v, at] = base[k, v, at] + X["own"] * cross(6 + k, v)
            for out, begin, near in ((w_down, w_down0, (0, 1, 2)), (w_up, w_up0, (5, 4, 3))):
                q = [cross(r, v) for r in near]
                for k in range(3):
                    total = begin[k, v, at]
                    for j in range(1, 4 - k):
                        total = total + X["band_q"][k + j] * q[j - 1]
                    out[k, v, at] = total


def part_kernel(begin, rho_hbm, mom_hbm, ene_hbm, inc_hbm, y_halo, fix, *rest):
    part, token, rho, mom, ene, inc, pad, sems = rest[-8:]
    token[...] = jnp.zeros_like(token)
    nx, ny, nz = rho.shape
    lane = lanes((8, nz))
    edge_lane = (lane < 3) | (lane >= nz - 3)
    scale = -time_step / 60.0
    some = 4
    blocks = Blocks((rho_hbm, mom_hbm, ene_hbm, inc_hbm), (rho, mom, ene, inc), sems, (0, 1, 0, 1), some, begin)

    def one_row(x, _):
        turn = turn_of(begin + x, nz)
        group = (begin + x) // 16
        for v in range(5):
            pad[v, 0:8] = y_halo[v, begin + x]
            pad[v, ny + 8 : ny + 16] = y_halo[v, begin + x]
        for t in range(ny // 8):
            at = slice(8 * t, 8 * t + 8)
            cells = cells_at(rho, mom, ene, x, at)
            inverse, pressure = primitives(cells)
            g = flux(cells, inverse, pressure, 1)
            h = flux(cells, inverse, pressure, 2)
            for v in range(5):
                pad[v, 8 + 8 * t : 16 + 8 * t] = g[v]
                dz = around(lambda n, v=v: roll(h[v], -n))
                dz = dz + jnp.where(edge_lane, roll(fix[group, v, at], turn), 0.0)
                part[v, x, at] = section_a * inc[v, x, at] + scale * dz
        for t in range(ny // 8):
            at = slice(8 * t, 8 * t + 8)
            for v in range(5):
                dy = around(lambda n, v=v, t=t: pad[v, 8 + 8 * t + n : 16 + 8 * t + n])
                part[v, x, at] = part[v, x, at] + scale * dy
        return 0

    for k in range(nx // some):
        blocks.wait(k)
        lax.fori_loop(k * some, (k + 1) * some, one_row, 0)


def line_kernel(
    rho_hbm, mom_hbm, ene_hbm, edges, near, part0, part1,
    new_inc, local,
    rho, mom, ene, f_all, q_all, e_all, sems,
):
    nx, ny, nz = rho.shape
    rows = 16
    blocks = Blocks((rho_hbm, mom_hbm, ene_hbm), (rho, mom, ene), sems, (1, 2, 1), rows)
    for k in range(ny // rows):
        blocks.wait(k)
        at = slice(k * rows, (k + 1) * rows)

        def fluxes_at(x, _, at=at, part=part0, begin=0):
            cells = cells_at(rho, mom, ene, begin + x, at)
            for v, value in enumerate(flux(cells, *primitives(cells), 0)):
                f_all[v, begin + x] = value
                q_all[v, begin + x] = cells[v] + section_b * part[v, x, at]
            return 0

        lax.fori_loop(0, nx // 2, fluxes_at, 0)
        lax.fori_loop(0, nx // 2, functools.partial(fluxes_at, part=part1, begin=nx // 2), 0)
        lax.fori_loop(0, 5, functools.partial(one_line, at, (part0, part1), edges, near, new_inc, local, f_all, q_all, e_all), 0)


def one_line(at, part, edges, near, new_inc, local, f_all, q_all, e_all, v, _):
    nx = f_all.shape[1]
    f = [f_all[v, x] for x in range(nx)]
    q = [q_all[v, x] for x in range(nx)]
    low, high = edges[0, v, at], edges[1, v, at]
    forward = ROOT_D * near[0, v, at]
    for x in range(nx):
        e_all[x] = forward
        forward = ROOT_D * (f[x] + forward)
    backward = ROOT_D * near[1, v, at]
    for x in reversed(range(nx)):
        e_all[x] = e_all[x] - backward
        backward = ROOT_D * (f[x] + backward)
    ahead = None
    for x in range(nx):
        before = low if x == 0 else f[x - 1]
        after = high if x == nx - 1 else f[x + 1]
        e = e_all[x]
        deriv = X["kappa"] * (after - before) + X["deriv"] * e
        new_inc[v, x, at] = part[x // (nx // 2)][v, x % (nx // 2), at] - time_step * deriv
        total = (1.0 - X["band_q"][0] - X["own"]) * q[x] - X["slow"] * e
        total = total - (section_b * time_step) * deriv
        for n in range(1, 4):
            near = [q[i] for i in (x - n, x + n) if 0 <= i < nx]
            total = total - X["band_q"][n] * (near[0] if len(near) == 1 else near[0] + near[1])
        for n in range(1, 5):
            if x + n < nx and x - n >= 0:
                total = total - X["band_f"][n] * (f[x + n] - f[x - n])
            elif x + n < nx:
                total = total - X["band_f"][n] * f[x + n]
            else:
                total = total + X["band_f"][n] * f[x - n]
        if x == 3:
            total = total + X["band_f"][4] * low
        if x == nx - 4:
            total = total - X["band_f"][4] * high
        if ahead is not None:
            total = total - ahead
        local[v, x, at] = total
        plus = X["own"] * q[x] + X["pair"] * f[x]
        ahead = ROOT_F * (plus if ahead is None else plus + ahead)
    behind = None
    for x in reversed(range(nx)):
        if behind is not None:
            local[v, x, at] = local[v, x, at] - behind
        minus = X["own"] * q[x] - X["pair"] * f[x]
        behind = ROOT_F * (minus if behind is None else minus + behind)
    return 0


def mix_kernel(members, nx, own, from_low, from_high, after, onward, near, edges, token):
    token[...] = jnp.zeros_like(token)
    rate = ROOT_D**nx
    closure = 1.0 / (1.0 - rate**members)
    for k, came in enumerate((from_low, from_high)):
        onward[k] = own[k] + rate * came[1]
        near[k] = closure * (came[1] + rate ** (members - 1) * own[k])
        edges[k] = came[0]


def pair_kernel(nx, own, opposite, after, up, down, rest):
    rate = ROOT_F**nx
    closure = 1.0 / (1.0 - rate**4)
    up[...] = own[0] + rate**2 * opposite[0]
    down[...] = own[1] + rate**2 * opposite[1]
    rest[...] = (closure * rate) * opposite[...] + (closure * rate**3) * own[...]


def far_part(members, nx, x, across, v):
    rate = ROOT_D**nx
    closure = 1.0 / (1.0 - rate**members)
    low, high = across[0, v], across[1, v]
    return (closure * rate * ROOT_D ** (x + 1)) * low - (closure * rate * ROOT_D ** (nx - x)) * high


def register_kernel(members, new_inc, across, local, w_low, w_high, out_hbm, rim, out, sems):
    nx = new_inc.shape[1]
    for k in range(3):
        for v in range(5):
            rim[k, v] = local[v, k] - w_low[k, v]
            rim[5 - k, v] = local[v, nx - 1 - k] - w_high[k, v]
    done = []
    for v in range(5):
        for x in range(nx):
            e = far_part(members, nx, x, across, v)
            out[v, x] = new_inc[v, x] - (time_step * X["deriv"]) * e
        copy = pltpu.make_async_copy(out.at[v], out_hbm.at[v], sems.at[v])
        copy.start()
        done.append(copy)
    for copy in done:
        copy.wait()


def final_kernel(members, local, rim, across, incoming, out_hbm, out, sems):
    nx = local.shape[1]
    through = -section_b * time_step * X["deriv"] - X["slow"]
    done = []
    for v in range(5):
        low, high = incoming[0, v], incoming[1, v]
        for x in range(nx):
            value = local[v, x] if 3 <= x < nx - 3 else rim[x if x < 3 else x - nx + 6, v]
            value = value + through * far_part(members, nx, x, across, v)
            value = value - (ROOT_F ** (x + 1)) * low - (ROOT_F ** (nx - x)) * high
            out[v, x] = value
        copy = pltpu.make_async_copy(out.at[v], out_hbm.at[v], sems.at[v])
        copy.start()
        done.append(copy)
    for copy in done:
        copy.wait()


def shifted(value, axis, by):
    size = lax.axis_size(axis)
    return lax.ppermute(value, axis, [(i, (i + by) % size) for i in range(size)])


def ring_sums(own, rate):
    size = lax.axis_size("gx")
    gathered = lax.all_gather(own, "gx", axis=0)
    here = lax.axis_index("gx")
    member = jnp.arange(size, dtype=jnp.int32)
    table = jnp.asarray([rate**k / (1.0 - rate**size) for k in range(size)], f32)
    up = table[(here - 1 - member) % size]
    down = table[(member - here - 1) % size]
    shape = (size,) + (1,) * (own.ndim - 1)
    low = jnp.sum(up.reshape(shape) * gathered[:, 0], axis=0)
    high = jnp.sum(down.reshape(shape) * gathered[:, 1], axis=0)
    return jnp.stack([low, high])


def call(kernel, name, inputs, hbm, outputs, scratch):
    place = {True: pl.BlockSpec(memory_space=pltpu.HBM), False: pl.BlockSpec(memory_space=pltpu.VMEM)}
    shapes = [dims[1] if dims[0] == "hbm" else dims for dims in outputs]
    return pl.pallas_call(
        kernel,
        in_specs=[place[i < hbm] for i in range(len(inputs))],
        out_specs=[place[dims[0] == "hbm"] for dims in outputs],
        out_shape=[jax.ShapeDtypeStruct(dims, f32) for dims in shapes],
        scratch_shapes=scratch,
        compiler_params=pltpu.CompilerParams(vmem_limit_bytes=40 * 2**20),
        cost_estimate=pl.CostEstimate(flops=1000, bytes_accessed=1000, transcendentals=0),
        name=name,
    )(*[pltpu.with_memory_space_constraint(a, pltpu.HBM) if i < hbm else a for i, a in enumerate(inputs)])


def on_device(density, momentum, energy, increment):
    nx, ny, nz = density.shape
    members = lax.axis_size("gx")
    cells = nx * ny * nz
    state = (density, momentum, energy)
    face = (5, ny, nz)
    whole = (5, nx, ny, nz)

    def vmem(*dims):
        return pltpu.VMEM(dims, f32)

    def sems(*dims):
        return pltpu.SemaphoreType.DMA(dims)

    state_room = [vmem(nx, ny, nz), vmem(3, nx, ny, nz), vmem(nx, ny, nz)]

    up, down, own, g_rows, h_rows, z_up, z_down, z_own, y_edge, begun = call(
        face_kernel,
        "faces",
        state,
        3,
        [(2, *face), (2, *face), (2, *face), (8, *face), (8, *face), face, face, (2, *face), (5, nx + 2, 8, nz), (8, nz)],
        state_room + [sems(3, ny // 16)],
    )
    from_low = shifted(up, "gx", 1)
    from_high = shifted(down, "gx", -1)
    z_low = shifted(z_up, "gz", 1)
    z_high = shifted(z_down, "gz", -1)
    y_halo = shifted(y_edge, "gy", 1)

    base, w_up0, w_down0 = call(
        base_kernel,
        "base",
        (*state, increment, begun),
        4,
        [(2, *face), (3, *face), (3, *face)],
        state_room + [vmem(*whole), sems(4, ny // 16)],
    )
    table = jnp.asarray(fix_table(nz), jnp.bfloat16)
    sums, own_sums, w_up, w_down, fix = call(
        end_kernel,
        "ends",
        (base, w_up0, w_down0, g_rows, h_rows, y_halo, z_low, z_high, z_own, table),
        0,
        [(2, *face), (2, *face), (3, *face), (3, *face), (2, *face)],
        [vmem(8, 5, ny + 16, nz), vmem(8, *face)],
    )
    half = nx // 2
    half_room = [vmem(half, ny, nz), vmem(3, half, ny, nz), vmem(half, ny, nz), vmem(5, half, ny, nz)]
    part0, token = call(
        functools.partial(part_kernel, 0),
        "part0",
        (*state, increment, y_halo, fix),
        4,
        [(5, half, ny, nz), (8, nz)],
        half_room + [vmem(5, ny + 16, nz), sems(4, half // 4)],
    )
    onward, near, edges, mixed = call(
        functools.partial(mix_kernel, members, nx),
        "mix",
        (own, from_low, from_high, token),
        0,
        [(2, *face)] * 3 + [(8, nz)],
        [],
    )
    part1, token1 = call(
        functools.partial(part_kernel, half),
        "part1",
        (*state, increment, y_halo, fix, mixed),
        4,
        [(5, half, ny, nz), (8, nz)],
        half_room + [vmem(5, ny + 16, nz), sems(4, half // 4)],
    )

    rate_d, rate_f = ROOT_D**nx, ROOT_F**nx
    w_low = shifted(w_up, "gx", 1)
    w_high = shifted(w_down, "gx", -1)
    if members == 4:
        across = shifted(onward, "gx", 2)
        opposite = shifted(sums, "gx", 2)
        mixed_up, mixed_down, rest = call(
            functools.partial(pair_kernel, nx), "pair", (own_sums, opposite, token1), 0, [face, face, (2, *face)], []
        )
        beside = jnp.stack([shifted(mixed_up, "gx", 1), shifted(mixed_down, "gx", -1)])
        incoming = beside * (1.0 / (1.0 - rate_f**4)) + rest
    else:
        near = ring_sums(own, rate_d)
        across = jnp.zeros_like(near)
        incoming = ring_sums(sums, rate_f)

    new_local, local = call(
        line_kernel,
        "lines",
        (*state, edges, near, part0, part1),
        3,
        [whole, whole],
        state_room + [vmem(5, nx, 16, nz), vmem(5, nx, 16, nz), vmem(nx, 16, nz), sems(3, ny // 16)],
    )
    out_room = [vmem(*whole), sems(5)]
    new_increment, rim = call(
        functools.partial(register_kernel, members),
        "register",
        (new_local, across, local, w_low, w_high),
        0,
        [("hbm", whole), (6, *face)],
        out_room,
    )
    (new_state,) = call(
        functools.partial(final_kernel, members),
        "final",
        (local, rim, across, incoming),
        0,
        [("hbm", whole)],
        out_room,
    )
    return (new_state, new_increment)


def solution(mesh):
    in_specs = (
        P("gx", "gy", "gz"),
        P(None, "gx", "gy", "gz"),
        P("gx", "gy", "gz"),
        P(None, "gx", "gy", "gz"),
    )
    out_specs = (P(None, "gx", "gy", "gz"), P(None, "gx", "gy", "gz"))
    return jax.shard_map(
        on_device, mesh=mesh, in_specs=in_specs, out_specs=out_specs, check_vma=False
    )
```

profile of v0, /device:TPU:3, one launch (start us, length us, event | category | flops | bytes accessed | tf_op | source)
XLA Modules:
  0.0 63.8 jit_solution(13805786985492305111)
XLA Ops:
  0.6 5.5 %faces.1 = (f32[2,5,64,128]{3,2,1,0:T(8,128)S(1)}, f32[2,5,64,128]{3,2,1,0:T(8,128)S(1)}, f32[2,5,64,128]{3,2,1,0:T(8,128)S(1)}, f32[8,5,64,128]{3,2,1,0:T(8,128...) custom-call(f32[24,64,128]{2,1,0:T(8,128)} %rho_hbm.9, ...), custom_call_target="tpu_custom_call" | custom-call | flops 1000 | bytes 1000 | tf_op jit(solution)/shard_map/faces/pallas_call | solution.py:540
  6.2 0.7 %collective-permute-start.2 = (f32[5,26,8,128]{3,2,1,0:T(8,128)S(1)}, f32[5,26,8,128]{3,2,1,0:T(8,128)S(1)}, u32[]{:S(2)}, u32[]{:S(2)}) collective-permute-start(f32[5,26,8,128]{3,2,1,0:T(8,128)S(1)} %get-tuple-element.38), channel_id=1, source_target_pairs={{0,4},{4,0},{1,5},{5,1},{2,6},{6,2},{3,7},{7,3},{8,12},{12,8},{9,1... | collective-permute-start | bytes 1597448 | tf_op jit(solution)/shard_map/ppermute | solution.py:520
  6.9 1.3 %collective-permute-start.3 = (f32[5,64,128]{2,1,0:T(8,128)S(1)}, f32[5,64,128]{2,1,0:T(8,128)S(1)}, u32[]{:S(2)}, u32[]{:S(2)}) collective-permute-start(f32[5,64,128]{2,1,0:T(8,128)S(1)} %get-tuple-element.45), channel_id=1, source_target_pairs={{0,1},{1,2},{2,3},{3,0},{4,5},{5,6},{6,7},{7,4},{8,9},{9,10},{10,1... | collective-permute-start | bytes 491528 | tf_op jit(solution)/shard_map/ppermute | solution.py:520
  8.2 2.0 %collective-permute-start.4 = (f32[5,64,128]{2,1,0:T(8,128)S(1)}, f32[5,64,128]{2,1,0:T(8,128)S(1)}, u32[]{:S(2)}, u32[]{:S(2)}) collective-permute-start(f32[5,64,128]{2,1,0:T(8,128)S(1)} %get-tuple-element.46), channel_id=1, source_target_pairs={{0,3},{1,0},{2,1},{3,2},{4,7},{5,4},{6,5},{7,6},{8,11},{9,8},{10,9... | collective-permute-start | bytes 491528 | tf_op jit(solution)/shard_map/ppermute | solution.py:520
  10.2 1.2 %collective-permute-start = (f32[2,5,64,128]{3,2,1,0:T(8,128)S(1)}, f32[2,5,64,128]{3,2,1,0:T(8,128)S(1)}, u32[]{:S(2)}, u32[]{:S(2)}) collective-permute-start(f32[2,5,64,128]{3,2,1,0:T(8,128)S(1)} %get-tuple-element.36), channel_id=1, source_target_pairs={{0,8},{8,16},{16,24},{24,0},{1,9},{9,17},{17,25},{25,1},{2,10},{10... | collective-permute-start | bytes 983048 | tf_op jit(solution)/shard_map/ppermute | solution.py:520
  11.4 0.3 collective-permute-start.1
  11.7 4.1 %base.1 = (f32[2,5,64,128]{3,2,1,0:T(8,128)S(1)}, f32[3,5,64,128]{3,2,1,0:T(8,128)S(1)}, f32[3,5,64,128]{3,2,1,0:T(8,128)S(1)}) custom-call(f32[24,64,128]{2,1,0:T(8,128)} %rho_hbm.9, f32[3,24,64,128]{3,2,1,0:T(8,128)} %mom_hbm.9, f32[24,64,128]{2,1,0:T(8,128)} %ene_hbm.9, f32[5,24,64,128]{3,2,1,0:T(8,128)} %inc_hbm.5, f32[8,128]{1,0:T(8,128)S(1)} %get-tuple-element.39.after), custom_call_target="tpu_custom_call" | custom-call | flops 1000 | bytes 1000 | tf_op jit(solution)/shard_map/base/pallas_call | solution.py:540
  15.8 1.5 %collective-permute-done.4.z_high = f32[5,64,128]{2,1,0:T(8,128)S(1)} collective-permute-done((f32[5,64,128]{2,1,0:T(8,128)S(1)}, f32[5,64,128]{2,1,0:T(8,128)S(1)}, u32[]{:S(2)}, u32[]{:S(2)}) %collective-permute-start.4) | collective-permute-done | bytes 163872 | tf_op jit(solution)/shard_map/ppermute | solution.py:520
  17.3 0.0 collective-permute-done.2.y_halo
  17.3 3.9 %ends.1 = (f32[2,5,64,128]{3,2,1,0:T(8,128)S(1)}, f32[2,5,64,128]{3,2,1,0:T(8,128)S(1)}, f32[3,5,64,128]{3,2,1,0:T(8,128)S(1)}, f32[3,5,64,128]{3,2,1,0:T(8,128)S(1)}, f32[2,5,64,128]{3,2,1,0:T(8,128)S(1)}) custom-call(f32[2,5,64,128]{3,2,1,0:T(8,128)S(1)} %get-tuple-element.40.base, f32[3,5,64,128]{3,2,1,0:T(8,128)S(1)} %get-tuple-element.41.w_up0, ...), custom_call_target="tpu_custom_call" | custom-call | flops 1000 | bytes 1000 | tf_op jit(solution)/shard_map/ends/pallas_call | solution.py:540
  21.2 1.3 %collective-permute-start.8 = (f32[2,5,64,128]{3,2,1,0:T(8,128)S(1)}, f32[2,5,64,128]{3,2,1,0:T(8,128)S(1)}, u32[]{:S(2)}, u32[]{:S(2)}) collective-permute-start(f32[2,5,64,128]{3,2,1,0:T(8,128)S(1)} %get-tuple-element.62), channel_id=1, source_target_pairs={{0,16},{8,24},{16,0},{24,8},{1,17},{9,25},{17,1},{25,9},{2,18},{10... | collective-permute-start | bytes 983048 | tf_op jit(solution)/shard_map/ppermute | solution.py:520
  22.5 0.2 collective-permute-start.6
  22.7 1.3 %collective-permute-start.7 = (f32[3,5,64,128]{3,2,1,0:T(8,128)S(1)}, f32[3,5,64,128]{3,2,1,0:T(8,128)S(1)}, u32[]{:S(2)}, u32[]{:S(2)}) collective-permute-start(f32[3,5,64,128]{3,2,1,0:T(8,128)S(1)} %get-tuple-element.59), channel_id=1, source_target_pairs={{0,24},{8,0},{16,8},{24,16},{1,25},{9,1},{17,9},{25,17},{2,26},{10... | collective-permute-start | bytes 1474568 | tf_op jit(solution)/shard_map/ppermute | solution.py:520
  24.0 6.0 %part0.1 = (f32[5,12,64,128]{3,2,1,0:T(8,128)S(1)}, f32[8,128]{1,0:T(8,128)S(1)}) custom-call(f32[24,64,128]{2,1,0:T(8,128)} %rho_hbm.9, f32[3,24,64,128]{3,2,1,0:T(8,128)} %mom_hbm.9, f32[24,64,128]{2,1,0:T(8,128)} %ene_hbm.9, f32[5,24,64,128]{3,2,1,0:T(8,128)} %inc_hbm.5, f32[5,26,8,128]{3,2,1,0:T(8,128)S(1)} %collective-permute-done.2.y_halo, ...), custom_call_target="tpu_custom_call" | custom-call | flops 1000 | bytes 1000 | tf_op jit(solution)/shard_map/part0/pallas_call | solution.py:540
  30.0 0.1 mix.1
  30.1 6.0 %part1.1 = (f32[5,12,64,128]{3,2,1,0:T(8,128)S(1)}, f32[8,128]{1,0:T(8,128)S(1)}) custom-call(f32[24,64,128]{2,1,0:T(8,128)} %rho_hbm.9, f32[3,24,64,128]{3,2,1,0:T(8,128)} %mom_hbm.9, f32[24,64,128]{2,1,0:T(8,128)} %ene_hbm.9, f32[5,24,64,128]{3,2,1,0:T(8,128)} %inc_hbm.5, f32[5,26,8,128]{3,2,1,0:T(8,128)S(1)} %collective-permute-done.2.y_halo, ...), custom_call_target="tpu_custom_call" | custom-call | flops 1000 | bytes 1000 | tf_op jit(solution)/shard_map/part1/pallas_call | solution.py:540
  36.2 0.1 pair.1
  36.3 5.1 %collective-permute-start.9 = (f32[5,64,128]{2,1,0:T(8,128)S(1)}, f32[5,64,128]{2,1,0:T(8,128)S(1)}, u32[]{:S(2)}, u32[]{:S(2)}) collective-permute-start(f32[5,64,128]{2,1,0:T(8,128)S(1)} %get-tuple-element.64), channel_id=1, source_target_pairs={{0,8},{8,16},{16,24},{24,0},{1,9},{9,17},{17,25},{25,1},{2,10},{10... | collective-permute-start | bytes 491528 | tf_op jit(solution)/shard_map/ppermute | solution.py:520
  41.4 0.3 collective-permute-start.5
  41.7 9.7 %lines.1 = (f32[5,24,64,128]{3,2,1,0:T(8,128)S(1)}, f32[5,24,64,128]{3,2,1,0:T(8,128)S(1)}) custom-call(f32[24,64,128]{2,1,0:T(8,128)} %rho_hbm.9, f32[3,24,64,128]{3,2,1,0:T(8,128)} %mom_hbm.9, f32[24,64,128]{2,1,0:T(8,128)} %ene_hbm.9, f32[2,5,64,128]{3,2,1,0:T(8,128)S(1)} %get-tuple-element.50.edges, f32[2,5,64,128]{3,2,1,0:T(8,128)S(1)} %get-tuple-element.51.near, ...), custom_call_target="tpu_custom_call" | custom-call | flops 1000 | bytes 1000 | tf_op jit(solution)/shard_map/lines/pallas_call | solution.py:540
  51.4 3.7 %collective-permute-done.10 = f32[5,64,128]{2,1,0:T(8,128)S(1)} collective-permute-done((f32[5,64,128]{2,1,0:T(8,128)S(1)}, f32[5,64,128]{2,1,0:T(8,128)S(1)}, u32[]{:S(2)}, u32[]{:S(2)}) %collective-permute-start.10) | collective-permute-done | bytes 163872 | tf_op jit(solution)/shard_map/ppermute | solution.py:520
  55.2 4.3 %collective-permute-done.5.across = f32[2,5,64,128]{3,2,1,0:T(8,128)S(1)} collective-permute-done((f32[2,5,64,128]{3,2,1,0:T(8,128)S(1)}, f32[2,5,64,128]{3,2,1,0:T(8,128)S(1)}, u32[]{:S(2)}, u32[]{:S(2)}) %collective-permute-start.5) | collective-permute-done | bytes 327712 | tf_op jit(solution)/shard_map/ppermute | solution.py:520
  59.5 2.1 %register.1 = (f32[5,24,64,128]{3,2,1,0:T(8,128)}, f32[6,5,64,128]{3,2,1,0:T(8,128)S(1)}) custom-call(f32[5,24,64,128]{3,2,1,0:T(8,128)S(1)} %get-tuple-element.56.new_inc, f32[2,5,64,128]{3,2,1,0:T(8,128)S(1)} %collective-permute-done.5.across, f32[5,24,64,128]{3,2,1,0:T(8,128)S(1)} %get-tuple-element.55.local, ...), custom_call_target="tpu_custom_call" | custom-call | flops 1000 | bytes 1000 | tf_op jit(solution)/shard_map/register/pallas_call | solution.py:540
  61.6 2.2 %final.1 = f32[5,24,64,128]{3,2,1,0:T(8,128)} custom-call(f32[5,24,64,128]{3,2,1,0:T(8,128)S(1)} %get-tuple-element.55.local, f32[6,5,64,128]{3,2,1,0:T(8,128)S(1)} %get-tuple-element.60.rim, f32[2,5,64,128]{3,2,1,0:T(8,128)S(1)} %collective-permute-done.5.across, f32[2,5,64,128]{3,2,1,0:T(8,128)S(1)} %fusion.incoming), custom_call_target="tpu_custom_call" | custom-call | flops 1000 | bytes 1000 | tf_op jit(solution)/shard_map/final/pallas_call | solution.py:540
  (11 shorter events, 0.1 us)
Async XLA Ops:
  6.2 11.1 %collective-permute-start.2 = (f32[5,26,8,128]{3,2,1,0:T(8,128)S(1)}, f32[5,26,8,128]{3,2,1,0:T(8,128)S(1)}, u32[]{:S(2)}, u32[]{:S(2)}) collective-permute-start(f32[5,26,8,128]{3,2,1,0:T(8,128)S(1)} %get-tuple-element.38), channel_id=1, source_target_pairs={{0,4},{4,0},{1,5},{5,1},{2,6},{6,2},{3,7},{7,3},{8,12},{12,8},{9,1... | collective-permute-start | bytes 1597448 | tf_op jit(solution)/shard_map/ppermute | solution.py:520
  6.9 8.9 %collective-permute-start.3 = (f32[5,64,128]{2,1,0:T(8,128)S(1)}, f32[5,64,128]{2,1,0:T(8,128)S(1)}, u32[]{:S(2)}, u32[]{:S(2)}) collective-permute-start(f32[5,64,128]{2,1,0:T(8,128)S(1)} %get-tuple-element.45), channel_id=1, source_target_pairs={{0,1},{1,2},{2,3},{3,0},{4,5},{5,6},{6,7},{7,4},{8,9},{9,10},{10,1... | collective-permute-start | bytes 491528 | tf_op jit(solution)/shard_map/ppermute | solution.py:520
  8.2 9.1 %collective-permute-start.4 = (f32[5,64,128]{2,1,0:T(8,128)S(1)}, f32[5,64,128]{2,1,0:T(8,128)S(1)}, u32[]{:S(2)}, u32[]{:S(2)}) collective-permute-start(f32[5,64,128]{2,1,0:T(8,128)S(1)} %get-tuple-element.46), channel_id=1, source_target_pairs={{0,3},{1,0},{2,1},{3,2},{4,7},{5,4},{6,5},{7,6},{8,11},{9,8},{10,9... | collective-permute-start | bytes 491528 | tf_op jit(solution)/shard_map/ppermute | solution.py:520
  10.2 19.8 %collective-permute-start = (f32[2,5,64,128]{3,2,1,0:T(8,128)S(1)}, f32[2,5,64,128]{3,2,1,0:T(8,128)S(1)}, u32[]{:S(2)}, u32[]{:S(2)}) collective-permute-start(f32[2,5,64,128]{3,2,1,0:T(8,128)S(1)} %get-tuple-element.36), channel_id=1, source_target_pairs={{0,8},{8,16},{16,24},{24,0},{1,9},{9,17},{17,25},{25,1},{2,10},{10... | collective-permute-start | bytes 983048 | tf_op jit(solution)/shard_map/ppermute | solution.py:520
  11.4 18.6 %collective-permute-start.1 = (f32[2,5,64,128]{3,2,1,0:T(8,128)S(1)}, f32[2,5,64,128]{3,2,1,0:T(8,128)S(1)}, u32[]{:S(2)}, u32[]{:S(2)}) collective-permute-start(f32[2,5,64,128]{3,2,1,0:T(8,128)S(1)} %get-tuple-element.37), channel_id=1, source_target_pairs={{0,24},{8,0},{16,8},{24,16},{1,25},{9,1},{17,9},{25,17},{2,26},{10... | collective-permute-start | bytes 983048 | tf_op jit(solution)/shard_map/ppermute | solution.py:520
  11.7 5.6 %copy-start = (bf16[512,256]{1,0:T(8,128)(2,1)S(1)}, bf16[512,256]{1,0:T(8,128)(2,1)}, u32[]{:S(2)}) copy-start(bf16[512,256]{1,0:T(8,128)(2,1)} %constant.4.clone.table) | copy-start | bytes 786436
  21.2 14.9 %collective-permute-start.8 = (f32[2,5,64,128]{3,2,1,0:T(8,128)S(1)}, f32[2,5,64,128]{3,2,1,0:T(8,128)S(1)}, u32[]{:S(2)}, u32[]{:S(2)}) collective-permute-start(f32[2,5,64,128]{3,2,1,0:T(8,128)S(1)} %get-tuple-element.62), channel_id=1, source_target_pairs={{0,16},{8,24},{16,0},{24,8},{1,17},{9,25},{17,1},{25,9},{2,18},{10... | collective-permute-start | bytes 983048 | tf_op jit(solution)/shard_map/ppermute | solution.py:520
  22.5 37.0 %collective-permute-start.6 = (f32[3,5,64,128]{3,2,1,0:T(8,128)S(1)}, f32[3,5,64,128]{3,2,1,0:T(8,128)S(1)}, u32[]{:S(2)}, u32[]{:S(2)}) collective-permute-start(f32[3,5,64,128]{3,2,1,0:T(8,128)S(1)} %get-tuple-element.58), channel_id=1, source_target_pairs={{0,8},{8,16},{16,24},{24,0},{1,9},{9,17},{17,25},{25,1},{2,10},{10... | collective-permute-start | bytes 1474568 | tf_op jit(solution)/shard_map/ppermute | solution.py:520
  22.7 36.7 %collective-permute-start.7 = (f32[3,5,64,128]{3,2,1,0:T(8,128)S(1)}, f32[3,5,64,128]{3,2,1,0:T(8,128)S(1)}, u32[]{:S(2)}, u32[]{:S(2)}) collective-permute-start(f32[3,5,64,128]{3,2,1,0:T(8,128)S(1)} %get-tuple-element.59), channel_id=1, source_target_pairs={{0,24},{8,0},{16,8},{24,16},{1,25},{9,1},{17,9},{25,17},{2,26},{10... | collective-permute-start | bytes 1474568 | tf_op jit(solution)/shard_map/ppermute | solution.py:520
  36.3 15.2 %collective-permute-start.9 = (f32[5,64,128]{2,1,0:T(8,128)S(1)}, f32[5,64,128]{2,1,0:T(8,128)S(1)}, u32[]{:S(2)}, u32[]{:S(2)}) collective-permute-start(f32[5,64,128]{2,1,0:T(8,128)S(1)} %get-tuple-element.64), channel_id=1, source_target_pairs={{0,8},{8,16},{16,24},{24,0},{1,9},{9,17},{17,25},{25,1},{2,10},{10... | collective-permute-start | bytes 491528 | tf_op jit(solution)/shard_map/ppermute | solution.py:520
  41.4 13.8 %collective-permute-start.10 = (f32[5,64,128]{2,1,0:T(8,128)S(1)}, f32[5,64,128]{2,1,0:T(8,128)S(1)}, u32[]{:S(2)}, u32[]{:S(2)}) collective-permute-start(f32[5,64,128]{2,1,0:T(8,128)S(1)} %get-tuple-element.65), channel_id=1, source_target_pairs={{0,24},{8,0},{16,8},{24,16},{1,25},{9,1},{17,9},{25,17},{2,26},{10... | collective-permute-start | bytes 491528 | tf_op jit(solution)/shard_map/ppermute | solution.py:520
  41.4 18.1 %collective-permute-start.5 = (f32[2,5,64,128]{3,2,1,0:T(8,128)S(1)}, f32[2,5,64,128]{3,2,1,0:T(8,128)S(1)}, u32[]{:S(2)}, u32[]{:S(2)}) collective-permute-start(f32[2,5,64,128]{3,2,1,0:T(8,128)S(1)} %get-tuple-element.57), channel_id=1, source_target_pairs={{0,16},{8,24},{16,0},{24,8},{1,17},{9,25},{17,1},{25,9},{2,18},{10... | collective-permute-start | bytes 983048 | tf_op jit(solution)/shard_map/ppermute | solution.py:520
where the time goes:
time: 64 us; the launch traced here: 63.8 us
  Pallas kernels  39.8 us (62%)
  starting transfers between devices  13.7 us (21%)
  waiting for transfers between devices  9.5 us (15%)
  between operations  0.75 us (1%)
    pallas_call x10, Pallas kernels, call(): pl.pallas_call(kernel, in_specs=[place[i < hbm] for i in range(len(inputs...  39.8 us
    ppermute x11, starting transfers between devices, shifted(): lax.ppermute(value, axis, [(i, (i + by) % size) for i in range(size)])  13.7 us
    ppermute x11, waiting for transfers between devices, shifted(): lax.ppermute(value, axis, [(i, (i + by) % size) for i in range(size)])  9.5 us
  transfers between devices with their start and end apart: 11, of which 3 were waited for; matrix products, arithmetic and copies ran while one was open for 0% of the time, Pallas kernels for 47%

commit v1 on v0

--- a/solution.py
+++ b/solution.py
@@ -103,37 +103,63 @@
     return pltpu.roll(value, amount, value.ndim - 1)
 
 
+class Blocks:
+    def __init__(self, sources, targets, sems, dims, size, begin=0):
+        self.parts = list(zip(sources, targets, dims, strict=True))
+        self.sems, self.size, self.begin = sems, size, begin
+        self.count = targets[0].shape[dims[0]] // size
+
+        def start(k, _):
+            for copy in self.piece(k):
+                copy.start()
+            return 0
+
+        lax.fori_loop(0, self.count, start, 0)
+
+    def piece(self, k):
+        copies = []
+        for n, (source, target, dim) in enumerate(self.parts):
+            lead = (slice(None),) * dim
+            first = pl.multiple_of(k * self.size, self.size)
+            there = source.at[(*lead, pl.ds(self.begin + first, self.size))]
+            here = target.at[(*lead, pl.ds(first, self.size))]
+            copies.append(pltpu.make_async_copy(there, here, self.sems.at[n, k]))
+        return copies
+
+    def wait(self, k):
+        for copy in self.piece(k):
+            copy.wait()
+
+    def each(self, body, steps):
+        def one(k, _):
+            self.wait(k)
+            lax.fori_loop(k * steps, (k + 1) * steps, body, 0)
+            return 0
+
+        lax.fori_loop(0, self.count, one, 0)
+
+
+def write_out(kernel_part, pieces, copy_of):
+    def one(k, _):
+        kernel_part(k)
+        copy_of(k).start()
+        return 0
+
+    def wait(k, _):
+        copy_of(k).wait()
+        return 0
+
+    lax.fori_loop(0, pieces, one, 0)
+    lax.fori_loop(0, pieces, wait, 0)
+
+
 def cells_at(rho, mom, ene, x, at):
     return [rho[x, at], mom[0, x, at], mom[1, x, at], mom[2, x, at], ene[x, at]]
 
 
-class Blocks:
-    def __init__(self, sources, targets, sems, dims, size, begin=0):
-        self.copies = []
-        for k in range(targets[0].shape[dims[0]] // size):
-            piece = []
-            for n, (source, target, dim) in enumerate(zip(sources, targets, dims)):
-                lead = (slice(None),) * dim
-                there = source.at[(*lead, pl.ds(begin + k * size, size))]
-                here = target.at[(*lead, pl.ds(k * size, size))]
-                piece.append(pltpu.make_async_copy(there, here, sems.at[n, k]))
-            self.copies.append(piece)
-        for piece in self.copies:
-            for copy in piece:
-                copy.start()
-
-    def wait(self, k):
-        for copy in self.copies[k]:
-            copy.wait()
-
-
-def cells_at(rho, mom, ene, x, at):
-    return [rho[x, at], mom[0, x, at], mom[1, x, at], mom[2, x, at], ene[x, at]]
-
-
 def face_kernel(
     rho_hbm, mom_hbm, ene_hbm,
-    up, down, own, g_rows, h_rows, z_up, z_down, z_own, y_edge, token,
+    to_partner, to_other, own, g_rows, h_rows, z_up, z_down, z_own, y_edge, token,
     rho, mom, ene, sems,
 ):
     nx, ny, nz = rho.shape
@@ -145,6 +171,7 @@
     rows = 16
     blocks = Blocks((rho_hbm, mom_hbm, ene_hbm), (rho, mom, ene), sems, (1, 2, 1), rows)
     token[...] = jnp.zeros_like(token)
+    odd = is_upper()
 
     def tile(t, _):
         at = pl.ds(pl.multiple_of(8 * t, 8), 8)
@@ -168,9 +195,11 @@
                     g_rows[stored[x], v, at] = g[v]
                     h_rows[stored[x], v, at] = h[v]
                 if x == 0:
-                    down[0, v, at] = f[v]
+                    to_other[v, at] = f[v]
                 if x == nx - 1:
-                    up[0, v, at] = f[v]
+                    first = to_other[v, at]
+                    to_partner[2, v, at] = jnp.where(odd, first, f[v])
+                    to_other[v, at] = jnp.where(odd, f[v], first)
             if x == 0:
                 totals, lower, upper = [g, h, g, h], f, f
             else:
@@ -183,8 +212,8 @@
                 ]
         h = [flux(packed[group], *primitives(packed[group]), 2) for group in range(2)]
         for v in range(5):
-            up[1, v, at] = own[0, v, at] = lower[v]
-            down[1, v, at] = own[1, v, at] = upper[v]
+            to_partner[0, v, at] = own[0, v, at] = lower[v]
+            to_partner[1, v, at] = own[1, v, at] = upper[v]
             for k in range(2):
                 g_rows[6 + k, v, at] = totals[2 * k][v]
                 h_rows[6 + k, v, at] = totals[2 * k + 1][v]
@@ -198,9 +227,7 @@
             z_down[v, at] = jnp.where(first_half, roll(h[0][v], -3), roll(h[1][v], 1))
         return 0
 
-    for k in range(ny // rows):
-        blocks.wait(k)
-        lax.fori_loop(k * rows // 8, (k + 1) * rows // 8, tile, 0)
+    blocks.each(tile, rows // 8)
 
 
 def base_kernel(rho_hbm, mom_hbm, ene_hbm, inc_hbm, after, base, w_up, w_down, rho, mom, ene, inc, sems):
@@ -247,9 +274,7 @@
                 w_up[k, v, at] = ends[-1.0][k][v]
         return 0
 
-    for k in range(ny // rows):
-        blocks.wait(k)
-        lax.fori_loop(k * rows // 8, (k + 1) * rows // 8, tile, 0)
+    blocks.each(tile, rows // 8)
 
 
 def fix_table(nz):
@@ -280,6 +305,13 @@
     return 45.0 * (at(1) - at(-1)) - 9.0 * (at(2) - at(-2)) + (at(3) - at(-3))
 
 
+def along_lanes(h):
+    v1 = roll(h, -1)
+    v2 = roll(v1 - 9.0 * h, -2)
+    both = 9.0 * v1 - h
+    return 5.0 * both + v2 + roll(both + 5.0 * v2, 3)
+
+
 def turn_of(x, nz):
     if isinstance(x, int):
         return (2 * nz - 3 - 8 * (x % 16)) % nz
@@ -288,8 +320,9 @@
 
 def end_kernel(
     base, w_up0, w_down0, g_rows, h_rows, y_halo, z_low, z_high, z_own, table,
-    sums, own_sums, w_up, w_down, fix, pad, dz_all,
+    sums, own_sums, to_other, to_partner, fix, token, pad, dz_all,
 ):
+    token[...] = jnp.zeros_like(token)
     ny, nz = base.shape[2:]
     nx = y_halo.shape[1] - 2
     lane = lanes((8, nz))
@@ -316,47 +349,59 @@
                 h = h_rows[r, v, at]
                 pad[r, v, inside] = g_rows[r, v, at]
                 moved = roll(fix[x // 16, v, at], turn_of(x, nz))
-                dz_all[r, v, at] = around(lambda n: roll(h, -n)) + jnp.where(edge_lane, moved, 0.0)
+                dz_all[r, v, at] = along_lanes(h) + jnp.where(edge_lane, moved, 0.0)
         return 0
 
     lax.fori_loop(0, ny // 8, first, 0)
     scale = -time_step * section_b / 60.0
 
-    for t in range(ny // 8):
-        at = slice(8 * t, 8 * t + 8)
-
-        def cross(r, v, t=t):
-            dy = around(lambda n: pad[r, v, 8 + 8 * t + n : 16 + 8 * t + n])
-            return scale * (dy + dz_all[r, v, slice(8 * t, 8 * t + 8)])
-
-        for v in range(5):
+    odd = is_upper()
+
+    def second(v, _):
+        for t in range(ny // 8):
+            at = slice(8 * t, 8 * t + 8)
+
+            def cross(r, t=t, at=at):
+                dy = around(lambda n: pad[r, v, 8 + 8 * t + n : 16 + 8 * t + n])
+                return scale * (dy + dz_all[r, v, at])
+
             for k in range(2):
-                sums[k, v, at] = own_sums[k, v, at] = base[k, v, at] + X["own"] * cross(6 + k, v)
-            for out, begin, near in ((w_down, w_down0, (0, 1, 2)), (w_up, w_up0, (5, 4, 3))):
-                q = [cross(r, v) for r in near]
+                sums[k, v, at] = own_sums[k, v, at] = base[k, v, at] + X["own"] * cross(6 + k)
+            faces = []
+            for begin, near in ((w_down0, (0, 1, 2)), (w_up0, (5, 4, 3))):
+                q = [cross(r) for r in near]
                 for k in range(3):
                     total = begin[k, v, at]
                     for j in range(1, 4 - k):
                         total = total + X["band_q"][k + j] * q[j - 1]
-                    out[k, v, at] = total
-
-
-def part_kernel(begin, rho_hbm, mom_hbm, ene_hbm, inc_hbm, y_halo, fix, *rest):
-    part, token, rho, mom, ene, inc, pad, sems = rest[-8:]
+                    faces.append(total)
+            for k in range(3):
+                to_other[k, v, at] = jnp.where(odd, faces[3 + k], faces[k])
+                to_partner[k, v, at] = jnp.where(odd, faces[k], faces[3 + k])
+        return 0
+
+    lax.fori_loop(0, 5, second, 0)
+
+
+def part_kernel(
+    rho_hbm, mom_hbm, ene_hbm, inc_hbm, y_halo, fix, after,
+    part, token,
+    rho, mom, ene, inc, pad, sems,
+):
     token[...] = jnp.zeros_like(token)
     nx, ny, nz = rho.shape
     lane = lanes((8, nz))
     edge_lane = (lane < 3) | (lane >= nz - 3)
     scale = -time_step / 60.0
     some = 4
-    blocks = Blocks((rho_hbm, mom_hbm, ene_hbm, inc_hbm), (rho, mom, ene, inc), sems, (0, 1, 0, 1), some, begin)
+    blocks = Blocks((rho_hbm, mom_hbm, ene_hbm, inc_hbm), (rho, mom, ene, inc), sems, (0, 1, 0, 1), some)
 
     def one_row(x, _):
-        turn = turn_of(begin + x, nz)
-        group = (begin + x) // 16
+        turn = turn_of(x, nz)
+        group = x // 16
         for v in range(5):
-            pad[v, 0:8] = y_halo[v, begin + x]
-            pad[v, ny + 8 : ny + 16] = y_halo[v, begin + x]
+            pad[v, 0:8] = y_halo[v, x]
+            pad[v, ny + 8 : ny + 16] = y_halo[v, x]
         for t in range(ny // 8):
             at = slice(8 * t, 8 * t + 8)
             cells = cells_at(rho, mom, ene, x, at)
@@ -365,7 +410,7 @@
             h = flux(cells, inverse, pressure, 2)
             for v in range(5):
                 pad[v, 8 + 8 * t : 16 + 8 * t] = g[v]
-                dz = around(lambda n, v=v: roll(h[v], -n))
+                dz = along_lanes(h[v])
                 dz = dz + jnp.where(edge_lane, roll(fix[group, v, at], turn), 0.0)
                 part[v, x, at] = section_a * inc[v, x, at] + scale * dz
         for t in range(ny // 8):
@@ -375,45 +420,49 @@
                 part[v, x, at] = part[v, x, at] + scale * dy
         return 0
 
-    for k in range(nx // some):
-        blocks.wait(k)
-        lax.fori_loop(k * some, (k + 1) * some, one_row, 0)
-
-
-def line_kernel(
-    rho_hbm, mom_hbm, ene_hbm, edges, near, part0, part1,
-    new_inc, local,
-    rho, mom, ene, f_all, q_all, e_all, sems,
-):
+    blocks.each(one_row, some)
+
+
+def line_kernel(rho_hbm, mom_hbm, ene_hbm, f_low, f_high, part, *rest):
+    *sums, new_inc_hbm, local = rest[:-9]
+    rho, mom, ene, new_inc, f_all, q_all, e_all, sems, out_sems = rest[-9:]
     nx, ny, nz = rho.shape
     rows = 16
     blocks = Blocks((rho_hbm, mom_hbm, ene_hbm), (rho, mom, ene), sems, (1, 2, 1), rows)
-    for k in range(ny // rows):
+
+    def copy_of(k):
+        at = pl.ds(pl.multiple_of(k * rows, rows), rows)
+        return pltpu.make_async_copy(new_inc.at[:, :, at], new_inc_hbm.at[:, :, at], out_sems.at[k])
+
+    def slab(k):
         blocks.wait(k)
-        at = slice(k * rows, (k + 1) * rows)
-
-        def fluxes_at(x, _, at=at, part=part0, begin=0):
-            cells = cells_at(rho, mom, ene, begin + x, at)
+        at = pl.ds(pl.multiple_of(k * rows, rows), rows)
+
+        def fluxes_at(x, _):
+            cells = cells_at(rho, mom, ene, x, at)
             for v, value in enumerate(flux(cells, *primitives(cells), 0)):
-                f_all[v, begin + x] = value
-                q_all[v, begin + x] = cells[v] + section_b * part[v, x, at]
+                f_all[v, x] = value
+                q_all[v, x] = cells[v] + section_b * part[v, x, at]
             return 0
 
-        lax.fori_loop(0, nx // 2, fluxes_at, 0)
-        lax.fori_loop(0, nx // 2, functools.partial(fluxes_at, part=part1, begin=nx // 2), 0)
-        lax.fori_loop(0, 5, functools.partial(one_line, at, (part0, part1), edges, near, new_inc, local, f_all, q_all, e_all), 0)
-
-
-def one_line(at, part, edges, near, new_inc, local, f_all, q_all, e_all, v, _):
+        lax.fori_loop(0, nx, fluxes_at, 0)
+        lines_of = functools.partial(one_line, at, part, f_low, f_high, sums, new_inc, local, f_all, q_all, e_all)
+        lax.fori_loop(0, 5, lines_of, 0)
+
+    write_out(slab, ny // rows, copy_of)
+
+
+def one_line(at, part, f_low, f_high, sums, new_inc, local, f_all, q_all, e_all, v, _):
     nx = f_all.shape[1]
     f = [f_all[v, x] for x in range(nx)]
     q = [q_all[v, x] for x in range(nx)]
-    low, high = edges[0, v, at], edges[1, v, at]
-    forward = ROOT_D * near[0, v, at]
+    low, high = f_low[v, at], f_high[v, at]
+    from_low, from_high = incoming(ROOT_D**nx, sums, v, at)
+    forward = ROOT_D * from_low
     for x in range(nx):
         e_all[x] = forward
         forward = ROOT_D * (f[x] + forward)
-    backward = ROOT_D * near[1, v, at]
+    backward = ROOT_D * from_high
     for x in reversed(range(nx)):
         e_all[x] = e_all[x] - backward
         backward = ROOT_D * (f[x] + backward)
@@ -423,7 +472,7 @@
         after = high if x == nx - 1 else f[x + 1]
         e = e_all[x]
         deriv = X["kappa"] * (after - before) + X["deriv"] * e
-        new_inc[v, x, at] = part[x // (nx // 2)][v, x % (nx // 2), at] - time_step * deriv
+        new_inc[v, x, at] = part[v, x, at] - time_step * deriv
         total = (1.0 - X["band_q"][0] - X["own"]) * q[x] - X["slow"] * e
         total = total - (section_b * time_step) * deriv
         for n in range(1, 4):
@@ -454,65 +503,62 @@
     return 0
 
 
-def mix_kernel(members, nx, own, from_low, from_high, after, onward, near, edges, token):
+def is_upper():
+    return lax.axis_index("gx") % 2 == 1
+
+
+def incoming(rate, sums, v, at):
+    if len(sums) == 1:
+        return sums[0][0, v, at], sums[0][1, v, at]
+    beside, pair, opposite = sums
+    closure = 1.0 / (1.0 - rate**4)
+    low, high = (closure * (opposite[k, v, at] + rate**2 * pair[k, v, at]) for k in range(2))
+    odd = is_upper()
+    return (
+        jnp.where(odd, beside[0, v, at] + rate * low, low),
+        jnp.where(odd, high, beside[1, v, at] + rate * high),
+    )
+
+
+def mix_kernel(rate, own, came, after, *rest):
+    *others, out, pair, beside, token = rest
+    odd = is_upper()
     token[...] = jnp.zeros_like(token)
-    rate = ROOT_D**nx
-    closure = 1.0 / (1.0 - rate**members)
-    for k, came in enumerate((from_low, from_high)):
-        onward[k] = own[k] + rate * came[1]
-        near[k] = closure * (came[1] + rate ** (members - 1) * own[k])
-        edges[k] = came[0]
-
-
-def pair_kernel(nx, own, opposite, after, up, down, rest):
-    rate = ROOT_F**nx
-    closure = 1.0 / (1.0 - rate**4)
-    up[...] = own[0] + rate**2 * opposite[0]
-    down[...] = own[1] + rate**2 * opposite[1]
-    rest[...] = (closure * rate) * opposite[...] + (closure * rate**3) * own[...]
-
-
-def far_part(members, nx, x, across, v):
-    rate = ROOT_D**nx
-    closure = 1.0 / (1.0 - rate**members)
-    low, high = across[0, v], across[1, v]
-    return (closure * rate * ROOT_D ** (x + 1)) * low - (closure * rate * ROOT_D ** (nx - x)) * high
-
-
-def register_kernel(members, new_inc, across, local, w_low, w_high, out_hbm, rim, out, sems):
-    nx = new_inc.shape[1]
-    for k in range(3):
-        for v in range(5):
-            rim[k, v] = local[v, k] - w_low[k, v]
-            rim[5 - k, v] = local[v, nx - 1 - k] - w_high[k, v]
-    done = []
     for v in range(5):
+        upper = jnp.where(odd, own[0, v] + rate * came[0, v], came[0, v] + rate * own[0, v])
+        lower = jnp.where(odd, came[1, v] + rate * own[1, v], own[1, v] + rate * came[1, v])
+        out[0, v] = pair[0, v] = upper
+        out[1, v] = pair[1, v] = lower
+        if len(others) == 5:
+            w_taken, f_taken, f_near, w_given, f_given = others
+            f_near[v] = came[2, v]
+            f_given[v] = f_taken[v]
+            for k in range(3):
+                w_given[k, v] = w_taken[k, v]
+        else:
+            near, other, low, high = others
+            low[v] = jnp.where(odd, near[v], other[v])
+            high[v] = jnp.where(odd, other[v], near[v])
+    beside[0] = came[0]
+    beside[1] = came[1]
+
+
+def final_kernel(local, w_other, w_partner, *rest):
+    odd = is_upper()
+    *sums, out_hbm, out, sems = rest
+    nx = local.shape[1]
+
+    def one(v):
+        low, high = incoming(ROOT_F**nx, sums, v, slice(None))
         for x in range(nx):
-            e = far_part(members, nx, x, across, v)
-            out[v, x] = new_inc[v, x] - (time_step * X["deriv"]) * e
-        copy = pltpu.make_async_copy(out.at[v], out_hbm.at[v], sems.at[v])
-        copy.start()
-        done.append(copy)
-    for copy in done:
-        copy.wait()
-
-
-def final_kernel(members, local, rim, across, incoming, out_hbm, out, sems):
-    nx = local.shape[1]
-    through = -section_b * time_step * X["deriv"] - X["slow"]
-    done = []
-    for v in range(5):
-        low, high = incoming[0, v], incoming[1, v]
-        for x in range(nx):
-            value = local[v, x] if 3 <= x < nx - 3 else rim[x if x < 3 else x - nx + 6, v]
-            value = value + through * far_part(members, nx, x, across, v)
-            value = value - (ROOT_F ** (x + 1)) * low - (ROOT_F ** (nx - x)) * high
+            value = local[v, x] - (ROOT_F ** (x + 1)) * low - (ROOT_F ** (nx - x)) * high
+            if x < 3:
+                value = value - jnp.where(odd, w_partner[x, v], w_other[x, v])
+            if x >= nx - 3:
+                value = value - jnp.where(odd, w_other[nx - 1 - x, v], w_partner[nx - 1 - x, v])
             out[v, x] = value
-        copy = pltpu.make_async_copy(out.at[v], out_hbm.at[v], sems.at[v])
-        copy.start()
-        done.append(copy)
-    for copy in done:
-        copy.wait()
+
+    write_out(one, 5, lambda v: pltpu.make_async_copy(out.at[v], out_hbm.at[v], sems.at[v]))
 
 
 def shifted(value, axis, by):
@@ -565,16 +611,14 @@
 
     state_room = [vmem(nx, ny, nz), vmem(3, nx, ny, nz), vmem(nx, ny, nz)]
 
-    up, down, own, g_rows, h_rows, z_up, z_down, z_own, y_edge, begun = call(
+    to_partner, to_other, own_d, g_rows, h_rows, z_up, z_down, z_own, y_edge, begun = call(
         face_kernel,
         "faces",
         state,
         3,
-        [(2, *face), (2, *face), (2, *face), (8, *face), (8, *face), face, face, (2, *face), (5, nx + 2, 8, nz), (8, nz)],
+        [(3, *face), face, (2, *face), (8, *face), (8, *face), face, face, (2, *face), (5, nx + 2, 8, nz), (8, nz)],
         state_room + [sems(3, ny // 16)],
     )
-    from_low = shifted(up, "gx", 1)
-    from_high = shifted(down, "gx", -1)
     z_low = shifted(z_up, "gz", 1)
     z_high = shifted(z_down, "gz", -1)
     y_halo = shifted(y_edge, "gy", 1)
@@ -588,81 +632,79 @@
         state_room + [vmem(*whole), sems(4, ny // 16)],
     )
     table = jnp.asarray(fix_table(nz), jnp.bfloat16)
-    sums, own_sums, w_up, w_down, fix = call(
+    sums, own_sums, w_to_other, w_to_partner, fix, ended = call(
         end_kernel,
         "ends",
         (base, w_up0, w_down0, g_rows, h_rows, y_halo, z_low, z_high, z_own, table),
         0,
-        [(2, *face), (2, *face), (3, *face), (3, *face), (2, *face)],
+        [(2, *face), (2, *face), (3, *face), (3, *face), (2, *face), (8, nz)],
         [vmem(8, 5, ny + 16, nz), vmem(8, *face)],
     )
-    half = nx // 2
-    half_room = [vmem(half, ny, nz), vmem(3, half, ny, nz), vmem(half, ny, nz), vmem(5, half, ny, nz)]
-    part0, token = call(
-        functools.partial(part_kernel, 0),
-        "part0",
-        (*state, increment, y_halo, fix),
+    rate_d, rate_f = ROOT_D**nx, ROOT_F**nx
+    token = ended
+    if members == 4:
+        partner = [(i, i ^ 1) for i in range(members)]
+        other = [(i, (i + 1 - 2 * (i % 2 == 0)) % members) for i in range(members)]
+        mixed = [(2, *face)] * 3 + [(8, nz)]
+        d_came = lax.ppermute(to_partner, "gx", partner)
+        f_came = lax.ppermute(sums, "gx", partner)
+        w_partner = lax.ppermute(w_to_partner, "gx", partner)
+        f_near, w_to_other, to_other, group, d_pair, d_beside, token = call(
+            functools.partial(mix_kernel, rate_d),
+            "mixd",
+            (own_d, d_came, ended, w_to_other, to_other),
+            0,
+            [face, (3, *face), face] + mixed,
+            [],
+        )
+        f_other = lax.ppermute(to_other, "gx", other)
+        w_other = lax.ppermute(w_to_other, "gx", other)
+        far = (d_beside, d_pair, shifted(group, "gx", 2))
+    else:
+        odd = lax.axis_index("gx") % 2 == 1
+        f_low = shifted(jnp.where(odd, to_other, to_partner[2]), "gx", 1)
+        f_high = shifted(jnp.where(odd, to_partner[2], to_other), "gx", -1)
+        far = (ring_sums(own_d, rate_d),)
+        w_low = shifted(jnp.where(odd, w_to_other, w_to_partner), "gx", 1)
+        w_high = shifted(jnp.where(odd, w_to_partner, w_to_other), "gx", -1)
+        w_other, w_partner = jnp.where(odd, w_high, w_low), jnp.where(odd, w_low, w_high)
+    part, parted = call(
+        part_kernel,
+        "part",
+        (*state, increment, y_halo, fix, token),
         4,
-        [(5, half, ny, nz), (8, nz)],
-        half_room + [vmem(5, ny + 16, nz), sems(4, half // 4)],
-    )
-    onward, near, edges, mixed = call(
-        functools.partial(mix_kernel, members, nx),
-        "mix",
-        (own, from_low, from_high, token),
-        0,
-        [(2, *face)] * 3 + [(8, nz)],
-        [],
-    )
-    part1, token1 = call(
-        functools.partial(part_kernel, half),
-        "part1",
-        (*state, increment, y_halo, fix, mixed),
-        4,
-        [(5, half, ny, nz), (8, nz)],
-        half_room + [vmem(5, ny + 16, nz), sems(4, half // 4)],
-    )
-
-    rate_d, rate_f = ROOT_D**nx, ROOT_F**nx
-    w_low = shifted(w_up, "gx", 1)
-    w_high = shifted(w_down, "gx", -1)
+        [whole, (8, nz)],
+        state_room + [vmem(*whole), vmem(5, ny + 16, nz), sems(4, nx // 4)],
+    )
     if members == 4:
-        across = shifted(onward, "gx", 2)
-        opposite = shifted(sums, "gx", 2)
-        mixed_up, mixed_down, rest = call(
-            functools.partial(pair_kernel, nx), "pair", (own_sums, opposite, token1), 0, [face, face, (2, *face)], []
+        f_low, f_high, group, f_pair, f_beside, _ = call(
+            functools.partial(mix_kernel, rate_f),
+            "mixf",
+            (own_sums, f_came, parted, f_near, f_other),
+            0,
+            [face, face] + mixed,
+            [],
         )
-        beside = jnp.stack([shifted(mixed_up, "gx", 1), shifted(mixed_down, "gx", -1)])
-        incoming = beside * (1.0 / (1.0 - rate_f**4)) + rest
+        from_others = (f_beside, f_pair, shifted(group, "gx", 2))
     else:
-        near = ring_sums(own, rate_d)
-        across = jnp.zeros_like(near)
-        incoming = ring_sums(sums, rate_f)
-
-    new_local, local = call(
+        from_others = (ring_sums(own_sums, rate_f),)
+    new_increment, local = call(
         line_kernel,
         "lines",
-        (*state, edges, near, part0, part1),
+        (*state, f_low, f_high, part, *far),
         3,
-        [whole, whole],
-        state_room + [vmem(5, nx, 16, nz), vmem(5, nx, 16, nz), vmem(nx, 16, nz), sems(3, ny // 16)],
-    )
-    out_room = [vmem(*whole), sems(5)]
-    new_increment, rim = call(
-        functools.partial(register_kernel, members),
-        "register",
-        (new_local, across, local, w_low, w_high),
-        0,
-        [("hbm", whole), (6, *face)],
-        out_room,
+        [("hbm", whole), whole],
+        state_room
+        + [vmem(*whole), vmem(5, nx, 16, nz), vmem(5, nx, 16, nz), vmem(nx, 16, nz)]
+        + [sems(3, ny // 16), sems(ny // 16)],
     )
     (new_state,) = call(
-        functools.partial(final_kernel, members),
+        final_kernel,
         "final",
-        (local, rim, across, incoming),
+        (local, w_other, w_partner, *from_others),
         0,
         [("hbm", whole)],
-        out_room,
+        [vmem(*whole), sems(5)],
     )
     return (new_state, new_increment)
 

time: 64 us -> 62.2 us (0.972)
  the two profiles are of different devices: /device:TPU:3 before, /device:TPU:0 now
where the time goes in v1:
time: 62.2 us; the launch traced here: 62 us
  Pallas kernels  37.1 us (60%)
  starting transfers between devices  14 us (23%)
  waiting for transfers between devices  10.1 us (16%)
  between operations  0.7 us (1%)
    pallas_call x8, Pallas kernels, call(): pl.pallas_call(kernel, in_specs=[place[i < hbm] for i in range(len(inputs...  37.1 us
    ppermute x5, starting transfers between devices, shifted(): lax.ppermute(value, axis, [(i, (i + by) % size) for i in range(size)])  6.37 us
    ppermute x1, waiting for transfers between devices, on_device(): w_other = lax.ppermute(w_to_other, 'gx', other)  6.18 us
    ppermute x5, waiting for transfers between devices, shifted(): lax.ppermute(value, axis, [(i, (i + by) % size) for i in range(size)])  3.95 us
    ppermute x1, starting transfers between devices, on_device(): d_came = lax.ppermute(to_partner, 'gx', partner)  2.56 us
    ppermute x1, starting transfers between devices, on_device(): f_other = lax.ppermute(to_other, 'gx', other)  2.5 us
    ppermute x1, starting transfers between devices, on_device(): w_other = lax.ppermute(w_to_other, 'gx', other)  1.43 us
  transfers between devices with their start and end apart: 10, of which 4 were waited for; matrix products, arithmetic and copies ran while one was open for 0% of the time, Pallas kernels for 48%

profile of v1, /device:TPU:0, one launch (start us, length us, event | category | flops | bytes accessed | tf_op | source)
XLA Modules:
  0.0 62.0 jit_solution(289122502350969063)
XLA Ops:
  0.6 5.5 %faces.1 = (f32[3,5,64,128]{3,2,1,0:T(8,128)S(1)}, f32[5,64,128]{2,1,0:T(8,128)S(1)}, f32[2,5,64,128]{3,2,1,0:T(8,128)S(1)}, f32[8,5,64,128]{3,2,1,0:T(8,128)S(1...) custom-call(f32[24,64,128]{2,1,0:T(8,128)} %rho_hbm.7, ...), custom_call_target="tpu_custom_call" | custom-call | flops 1000 | bytes 1000 | tf_op jit(solution)/shard_map/faces/pallas_call | solution.py:586
  6.2 0.5 collective-permute-start
  6.7 2.6 %collective-permute-start.4 = (f32[3,5,64,128]{3,2,1,0:T(8,128)S(1)}, f32[3,5,64,128]{3,2,1,0:T(8,128)S(1)}, u32[]{:S(2)}, u32[]{:S(2)}) collective-permute-start(f32[3,5,64,128]{3,2,1,0:T(8,128)S(1)} %get-tuple-element.51), channel_id=1, source_target_pairs={{0,8},{8,0},{16,24},{24,16},{1,9},{9,1},{17,25},{25,17},{2,10},{10... | collective-permute-start | bytes 1474568 | tf_op jit(solution)/shard_map/ppermute | solution.py:649
  9.3 1.6 %collective-permute-start.1 = (f32[5,64,128]{2,1,0:T(8,128)S(1)}, f32[5,64,128]{2,1,0:T(8,128)S(1)}, u32[]{:S(2)}, u32[]{:S(2)}) collective-permute-start(f32[5,64,128]{2,1,0:T(8,128)S(1)} %get-tuple-element.44), channel_id=1, source_target_pairs={{0,1},{1,2},{2,3},{3,0},{4,5},{5,6},{6,7},{7,4},{8,9},{9,10},{10,1... | collective-permute-start | bytes 491528 | tf_op jit(solution)/shard_map/ppermute | solution.py:566
  10.8 2.2 %collective-permute-start.2 = (f32[5,64,128]{2,1,0:T(8,128)S(1)}, f32[5,64,128]{2,1,0:T(8,128)S(1)}, u32[]{:S(2)}, u32[]{:S(2)}) collective-permute-start(f32[5,64,128]{2,1,0:T(8,128)S(1)} %get-tuple-element.45), channel_id=1, source_target_pairs={{0,3},{1,0},{2,1},{3,2},{4,7},{5,4},{6,5},{7,6},{8,11},{9,8},{10,9... | collective-permute-start | bytes 491528 | tf_op jit(solution)/shard_map/ppermute | solution.py:566
  13.1 4.1 %base.1 = (f32[2,5,64,128]{3,2,1,0:T(8,128)S(1)}, f32[3,5,64,128]{3,2,1,0:T(8,128)S(1)}, f32[3,5,64,128]{3,2,1,0:T(8,128)S(1)}) custom-call(f32[24,64,128]{2,1,0:T(8,128)} %rho_hbm.7, f32[3,24,64,128]{3,2,1,0:T(8,128)} %mom_hbm.7, f32[24,64,128]{2,1,0:T(8,128)} %ene_hbm.7, f32[5,24,64,128]{3,2,1,0:T(8,128)} %inc_hbm.3, f32[8,128]{1,0:T(8,128)S(1)} %get-tuple-element.37.after), custom_call_target="tpu_custom_call" | custom-call | flops 1000 | bytes 1000 | tf_op jit(solution)/shard_map/base/pallas_call | solution.py:586
  17.2 1.0 %collective-permute-done.1.z_low = f32[5,64,128]{2,1,0:T(8,128)S(1)} collective-permute-done((f32[5,64,128]{2,1,0:T(8,128)S(1)}, f32[5,64,128]{2,1,0:T(8,128)S(1)}, u32[]{:S(2)}, u32[]{:S(2)}) %collective-permute-start.1) | collective-permute-done | bytes 163872 | tf_op jit(solution)/shard_map/ppermute | solution.py:566
  18.1 2.2 %collective-permute-done.2.z_high = f32[5,64,128]{2,1,0:T(8,128)S(1)} collective-permute-done((f32[5,64,128]{2,1,0:T(8,128)S(1)}, f32[5,64,128]{2,1,0:T(8,128)S(1)}, u32[]{:S(2)}, u32[]{:S(2)}) %collective-permute-start.2) | collective-permute-done | bytes 163872 | tf_op jit(solution)/shard_map/ppermute | solution.py:566
  20.3 0.0 collective-permute-done.y_halo
  20.4 4.0 %ends.1 = (f32[2,5,64,128]{3,2,1,0:T(8,128)S(1)}, f32[2,5,64,128]{3,2,1,0:T(8,128)S(1)}, f32[3,5,64,128]{3,2,1,0:T(8,128)S(1)}, f32[3,5,64,128]{3,2,1,0:T(8,128)...) custom-call(f32[2,5,64,128]{3,2,1,0:T(8,128)S(1)} %get-tuple-element.38.base, ...), custom_call_target="tpu_custom_call" | custom-call | flops 1000 | bytes 1000 | tf_op jit(solution)/shard_map/ends/pallas_call | solution.py:586
  24.4 0.6 collective-permute-start.3
  25.0 0.1 mixd.1
  25.1 2.5 %collective-permute-start.5 = (f32[5,64,128]{2,1,0:T(8,128)S(1)}, f32[5,64,128]{2,1,0:T(8,128)S(1)}, u32[]{:S(2)}, u32[]{:S(2)}) collective-permute-start(f32[5,64,128]{2,1,0:T(8,128)S(1)} %get-tuple-element.58), channel_id=1, source_target_pairs={{0,24},{8,16},{16,8},{24,0},{1,25},{9,17},{17,9},{25,1},{2,26},{10... | collective-permute-start | bytes 491528 | tf_op jit(solution)/shard_map/ppermute | solution.py:660
  27.6 0.5 collective-permute-start.8
  28.1 1.4 %collective-permute-start.7 = (f32[3,5,64,128]{3,2,1,0:T(8,128)S(1)}, f32[3,5,64,128]{3,2,1,0:T(8,128)S(1)}, u32[]{:S(2)}, u32[]{:S(2)}) collective-permute-start(f32[3,5,64,128]{3,2,1,0:T(8,128)S(1)} %get-tuple-element.66), channel_id=1, source_target_pairs={{0,24},{8,16},{16,8},{24,0},{1,25},{9,17},{17,9},{25,1},{2,26},{10... | collective-permute-start | bytes 1474568 | tf_op jit(solution)/shard_map/ppermute | solution.py:661
  29.6 1.5 %collective-permute-start.6 = (f32[2,5,64,128]{3,2,1,0:T(8,128)S(1)}, f32[2,5,64,128]{3,2,1,0:T(8,128)S(1)}, u32[]{:S(2)}, u32[]{:S(2)}) collective-permute-start(f32[2,5,64,128]{3,2,1,0:T(8,128)S(1)} %get-tuple-element.64), channel_id=1, source_target_pairs={{0,16},{8,24},{16,0},{24,8},{1,17},{9,25},{17,1},{25,9},{2,18},{10... | collective-permute-start | bytes 983048 | tf_op jit(solution)/shard_map/ppermute | solution.py:566
  31.1 9.9 %part.1 = (f32[5,24,64,128]{3,2,1,0:T(8,128)S(1)}, f32[8,128]{1,0:T(8,128)S(1)}) custom-call(f32[24,64,128]{2,1,0:T(8,128)} %rho_hbm.7, f32[3,24,64,128]{3,2,1,0:T(8,128)} %mom_hbm.7, f32[24,64,128]{2,1,0:T(8,128)} %ene_hbm.7, f32[5,24,64,128]{3,2,1,0:T(8,128)} %inc_hbm.3, f32[5,26,8,128]{3,2,1,0:T(8,128)S(1)} %collective-permute-done.y_halo, ...), custom_call_target="tpu_custom_call" | custom-call | flops 1000 | bytes 1000 | tf_op jit(solution)/shard_map/part/pallas_call | solution.py:586
  41.0 0.0 collective-permute-done.3.came
  41.0 0.7 %mixf.1 = (f32[5,64,128]{2,1,0:T(8,128)S(1)}, f32[5,64,128]{2,1,0:T(8,128)S(1)}, f32[2,5,64,128]{3,2,1,0:T(8,128)S(1)}, f32[2,5,64,128]{3,2,1,0:T(8,128)S(1)}, f...) custom-call(f32[2,5,64,128]{3,2,1,0:T(8,128)S(1)} %get-tuple-element.47.own, ...), custom_call_target="tpu_custom_call" | custom-call | flops 1000 | bytes 1000 | tf_op jit(solution)/shard_map/mixf/pallas_call | solution.py:586
  41.7 0.5 collective-permute-start.9
  42.2 10.7 %lines.1 = (f32[5,24,64,128]{3,2,1,0:T(8,128)}, f32[5,24,64,128]{3,2,1,0:T(8,128)S(1)}) custom-call(f32[24,64,128]{2,1,0:T(8,128)} %rho_hbm.7, f32[3,24,64,128]{3,2,1,0:T(8,128)} %mom_hbm.7, f32[24,64,128]{2,1,0:T(8,128)} %ene_hbm.7, f32[5,64,128]{2,1,0:T(8,128)S(1)} %get-tuple-element.59.f_low, f32[5,64,128]{2,1,0:T(8,128)S(1)} %get-tuple-element.60.f_high, ...), custom_call_target="tpu_custom_call" | custom-call | flops 1000 | bytes 1000 | tf_op jit(solution)/shard_map/lines/pallas_call | solution.py:586
  52.9 6.2 %collective-permute-done.7.w_other = f32[3,5,64,128]{3,2,1,0:T(8,128)S(1)} collective-permute-done((f32[3,5,64,128]{3,2,1,0:T(8,128)S(1)}, f32[3,5,64,128]{3,2,1,0:T(8,128)S(1)}, u32[]{:S(2)}, u32[]{:S(2)}) %collective-permute-start.7) | collective-permute-done | bytes 491552 | tf_op jit(solution)/shard_map/ppermute | solution.py:661
  59.1 0.8 %collective-permute-done.9.rest_2_ = f32[2,5,64,128]{3,2,1,0:T(8,128)S(1)} collective-permute-done((f32[2,5,64,128]{3,2,1,0:T(8,128)S(1)}, f32[2,5,64,128]{3,2,1,0:T(8,128)S(1)}, u32[]{:S(2)}, u32[]{:S(2)}) %collective-permute-start.9) | collective-permute-done | bytes 327712 | tf_op jit(solution)/shard_map/ppermute | solution.py:566
  59.9 2.1 %final.1 = f32[5,24,64,128]{3,2,1,0:T(8,128)} custom-call(f32[5,24,64,128]{3,2,1,0:T(8,128)S(1)} %get-tuple-element.65.local, f32[3,5,64,128]{3,2,1,0:T(8,128)S(1)} %collective-permute-done.7.w_other, f32[3,5,64,128]{3,2,1,0:T(8,128)S(1)} %collective-permute-done.8.w_partner, f32[2,5,64,128]{3,2,1,0:T(8,128)S(1)} %get-tuple-element.68.rest_0_, ...), custom_call_target="tpu_custom_call" | custom-call | flops 1000 | bytes 1000 | tf_op jit(solution)/shard_map/final/pallas_call | solution.py:586
  (6 shorter events, 0.0 us)
Async XLA Ops:
  6.2 14.2 %collective-permute-start = (f32[5,26,8,128]{3,2,1,0:T(8,128)S(1)}, f32[5,26,8,128]{3,2,1,0:T(8,128)S(1)}, u32[]{:S(2)}, u32[]{:S(2)}) collective-permute-start(f32[5,26,8,128]{3,2,1,0:T(8,128)S(1)} %get-tuple-element.43), channel_id=1, source_target_pairs={{0,4},{4,0},{1,5},{5,1},{2,6},{6,2},{3,7},{7,3},{8,12},{12,8},{9,1... | collective-permute-start | bytes 1597448 | tf_op jit(solution)/shard_map/ppermute | solution.py:566
  6.7 18.3 %collective-permute-start.4 = (f32[3,5,64,128]{3,2,1,0:T(8,128)S(1)}, f32[3,5,64,128]{3,2,1,0:T(8,128)S(1)}, u32[]{:S(2)}, u32[]{:S(2)}) collective-permute-start(f32[3,5,64,128]{3,2,1,0:T(8,128)S(1)} %get-tuple-element.51), channel_id=1, source_target_pairs={{0,8},{8,0},{16,24},{24,16},{1,9},{9,1},{17,25},{25,17},{2,10},{10... | collective-permute-start | bytes 1474568 | tf_op jit(solution)/shard_map/ppermute | solution.py:649
  9.3 8.9 %collective-permute-start.1 = (f32[5,64,128]{2,1,0:T(8,128)S(1)}, f32[5,64,128]{2,1,0:T(8,128)S(1)}, u32[]{:S(2)}, u32[]{:S(2)}) collective-permute-start(f32[5,64,128]{2,1,0:T(8,128)S(1)} %get-tuple-element.44), channel_id=1, source_target_pairs={{0,1},{1,2},{2,3},{3,0},{4,5},{5,6},{6,7},{7,4},{8,9},{9,10},{10,1... | collective-permute-start | bytes 491528 | tf_op jit(solution)/shard_map/ppermute | solution.py:566
  10.8 9.5 %collective-permute-start.2 = (f32[5,64,128]{2,1,0:T(8,128)S(1)}, f32[5,64,128]{2,1,0:T(8,128)S(1)}, u32[]{:S(2)}, u32[]{:S(2)}) collective-permute-start(f32[5,64,128]{2,1,0:T(8,128)S(1)} %get-tuple-element.45), channel_id=1, source_target_pairs={{0,3},{1,0},{2,1},{3,2},{4,7},{5,4},{6,5},{7,6},{8,11},{9,8},{10,9... | collective-permute-start | bytes 491528 | tf_op jit(solution)/shard_map/ppermute | solution.py:566
  13.1 7.3 %copy-start = (bf16[512,256]{1,0:T(8,128)(2,1)S(1)}, bf16[512,256]{1,0:T(8,128)(2,1)}, u32[]{:S(2)}) copy-start(bf16[512,256]{1,0:T(8,128)(2,1)} %constant.2.clone.table) | copy-start | bytes 786436
  24.4 16.6 %collective-permute-start.3 = (f32[2,5,64,128]{3,2,1,0:T(8,128)S(1)}, f32[2,5,64,128]{3,2,1,0:T(8,128)S(1)}, u32[]{:S(2)}, u32[]{:S(2)}) collective-permute-start(f32[2,5,64,128]{3,2,1,0:T(8,128)S(1)} %get-tuple-element.48), channel_id=1, source_target_pairs={{0,8},{8,0},{16,24},{24,16},{1,9},{9,1},{17,25},{25,17},{2,10},{10... | collective-permute-start | bytes 983048 | tf_op jit(solution)/shard_map/ppermute | solution.py:650
  25.1 15.9 %collective-permute-start.5 = (f32[5,64,128]{2,1,0:T(8,128)S(1)}, f32[5,64,128]{2,1,0:T(8,128)S(1)}, u32[]{:S(2)}, u32[]{:S(2)}) collective-permute-start(f32[5,64,128]{2,1,0:T(8,128)S(1)} %get-tuple-element.58), channel_id=1, source_target_pairs={{0,24},{8,16},{16,8},{24,0},{1,25},{9,17},{17,9},{25,1},{2,26},{10... | collective-permute-start | bytes 491528 | tf_op jit(solution)/shard_map/ppermute | solution.py:660
  27.6 25.3 %collective-permute-start.8 = (f32[3,5,64,128]{3,2,1,0:T(8,128)S(1)}, f32[3,5,64,128]{3,2,1,0:T(8,128)S(1)}, u32[]{:S(2)}, u32[]{:S(2)}) collective-permute-start(f32[3,5,64,128]{3,2,1,0:T(8,128)S(1)} %get-tuple-element.67), channel_id=1, source_target_pairs={{0,8},{8,0},{16,24},{24,16},{1,9},{9,1},{17,25},{25,17},{2,10},{10... | collective-permute-start | bytes 1474568 | tf_op jit(solution)/shard_map/ppermute | solution.py:651
  28.1 31.0 %collective-permute-start.7 = (f32[3,5,64,128]{3,2,1,0:T(8,128)S(1)}, f32[3,5,64,128]{3,2,1,0:T(8,128)S(1)}, u32[]{:S(2)}, u32[]{:S(2)}) collective-permute-start(f32[3,5,64,128]{3,2,1,0:T(8,128)S(1)} %get-tuple-element.66), channel_id=1, source_target_pairs={{0,24},{8,16},{16,8},{24,0},{1,25},{9,17},{17,9},{25,1},{2,26},{10... | collective-permute-start | bytes 1474568 | tf_op jit(solution)/shard_map/ppermute | solution.py:661
  29.6 12.6 %collective-permute-start.6 = (f32[2,5,64,128]{3,2,1,0:T(8,128)S(1)}, f32[2,5,64,128]{3,2,1,0:T(8,128)S(1)}, u32[]{:S(2)}, u32[]{:S(2)}) collective-permute-start(f32[2,5,64,128]{3,2,1,0:T(8,128)S(1)} %get-tuple-element.64), channel_id=1, source_target_pairs={{0,16},{8,24},{16,0},{24,8},{1,17},{9,25},{17,1},{25,9},{2,18},{10... | collective-permute-start | bytes 983048 | tf_op jit(solution)/shard_map/ppermute | solution.py:566
  41.7 18.2 %collective-permute-start.9 = (f32[2,5,64,128]{3,2,1,0:T(8,128)S(1)}, f32[2,5,64,128]{3,2,1,0:T(8,128)S(1)}, u32[]{:S(2)}, u32[]{:S(2)}) collective-permute-start(f32[2,5,64,128]{3,2,1,0:T(8,128)S(1)} %get-tuple-element.70), channel_id=1, source_target_pairs={{0,16},{8,24},{16,0},{24,8},{1,17},{9,25},{17,1},{25,9},{2,18},{10... | collective-permute-start | bytes 983048 | tf_op jit(solution)/shard_map/ppermute | solution.py:566

commit v2 on v1

--- a/solution.py
+++ b/solution.py
@@ -17,6 +17,7 @@
 section_b = 15.0 / 16.0
 explicit_weights = (0.75, -0.15, 1.0 / 60.0)
 f32 = jnp.float32
+FIRST_ROWS = 12
 
 
 def root_of(coupling):
@@ -159,7 +160,7 @@
 
 def face_kernel(
     rho_hbm, mom_hbm, ene_hbm,
-    to_partner, to_other, own, g_rows, h_rows, z_up, z_down, z_own, y_edge, token,
+    to_partner, own, g_rows, h_rows, z_up, z_down, z_own, y_edge, token,
     rho, mom, ene, sems,
 ):
     nx, ny, nz = rho.shape
@@ -195,11 +196,11 @@
                     g_rows[stored[x], v, at] = g[v]
                     h_rows[stored[x], v, at] = h[v]
                 if x == 0:
-                    to_other[v, at] = f[v]
+                    to_partner[2, v, at] = f[v]
                 if x == nx - 1:
-                    first = to_other[v, at]
+                    first = to_partner[2, v, at]
                     to_partner[2, v, at] = jnp.where(odd, first, f[v])
-                    to_other[v, at] = jnp.where(odd, f[v], first)
+                    to_partner[3, v, at] = jnp.where(odd, f[v], first)
             if x == 0:
                 totals, lower, upper = [g, h, g, h], f, f
             else:
@@ -384,7 +385,7 @@
 
 
 def part_kernel(
-    rho_hbm, mom_hbm, ene_hbm, inc_hbm, y_halo, fix, after,
+    begin, rho_hbm, mom_hbm, ene_hbm, inc_hbm, y_halo, fix, after,
     part, token,
     rho, mom, ene, inc, pad, sems,
 ):
@@ -394,14 +395,14 @@
     edge_lane = (lane < 3) | (lane >= nz - 3)
     scale = -time_step / 60.0
     some = 4
-    blocks = Blocks((rho_hbm, mom_hbm, ene_hbm, inc_hbm), (rho, mom, ene, inc), sems, (0, 1, 0, 1), some)
+    blocks = Blocks((rho_hbm, mom_hbm, ene_hbm, inc_hbm), (rho, mom, ene, inc), sems, (0, 1, 0, 1), some, begin)
 
     def one_row(x, _):
-        turn = turn_of(x, nz)
-        group = x // 16
+        turn = turn_of(begin + x, nz)
+        group = (begin + x) // 16
         for v in range(5):
-            pad[v, 0:8] = y_halo[v, x]
-            pad[v, ny + 8 : ny + 16] = y_halo[v, x]
+            pad[v, 0:8] = y_halo[v, begin + x]
+            pad[v, ny + 8 : ny + 16] = y_halo[v, begin + x]
         for t in range(ny // 8):
             at = slice(8 * t, 8 * t + 8)
             cells = cells_at(rho, mom, ene, x, at)
@@ -423,7 +424,7 @@
     blocks.each(one_row, some)
 
 
-def line_kernel(rho_hbm, mom_hbm, ene_hbm, f_low, f_high, part, *rest):
+def line_kernel(rho_hbm, mom_hbm, ene_hbm, f_near, part0, part1, *rest):
     *sums, new_inc_hbm, local = rest[:-9]
     rho, mom, ene, new_inc, f_all, q_all, e_all, sems, out_sems = rest[-9:]
     nx, ny, nz = rho.shape
@@ -438,25 +439,28 @@
         blocks.wait(k)
         at = pl.ds(pl.multiple_of(k * rows, rows), rows)
 
-        def fluxes_at(x, _):
-            cells = cells_at(rho, mom, ene, x, at)
+        def fluxes_at(part, begin, x, _):
+            cells = cells_at(rho, mom, ene, begin + x, at)
             for v, value in enumerate(flux(cells, *primitives(cells), 0)):
-                f_all[v, x] = value
-                q_all[v, x] = cells[v] + section_b * part[v, x, at]
+                f_all[v, begin + x] = value
+                q_all[v, begin + x] = cells[v] + section_b * part[v, x, at]
             return 0
 
-        lax.fori_loop(0, nx, fluxes_at, 0)
-        lines_of = functools.partial(one_line, at, part, f_low, f_high, sums, new_inc, local, f_all, q_all, e_all)
+        cut = part0.shape[1]
+        lax.fori_loop(0, cut, functools.partial(fluxes_at, part0, 0), 0)
+        lax.fori_loop(0, nx - cut, functools.partial(fluxes_at, part1, cut), 0)
+        lines_of = functools.partial(one_line, at, (part0, part1), f_near, sums, new_inc, local, f_all, q_all, e_all)
         lax.fori_loop(0, 5, lines_of, 0)
 
     write_out(slab, ny // rows, copy_of)
 
 
-def one_line(at, part, f_low, f_high, sums, new_inc, local, f_all, q_all, e_all, v, _):
-    nx = f_all.shape[1]
+def one_line(at, parts, f_near, sums, new_inc, local, f_all, q_all, e_all, v, _):
+    nx, cut = f_all.shape[1], parts[0].shape[1]
     f = [f_all[v, x] for x in range(nx)]
     q = [q_all[v, x] for x in range(nx)]
-    low, high = f_low[v, at], f_high[v, at]
+    near, other = f_near[v, at], sums[-1][2, v, at]
+    low, high = jnp.where(is_upper(), near, other), jnp.where(is_upper(), other, near)
     from_low, from_high = incoming(ROOT_D**nx, sums, v, at)
     forward = ROOT_D * from_low
     for x in range(nx):
@@ -472,7 +476,7 @@
         after = high if x == nx - 1 else f[x + 1]
         e = e_all[x]
         deriv = X["kappa"] * (after - before) + X["deriv"] * e
-        new_inc[v, x, at] = part[v, x, at] - time_step * deriv
+        new_inc[v, x, at] = (parts[0][v, x, at] if x < cut else parts[1][v, x - cut, at]) - time_step * deriv
         total = (1.0 - X["band_q"][0] - X["own"]) * q[x] - X["slow"] * e
         total = total - (section_b * time_step) * deriv
         for n in range(1, 4):
@@ -529,36 +533,48 @@
         lower = jnp.where(odd, came[1, v] + rate * own[1, v], own[1, v] + rate * came[1, v])
         out[0, v] = pair[0, v] = upper
         out[1, v] = pair[1, v] = lower
-        if len(others) == 5:
-            w_taken, f_taken, f_near, w_given, f_given = others
-            f_near[v] = came[2, v]
-            f_given[v] = f_taken[v]
+        if others:
+            taken, given, near = others
+            near[v] = came[2, v]
+            out[2, v] = came[3, v]
             for k in range(3):
-                w_given[k, v] = w_taken[k, v]
-        else:
-            near, other, low, high = others
-            low[v] = jnp.where(odd, near[v], other[v])
-            high[v] = jnp.where(odd, other[v], near[v])
+                given[k, v] = taken[k, v]
     beside[0] = came[0]
     beside[1] = came[1]
 
 
-def final_kernel(local, w_other, w_partner, *rest):
-    odd = is_upper()
-    *sums, out_hbm, out, sems = rest
+def inner_kernel(local, *rest):
+    *sums, out_hbm, rim, out, sems = rest
     nx = local.shape[1]
 
     def one(v):
         low, high = incoming(ROOT_F**nx, sums, v, slice(None))
         for x in range(nx):
             value = local[v, x] - (ROOT_F ** (x + 1)) * low - (ROOT_F ** (nx - x)) * high
-            if x < 3:
-                value = value - jnp.where(odd, w_partner[x, v], w_other[x, v])
-            if x >= nx - 3:
-                value = value - jnp.where(odd, w_other[nx - 1 - x, v], w_partner[nx - 1 - x, v])
-            out[v, x] = value
-
-    write_out(one, 5, lambda v: pltpu.make_async_copy(out.at[v], out_hbm.at[v], sems.at[v]))
+            if 3 <= x < nx - 3:
+                out[v, x] = value
+            else:
+                rim[x if x < 3 else x - nx + 6, v] = value
+
+    inside = pl.ds(3, nx - 6)
+    write_out(one, 5, lambda v: pltpu.make_async_copy(out.at[v, inside], out_hbm.at[v, inside], sems.at[v]))
+
+
+def rim_kernel(before, rim, w_other, w_partner, out_hbm, out, sems):
+    nx = out_hbm.shape[1]
+    odd = is_upper()
+    for k in range(3):
+        for v in range(5):
+            other, near = w_other[k, v], w_partner[k, v]
+            out[0, v, k] = rim[k, v] - jnp.where(odd, near, other)
+            out[1, v, 2 - k] = rim[5 - k, v] - jnp.where(odd, other, near)
+    copies = [
+        pltpu.make_async_copy(out.at[side], out_hbm.at[:, pl.ds(side * (nx - 3), 3)], sems.at[side]) for side in range(2)
+    ]
+    for copy in copies:
+        copy.start()
+    for copy in copies:
+        copy.wait()
 
 
 def shifted(value, axis, by):
@@ -580,7 +596,7 @@
     return jnp.stack([low, high])
 
 
-def call(kernel, name, inputs, hbm, outputs, scratch):
+def call(kernel, name, inputs, hbm, outputs, scratch, aliases=None):
     place = {True: pl.BlockSpec(memory_space=pltpu.HBM), False: pl.BlockSpec(memory_space=pltpu.VMEM)}
     shapes = [dims[1] if dims[0] == "hbm" else dims for dims in outputs]
     return pl.pallas_call(
@@ -589,6 +605,7 @@
         out_specs=[place[dims[0] == "hbm"] for dims in outputs],
         out_shape=[jax.ShapeDtypeStruct(dims, f32) for dims in shapes],
         scratch_shapes=scratch,
+        input_output_aliases=aliases or {},
         compiler_params=pltpu.CompilerParams(vmem_limit_bytes=40 * 2**20),
         cost_estimate=pl.CostEstimate(flops=1000, bytes_accessed=1000, transcendentals=0),
         name=name,
@@ -611,12 +628,12 @@
 
     state_room = [vmem(nx, ny, nz), vmem(3, nx, ny, nz), vmem(nx, ny, nz)]
 
-    to_partner, to_other, own_d, g_rows, h_rows, z_up, z_down, z_own, y_edge, begun = call(
+    to_partner, own_d, g_rows, h_rows, z_up, z_down, z_own, y_edge, begun = call(
         face_kernel,
         "faces",
         state,
         3,
-        [(3, *face), face, (2, *face), (8, *face), (8, *face), face, face, (2, *face), (5, nx + 2, 8, nz), (8, nz)],
+        [(4, *face), (2, *face), (8, *face), (8, *face), face, face, (2, *face), (5, nx + 2, 8, nz), (8, nz)],
         state_room + [sems(3, ny // 16)],
     )
     z_low = shifted(z_up, "gz", 1)
@@ -645,66 +662,75 @@
     if members == 4:
         partner = [(i, i ^ 1) for i in range(members)]
         other = [(i, (i + 1 - 2 * (i % 2 == 0)) % members) for i in range(members)]
-        mixed = [(2, *face)] * 3 + [(8, nz)]
+        mixed = [(2, *face), (2, *face), (8, nz)]
         d_came = lax.ppermute(to_partner, "gx", partner)
         f_came = lax.ppermute(sums, "gx", partner)
         w_partner = lax.ppermute(w_to_partner, "gx", partner)
-        f_near, w_to_other, to_other, group, d_pair, d_beside, token = call(
+        w_to_other, f_near, group, d_pair, d_beside, token = call(
             functools.partial(mix_kernel, rate_d),
             "mixd",
-            (own_d, d_came, ended, w_to_other, to_other),
+            (own_d, d_came, ended, w_to_other),
             0,
-            [face, (3, *face), face] + mixed,
+            [(3, *face), face, (3, *face)] + mixed,
             [],
         )
-        f_other = lax.ppermute(to_other, "gx", other)
         w_other = lax.ppermute(w_to_other, "gx", other)
         far = (d_beside, d_pair, shifted(group, "gx", 2))
     else:
         odd = lax.axis_index("gx") % 2 == 1
-        f_low = shifted(jnp.where(odd, to_other, to_partner[2]), "gx", 1)
-        f_high = shifted(jnp.where(odd, to_partner[2], to_other), "gx", -1)
-        far = (ring_sums(own_d, rate_d),)
+        f_low = shifted(jnp.where(odd, to_partner[3], to_partner[2]), "gx", 1)
+        f_high = shifted(jnp.where(odd, to_partner[2], to_partner[3]), "gx", -1)
+        f_near, f_other = jnp.where(odd, f_low, f_high), jnp.where(odd, f_high, f_low)
+        far = (jnp.concatenate([ring_sums(own_d, rate_d), f_other[None]]),)
         w_low = shifted(jnp.where(odd, w_to_other, w_to_partner), "gx", 1)
         w_high = shifted(jnp.where(odd, w_to_partner, w_to_other), "gx", -1)
         w_other, w_partner = jnp.where(odd, w_high, w_low), jnp.where(odd, w_low, w_high)
-    part, parted = call(
-        part_kernel,
-        "part",
-        (*state, increment, y_halo, fix, token),
-        4,
-        [whole, (8, nz)],
-        state_room + [vmem(*whole), vmem(5, ny + 16, nz), sems(4, nx // 4)],
-    )
-    if members == 4:
-        f_low, f_high, group, f_pair, f_beside, _ = call(
-            functools.partial(mix_kernel, rate_f),
-            "mixf",
-            (own_sums, f_came, parted, f_near, f_other),
-            0,
-            [face, face] + mixed,
-            [],
+    cut = FIRST_ROWS
+    parts = []
+    for begin, rows in ((0, cut), (cut, nx - cut)):
+        some_part, token = call(
+            functools.partial(part_kernel, begin),
+            "part%d" % begin,
+            (*state, increment, y_halo, fix, token),
+            4,
+            [(5, rows, ny, nz), (8, nz)],
+            [vmem(rows, ny, nz), vmem(3, rows, ny, nz), vmem(rows, ny, nz), vmem(5, rows, ny, nz)]
+            + [vmem(5, ny + 16, nz), sems(4, rows // 4)],
         )
-        from_others = (f_beside, f_pair, shifted(group, "gx", 2))
-    else:
+        parts.append(some_part)
+        if begin == 0 and members == 4:
+            group, f_pair, f_beside, token = call(
+                functools.partial(mix_kernel, rate_f), "mixf", (own_sums, f_came, token), 0, [(2, *face)] + mixed, []
+            )
+            from_others = (f_beside, f_pair, shifted(group, "gx", 2))
+    if members != 4:
         from_others = (ring_sums(own_sums, rate_f),)
     new_increment, local = call(
         line_kernel,
         "lines",
-        (*state, f_low, f_high, part, *far),
+        (*state, f_near, *parts, *far),
         3,
         [("hbm", whole), whole],
         state_room
         + [vmem(*whole), vmem(5, nx, 16, nz), vmem(5, nx, 16, nz), vmem(nx, 16, nz)]
         + [sems(3, ny // 16), sems(ny // 16)],
     )
+    inner, rim = call(
+        inner_kernel,
+        "inner",
+        (local, *from_others),
+        0,
+        [("hbm", whole), (6, *face)],
+        [vmem(*whole), sems(5)],
+    )
     (new_state,) = call(
-        final_kernel,
-        "final",
-        (local, w_other, w_partner, *from_others),
-        0,
+        rim_kernel,
+        "rim",
+        (inner, rim, w_other, w_partner),
+        1,
         [("hbm", whole)],
-        [vmem(*whole), sems(5)],
+        [vmem(2, 5, 3, ny, nz), sems(2)],
+        {0: 0},
     )
     return (new_state, new_increment)
 

time: 62.2 us -> 57.4 us (0.923)
  waiting for transfers between devices: 10.1 us -> 4.76 us
  Pallas kernels: 37.1 us -> 39.1 us
  starting transfers between devices: 14 us -> 12.6 us
    ppermute x1, waiting for transfers between devices: 6.18 us -> 0.01 us  [on_device(): w_other = lax.ppermute(w_to_other, 'gx', other)]
    ppermute x1 -> x0, starting transfers between devices: 2.5 us -> none  [on_device(): f_other = lax.ppermute(to_other, 'gx', other)]
    pallas_call x8 -> x10, Pallas kernels: 37.1 us -> 39.1 us  [call(): pl.pallas_call(kernel, in_specs=[place[i < hbm] for i in range(len(inputs...]
    ppermute x5, starting transfers between devices: 6.37 us -> 7.53 us  [shifted(): lax.ppermute(value, axis, [(i, (i + by) % size) for i in range(size)])]
    ppermute x1, starting transfers between devices: 1.43 us -> 0.45 us  [on_device(): w_other = lax.ppermute(w_to_other, 'gx', other)]
    ppermute x1, starting transfers between devices: 0.54 us -> 1.52 us  [on_device(): w_partner = lax.ppermute(w_to_partner, 'gx', partner)]
    ppermute x1, waiting for transfers between devices: 0.01 us -> 0.82 us  [on_device(): f_came = lax.ppermute(sums, 'gx', partner)]
  transfers between devices with their start and end apart: 10 -> 9, of which waited for: 4 -> 4; matrix products, arithmetic and copies ran while one was open for 0% -> 0% of each run, Pallas kernels for 48% -> 57%
where the time goes in v2:
time: 57.4 us; the launch traced here: 57.2 us
  Pallas kernels  39.1 us (68%)
  starting transfers between devices  12.6 us (22%)
  waiting for transfers between devices  4.76 us (8%)
  between operations  0.72 us (1%)
    pallas_call x10, Pallas kernels, call(): pl.pallas_call(kernel, in_specs=[place[i < hbm] for i in range(len(inputs...  39.1 us
    ppermute x5, starting transfers between devices, shifted(): lax.ppermute(value, axis, [(i, (i + by) % size) for i in range(size)])  7.53 us
    ppermute x5, waiting for transfers between devices, shifted(): lax.ppermute(value, axis, [(i, (i + by) % size) for i in range(size)])  3.93 us
    ppermute x1, starting transfers between devices, on_device(): d_came = lax.ppermute(to_partner, 'gx', partner)  2.56 us
    ppermute x1, starting transfers between devices, on_device(): w_partner = lax.ppermute(w_to_partner, 'gx', partner)  1.52 us
  transfers between devices with their start and end apart: 9, of which 4 were waited for; matrix products, arithmetic and copies ran while one was open for 0% of the time, Pallas kernels for 57%

profile of v2, /device:TPU:0, one launch (start us, length us, event | category | flops | bytes accessed | tf_op | source)
XLA Modules:
  0.0 57.2 jit_solution(11073942597758466250)
XLA Ops:
  0.6 5.5 %faces.1 = (f32[4,5,64,128]{3,2,1,0:T(8,128)S(1)}, f32[2,5,64,128]{3,2,1,0:T(8,128)S(1)}, f32[8,5,64,128]{3,2,1,0:T(8,128)S(1)}, f32[8,5,64,128]{3,2,1,0:T(8,128...) custom-call(f32[24,64,128]{2,1,0:T(8,128)} %rho_hbm.9, ...), custom_call_target="tpu_custom_call" | custom-call | flops 1000 | bytes 1000 | tf_op jit(solution)/shard_map/faces/pallas_call | solution.py:602
  6.1 0.5 collective-permute-start.1
  6.7 2.6 %collective-permute-start = (f32[4,5,64,128]{3,2,1,0:T(8,128)S(1)}, f32[4,5,64,128]{3,2,1,0:T(8,128)S(1)}, u32[]{:S(2)}, u32[]{:S(2)}) collective-permute-start(f32[4,5,64,128]{3,2,1,0:T(8,128)S(1)} %get-tuple-element.38), channel_id=1, source_target_pairs={{0,8},{8,0},{16,24},{24,16},{1,9},{9,1},{17,25},{25,17},{2,10},{10... | collective-permute-start | bytes 1966088 | tf_op jit(solution)/shard_map/ppermute | solution.py:666
  9.2 1.6 %collective-permute-start.2 = (f32[5,64,128]{2,1,0:T(8,128)S(1)}, f32[5,64,128]{2,1,0:T(8,128)S(1)}, u32[]{:S(2)}, u32[]{:S(2)}) collective-permute-start(f32[5,64,128]{2,1,0:T(8,128)S(1)} %get-tuple-element.46), channel_id=1, source_target_pairs={{0,1},{1,2},{2,3},{3,0},{4,5},{5,6},{6,7},{7,4},{8,9},{9,10},{10,1... | collective-permute-start | bytes 491528 | tf_op jit(solution)/shard_map/ppermute | solution.py:582
  10.8 2.2 %collective-permute-start.3 = (f32[5,64,128]{2,1,0:T(8,128)S(1)}, f32[5,64,128]{2,1,0:T(8,128)S(1)}, u32[]{:S(2)}, u32[]{:S(2)}) collective-permute-start(f32[5,64,128]{2,1,0:T(8,128)S(1)} %get-tuple-element.47), channel_id=1, source_target_pairs={{0,3},{1,0},{2,1},{3,2},{4,7},{5,4},{6,5},{7,6},{8,11},{9,8},{10,9... | collective-permute-start | bytes 491528 | tf_op jit(solution)/shard_map/ppermute | solution.py:582
  13.0 4.1 %base.1 = (f32[2,5,64,128]{3,2,1,0:T(8,128)S(1)}, f32[3,5,64,128]{3,2,1,0:T(8,128)S(1)}, f32[3,5,64,128]{3,2,1,0:T(8,128)S(1)}) custom-call(f32[24,64,128]{2,1,0:T(8,128)} %rho_hbm.9, f32[3,24,64,128]{3,2,1,0:T(8,128)} %mom_hbm.9, f32[24,64,128]{2,1,0:T(8,128)} %ene_hbm.9, f32[5,24,64,128]{3,2,1,0:T(8,128)} %inc_hbm.5, f32[8,128]{1,0:T(8,128)S(1)} %get-tuple-element.39.after), custom_call_target="tpu_custom_call" | custom-call | flops 1000 | bytes 1000 | tf_op jit(solution)/shard_map/base/pallas_call | solution.py:602
  17.1 1.0 %collective-permute-done.2.z_low = f32[5,64,128]{2,1,0:T(8,128)S(1)} collective-permute-done((f32[5,64,128]{2,1,0:T(8,128)S(1)}, f32[5,64,128]{2,1,0:T(8,128)S(1)}, u32[]{:S(2)}, u32[]{:S(2)}) %collective-permute-start.2) | collective-permute-done | bytes 163872 | tf_op jit(solution)/shard_map/ppermute | solution.py:582
  18.1 2.2 %collective-permute-done.3.z_high = f32[5,64,128]{2,1,0:T(8,128)S(1)} collective-permute-done((f32[5,64,128]{2,1,0:T(8,128)S(1)}, f32[5,64,128]{2,1,0:T(8,128)S(1)}, u32[]{:S(2)}, u32[]{:S(2)}) %collective-permute-start.3) | collective-permute-done | bytes 163872 | tf_op jit(solution)/shard_map/ppermute | solution.py:582
  20.3 0.0 collective-permute-done.1.y_halo
  20.3 4.0 %ends.1 = (f32[2,5,64,128]{3,2,1,0:T(8,128)S(1)}, f32[2,5,64,128]{3,2,1,0:T(8,128)S(1)}, f32[3,5,64,128]{3,2,1,0:T(8,128)S(1)}, f32[3,5,64,128]{3,2,1,0:T(8,128)...) custom-call(f32[2,5,64,128]{3,2,1,0:T(8,128)S(1)} %get-tuple-element.40.base, ...), custom_call_target="tpu_custom_call" | custom-call | flops 1000 | bytes 1000 | tf_op jit(solution)/shard_map/ends/pallas_call | solution.py:602
  24.3 0.6 %collective-permute-start.4 = (f32[2,5,64,128]{3,2,1,0:T(8,128)S(1)}, f32[2,5,64,128]{3,2,1,0:T(8,128)S(1)}, u32[]{:S(2)}, u32[]{:S(2)}) collective-permute-start(f32[2,5,64,128]{3,2,1,0:T(8,128)S(1)} %get-tuple-element.56), channel_id=1, source_target_pairs={{0,8},{8,0},{16,24},{24,16},{1,9},{9,1},{17,25},{25,17},{2,10},{10... | collective-permute-start | bytes 983048 | tf_op jit(solution)/shard_map/ppermute | solution.py:667
  24.9 0.1 mixd.1
  25.0 1.6 %collective-permute-start.5 = (f32[3,5,64,128]{3,2,1,0:T(8,128)S(1)}, f32[3,5,64,128]{3,2,1,0:T(8,128)S(1)}, u32[]{:S(2)}, u32[]{:S(2)}) collective-permute-start(f32[3,5,64,128]{3,2,1,0:T(8,128)S(1)} %get-tuple-element.62), channel_id=1, source_target_pairs={{0,16},{8,24},{16,0},{24,8},{1,17},{9,25},{17,1},{25,9},{2,18},{10... | collective-permute-start | bytes 1474568 | tf_op jit(solution)/shard_map/ppermute | solution.py:582
  26.6 1.5 %collective-permute-start.8 = (f32[3,5,64,128]{3,2,1,0:T(8,128)S(1)}, f32[3,5,64,128]{3,2,1,0:T(8,128)S(1)}, u32[]{:S(2)}, u32[]{:S(2)}) collective-permute-start(f32[3,5,64,128]{3,2,1,0:T(8,128)S(1)} %get-tuple-element.70), channel_id=1, source_target_pairs={{0,8},{8,0},{16,24},{24,16},{1,9},{9,1},{17,25},{25,17},{2,10},{10... | collective-permute-start | bytes 1474568 | tf_op jit(solution)/shard_map/ppermute | solution.py:668
  28.1 0.5 collective-permute-start.7
  28.6 5.6 %part0.1 = (f32[5,12,64,128]{3,2,1,0:T(8,128)S(1)}, f32[8,128]{1,0:T(8,128)S(1)}) custom-call(f32[24,64,128]{2,1,0:T(8,128)} %rho_hbm.9, f32[3,24,64,128]{3,2,1,0:T(8,128)} %mom_hbm.9, f32[24,64,128]{2,1,0:T(8,128)} %ene_hbm.9, f32[5,24,64,128]{3,2,1,0:T(8,128)} %inc_hbm.5, f32[5,26,8,128]{3,2,1,0:T(8,128)S(1)} %collective-permute-done.1.y_halo, ...), custom_call_target="tpu_custom_call" | custom-call | flops 1000 | bytes 1000 | tf_op jit(solution)/shard_map/part0/pallas_call | solution.py:602
  34.2 0.8 %collective-permute-done.4.came = f32[2,5,64,128]{3,2,1,0:T(8,128)S(1)} collective-permute-done((f32[2,5,64,128]{3,2,1,0:T(8,128)S(1)}, f32[2,5,64,128]{3,2,1,0:T(8,128)S(1)}, u32[]{:S(2)}, u32[]{:S(2)}) %collective-permute-start.4) | collective-permute-done | bytes 327712 | tf_op jit(solution)/shard_map/ppermute | solution.py:667
  35.0 0.1 mixf.1
  35.1 1.6 %collective-permute-start.6 = (f32[2,5,64,128]{3,2,1,0:T(8,128)S(1)}, f32[2,5,64,128]{3,2,1,0:T(8,128)S(1)}, u32[]{:S(2)}, u32[]{:S(2)}) collective-permute-start(f32[2,5,64,128]{3,2,1,0:T(8,128)S(1)} %get-tuple-element.66), channel_id=1, source_target_pairs={{0,16},{8,24},{16,0},{24,8},{1,17},{9,25},{17,1},{25,9},{2,18},{10... | collective-permute-start | bytes 983048 | tf_op jit(solution)/shard_map/ppermute | solution.py:582
  36.7 6.1 %part12.1 = (f32[5,12,64,128]{3,2,1,0:T(8,128)S(1)}, f32[8,128]{1,0:T(8,128)}) custom-call(f32[24,64,128]{2,1,0:T(8,128)} %rho_hbm.9, f32[3,24,64,128]{3,2,1,0:T(8,128)} %mom_hbm.9, f32[24,64,128]{2,1,0:T(8,128)} %ene_hbm.9, f32[5,24,64,128]{3,2,1,0:T(8,128)} %inc_hbm.5, f32[5,26,8,128]{3,2,1,0:T(8,128)S(1)} %collective-permute-done.1.y_halo, ...), custom_call_target="tpu_custom_call" | custom-call | flops 1000 | bytes 1000 | tf_op jit(solution)/shard_map/part12/pallas_call | solution.py:602
  42.9 10.7 %lines.1 = (f32[5,24,64,128]{3,2,1,0:T(8,128)}, f32[5,24,64,128]{3,2,1,0:T(8,128)S(1)}) custom-call(f32[24,64,128]{2,1,0:T(8,128)} %rho_hbm.9, f32[3,24,64,128]{3,2,1,0:T(8,128)} %mom_hbm.9, f32[24,64,128]{2,1,0:T(8,128)} %ene_hbm.9, f32[5,64,128]{2,1,0:T(8,128)S(1)} %get-tuple-element.51.f_near, f32[5,12,64,128]{3,2,1,0:T(8,128)S(1)} %get-tuple-element.54.part0, ...), custom_call_target="tpu_custom_call" | custom-call | flops 1000 | bytes 1000 | tf_op jit(solution)/shard_map/lines/pallas_call | solution.py:602
  53.6 0.8 %collective-permute-done.6.rest_2_ = f32[2,5,64,128]{3,2,1,0:T(8,128)S(1)} collective-permute-done((f32[2,5,64,128]{3,2,1,0:T(8,128)S(1)}, f32[2,5,64,128]{3,2,1,0:T(8,128)S(1)}, u32[]{:S(2)}, u32[]{:S(2)}) %collective-permute-start.6) | collective-permute-done | bytes 327712 | tf_op jit(solution)/shard_map/ppermute | solution.py:582
  54.4 1.7 %inner.1 = (f32[5,24,64,128]{3,2,1,0:T(8,128)}, f32[6,5,64,128]{3,2,1,0:T(8,128)S(1)}) custom-call(f32[5,24,64,128]{3,2,1,0:T(8,128)S(1)} %get-tuple-element.63.local, f32[2,5,64,128]{3,2,1,0:T(8,128)S(1)} %get-tuple-element.64.rest_0_, f32[2,5,64,128]{3,2,1,0:T(8,128)S(1)} %get-tuple-element.65.rest_1_, f32[2,5,64,128]{3,2,1,0:T(8,128)S(1)} %collective-permute-done.6.rest_2_), custom_call_target="tpu_custom_call" | custom-call | flops 1000 | bytes 1000 | tf_op jit(solution)/shard_map/inner/pallas_call | solution.py:602
  56.2 1.1 %rim.1 = f32[5,24,64,128]{3,2,1,0:T(8,128)} custom-call(f32[5,24,64,128]{3,2,1,0:T(8,128)} %get-tuple-element.67.before, f32[6,5,64,128]{3,2,1,0:T(8,128)S(1)} %get-tuple-element.68.rim, f32[3,5,64,128]{3,2,1,0:T(8,128)S(1)} %collective-permute-done.7.w_other, f32[3,5,64,128]{3,2,1,0:T(8,128)S(1)} %collective-permute-done.8.w_partner), custom_call_target="tpu_custom_call", output_to_operand_aliasing={{}: (0, {})} | custom-call | flops 1000 | bytes 1000 | tf_op jit(solution)/shard_map/rim/pallas_call | solution.py:602
  (6 shorter events, 0.0 us)
Async XLA Ops:
  6.1 14.2 %collective-permute-start.1 = (f32[5,26,8,128]{3,2,1,0:T(8,128)S(1)}, f32[5,26,8,128]{3,2,1,0:T(8,128)S(1)}, u32[]{:S(2)}, u32[]{:S(2)}) collective-permute-start(f32[5,26,8,128]{3,2,1,0:T(8,128)S(1)} %get-tuple-element.45), channel_id=1, source_target_pairs={{0,4},{4,0},{1,5},{5,1},{2,6},{6,2},{3,7},{7,3},{8,12},{12,8},{9,1... | collective-permute-start | bytes 1597448 | tf_op jit(solution)/shard_map/ppermute | solution.py:582
  6.7 18.3 %collective-permute-start = (f32[4,5,64,128]{3,2,1,0:T(8,128)S(1)}, f32[4,5,64,128]{3,2,1,0:T(8,128)S(1)}, u32[]{:S(2)}, u32[]{:S(2)}) collective-permute-start(f32[4,5,64,128]{3,2,1,0:T(8,128)S(1)} %get-tuple-element.38), channel_id=1, source_target_pairs={{0,8},{8,0},{16,24},{24,16},{1,9},{9,1},{17,25},{25,17},{2,10},{10... | collective-permute-start | bytes 1966088 | tf_op jit(solution)/shard_map/ppermute | solution.py:666
  9.2 8.9 %collective-permute-start.2 = (f32[5,64,128]{2,1,0:T(8,128)S(1)}, f32[5,64,128]{2,1,0:T(8,128)S(1)}, u32[]{:S(2)}, u32[]{:S(2)}) collective-permute-start(f32[5,64,128]{2,1,0:T(8,128)S(1)} %get-tuple-element.46), channel_id=1, source_target_pairs={{0,1},{1,2},{2,3},{3,0},{4,5},{5,6},{6,7},{7,4},{8,9},{9,10},{10,1... | collective-permute-start | bytes 491528 | tf_op jit(solution)/shard_map/ppermute | solution.py:582
  10.8 9.5 %collective-permute-start.3 = (f32[5,64,128]{2,1,0:T(8,128)S(1)}, f32[5,64,128]{2,1,0:T(8,128)S(1)}, u32[]{:S(2)}, u32[]{:S(2)}) collective-permute-start(f32[5,64,128]{2,1,0:T(8,128)S(1)} %get-tuple-element.47), channel_id=1, source_target_pairs={{0,3},{1,0},{2,1},{3,2},{4,7},{5,4},{6,5},{7,6},{8,11},{9,8},{10,9... | collective-permute-start | bytes 491528 | tf_op jit(solution)/shard_map/ppermute | solution.py:582
  13.0 7.3 %copy-start = (bf16[512,256]{1,0:T(8,128)(2,1)S(1)}, bf16[512,256]{1,0:T(8,128)(2,1)}, u32[]{:S(2)}) copy-start(bf16[512,256]{1,0:T(8,128)(2,1)} %constant.2.clone.table) | copy-start | bytes 786436
  24.3 10.7 %collective-permute-start.4 = (f32[2,5,64,128]{3,2,1,0:T(8,128)S(1)}, f32[2,5,64,128]{3,2,1,0:T(8,128)S(1)}, u32[]{:S(2)}, u32[]{:S(2)}) collective-permute-start(f32[2,5,64,128]{3,2,1,0:T(8,128)S(1)} %get-tuple-element.56), channel_id=1, source_target_pairs={{0,8},{8,0},{16,24},{24,16},{1,9},{9,1},{17,25},{25,17},{2,10},{10... | collective-permute-start | bytes 983048 | tf_op jit(solution)/shard_map/ppermute | solution.py:667
  25.0 17.8 %collective-permute-start.5 = (f32[3,5,64,128]{3,2,1,0:T(8,128)S(1)}, f32[3,5,64,128]{3,2,1,0:T(8,128)S(1)}, u32[]{:S(2)}, u32[]{:S(2)}) collective-permute-start(f32[3,5,64,128]{3,2,1,0:T(8,128)S(1)} %get-tuple-element.62), channel_id=1, source_target_pairs={{0,16},{8,24},{16,0},{24,8},{1,17},{9,25},{17,1},{25,9},{2,18},{10... | collective-permute-start | bytes 1474568 | tf_op jit(solution)/shard_map/ppermute | solution.py:582
  26.6 29.5 %collective-permute-start.8 = (f32[3,5,64,128]{3,2,1,0:T(8,128)S(1)}, f32[3,5,64,128]{3,2,1,0:T(8,128)S(1)}, u32[]{:S(2)}, u32[]{:S(2)}) collective-permute-start(f32[3,5,64,128]{3,2,1,0:T(8,128)S(1)} %get-tuple-element.70), channel_id=1, source_target_pairs={{0,8},{8,0},{16,24},{24,16},{1,9},{9,1},{17,25},{25,17},{2,10},{10... | collective-permute-start | bytes 1474568 | tf_op jit(solution)/shard_map/ppermute | solution.py:668
  28.1 28.0 %collective-permute-start.7 = (f32[3,5,64,128]{3,2,1,0:T(8,128)S(1)}, f32[3,5,64,128]{3,2,1,0:T(8,128)S(1)}, u32[]{:S(2)}, u32[]{:S(2)}) collective-permute-start(f32[3,5,64,128]{3,2,1,0:T(8,128)S(1)} %get-tuple-element.69), channel_id=1, source_target_pairs={{0,24},{8,16},{16,8},{24,0},{1,25},{9,17},{17,9},{25,1},{2,26},{10... | collective-permute-start | bytes 1474568 | tf_op jit(solution)/shard_map/ppermute | solution.py:677
  35.1 19.3 %collective-permute-start.6 = (f32[2,5,64,128]{3,2,1,0:T(8,128)S(1)}, f32[2,5,64,128]{3,2,1,0:T(8,128)S(1)}, u32[]{:S(2)}, u32[]{:S(2)}) collective-permute-start(f32[2,5,64,128]{3,2,1,0:T(8,128)S(1)} %get-tuple-element.66), channel_id=1, source_target_pairs={{0,16},{8,24},{16,0},{24,8},{1,17},{9,25},{17,1},{25,9},{2,18},{10... | collective-permute-start | bytes 983048 | tf_op jit(solution)/shard_map/ppermute | solution.py:582

commit v3 on v2

--- a/solution.py
+++ b/solution.py
@@ -17,7 +17,7 @@
 section_b = 15.0 / 16.0
 explicit_weights = (0.75, -0.15, 1.0 / 60.0)
 f32 = jnp.float32
-FIRST_ROWS = 12
+CUTS = (0, 4, 12)
 
 
 def root_of(coupling):
@@ -160,7 +160,7 @@
 
 def face_kernel(
     rho_hbm, mom_hbm, ene_hbm,
-    to_partner, own, g_rows, h_rows, z_up, z_down, z_own, y_edge, token,
+    d_out, f_out, own, g_rows, h_rows, z_up, z_down, z_own, y_edge, token,
     rho, mom, ene, sems,
 ):
     nx, ny, nz = rho.shape
@@ -196,11 +196,11 @@
                     g_rows[stored[x], v, at] = g[v]
                     h_rows[stored[x], v, at] = h[v]
                 if x == 0:
-                    to_partner[2, v, at] = f[v]
+                    f_out[0, v, at] = f[v]
                 if x == nx - 1:
-                    first = to_partner[2, v, at]
-                    to_partner[2, v, at] = jnp.where(odd, first, f[v])
-                    to_partner[3, v, at] = jnp.where(odd, f[v], first)
+                    first = f_out[0, v, at]
+                    f_out[0, v, at] = jnp.where(odd, first, f[v])
+                    f_out[1, v, at] = jnp.where(odd, f[v], first)
             if x == 0:
                 totals, lower, upper = [g, h, g, h], f, f
             else:
@@ -213,8 +213,8 @@
                 ]
         h = [flux(packed[group], *primitives(packed[group]), 2) for group in range(2)]
         for v in range(5):
-            to_partner[0, v, at] = own[0, v, at] = lower[v]
-            to_partner[1, v, at] = own[1, v, at] = upper[v]
+            d_out[0, v, at] = own[0, v, at] = lower[v]
+            d_out[1, v, at] = own[1, v, at] = upper[v]
             for k in range(2):
                 g_rows[6 + k, v, at] = totals[2 * k][v]
                 h_rows[6 + k, v, at] = totals[2 * k + 1][v]
@@ -231,7 +231,8 @@
     blocks.each(tile, rows // 8)
 
 
-def base_kernel(rho_hbm, mom_hbm, ene_hbm, inc_hbm, after, base, w_up, w_down, rho, mom, ene, inc, sems):
+def base_kernel(rho_hbm, mom_hbm, ene_hbm, inc_hbm, after, base, w_up, w_down, token, rho, mom, ene, inc, sems):
+    token[...] = jnp.zeros_like(token)
     nx, ny, nz = rho.shape
     rows = 16
     blocks = Blocks((rho_hbm, mom_hbm, ene_hbm, inc_hbm), (rho, mom, ene, inc), sems, (1, 2, 1, 2), rows)
@@ -319,13 +320,52 @@
     return lax.rem(2 * nz - 3 - 8 * lax.rem(x, 16), nz)
 
 
+def end_rows(nx):
+    return [0, 1, 2, nx - 3, nx - 2, nx - 1, nx, nx + 1]
+
+
+def add_cross(cross, sums, w_up, w_down):
+    scale = -time_step * section_b / 60.0
+    for k in range(2):
+        sums[k] = sums[k] + (scale * X["own"]) * cross[6 + k]
+    for w, near in ((w_down, (0, 1, 2)), (w_up, (5, 4, 3))):
+        for k in range(3):
+            for j in range(1, 4 - k):
+                w[k] = w[k] + (scale * X["band_q"][k + j]) * cross[near[j - 1]]
+
+
+def early_kernel(base, w_up0, w_down0, g_rows, h_rows, y_halo, after, sums, w_up, w_down, pad):
+    ny, nz = base.shape[2:]
+    nx = y_halo.shape[1] - 2
+    for r, x in enumerate(end_rows(nx)):
+        for v in range(5):
+            pad[r, v, 0:8] = y_halo[v, x]
+            pad[r, v, ny + 8 : ny + 16] = y_halo[v, x]
+            pad[r, v, 8 : ny + 8] = g_rows[r, v]
+
+    def one(v, _):
+        for t in range(ny // 8):
+            at = slice(8 * t, 8 * t + 8)
+            cross = []
+            for r in range(8):
+                dy = around(lambda n, r=r, t=t: pad[r, v, 8 + 8 * t + n : 16 + 8 * t + n])
+                cross.append(dy + along_lanes(h_rows[r, v, at]))
+            parts = [[ref[k, v, at] for k in range(ref.shape[0])] for ref in (base, w_up0, w_down0)]
+            add_cross(cross, *parts)
+            for ref, part in zip((sums, w_up, w_down), parts, strict=True):
+                for k, value in enumerate(part):
+                    ref[k, v, at] = value
+        return 0
+
+    lax.fori_loop(0, 5, one, 0)
+
+
 def end_kernel(
-    base, w_up0, w_down0, g_rows, h_rows, y_halo, z_low, z_high, z_own, table,
-    sums, own_sums, to_other, to_partner, fix, token, pad, dz_all,
+    nx, sums0, w_up0, w_down0, z_low, z_high, z_own, table,
+    sums, own_sums, to_other, to_partner, fix, token,
 ):
     token[...] = jnp.zeros_like(token)
-    ny, nz = base.shape[2:]
-    nx = y_halo.shape[1] - 2
+    ny, nz = sums0.shape[2:]
     lane = lanes((8, nz))
     edge_lane = (lane < 3) | (lane >= nz - 3)
     parts = [z_low[...], z_high[...], z_own[0], z_own[1]]
@@ -336,52 +376,24 @@
     )
     for group in range(2):
         fix[group] = fixed[:, group * nz : group * nz + nz].reshape(5, ny, nz)
-    rows = [0, 1, 2, nx - 3, nx - 2, nx - 1, nx, nx + 1]
-    for r, x in enumerate(rows):
-        for v in range(5):
-            pad[r, v, 0:8] = y_halo[v, x]
-            pad[r, v, ny + 8 : ny + 16] = y_halo[v, x]
-
-    def first(t, _):
-        at = pl.ds(pl.multiple_of(8 * t, 8), 8)
-        inside = pl.ds(pl.multiple_of(8 * t + 8, 8), 8)
-        for r, x in enumerate(rows):
-            for v in range(5):
-                h = h_rows[r, v, at]
-                pad[r, v, inside] = g_rows[r, v, at]
-                moved = roll(fix[x // 16, v, at], turn_of(x, nz))
-                dz_all[r, v, at] = along_lanes(h) + jnp.where(edge_lane, moved, 0.0)
-        return 0
-
-    lax.fori_loop(0, ny // 8, first, 0)
-    scale = -time_step * section_b / 60.0
-
     odd = is_upper()
 
-    def second(v, _):
+    def one(v, _):
         for t in range(ny // 8):
             at = slice(8 * t, 8 * t + 8)
-
-            def cross(r, t=t, at=at):
-                dy = around(lambda n: pad[r, v, 8 + 8 * t + n : 16 + 8 * t + n])
-                return scale * (dy + dz_all[r, v, at])
-
+            cross = [
+                jnp.where(edge_lane, roll(fix[x // 16, v, at], turn_of(x, nz)), 0.0) for x in end_rows(nx)
+            ]
+            parts = [[ref[k, v, at] for k in range(ref.shape[0])] for ref in (sums0, w_up0, w_down0)]
+            add_cross(cross, *parts)
             for k in range(2):
-                sums[k, v, at] = own_sums[k, v, at] = base[k, v, at] + X["own"] * cross(6 + k)
-            faces = []
-            for begin, near in ((w_down0, (0, 1, 2)), (w_up0, (5, 4, 3))):
-                q = [cross(r) for r in near]
-                for k in range(3):
-                    total = begin[k, v, at]
-                    for j in range(1, 4 - k):
-                        total = total + X["band_q"][k + j] * q[j - 1]
-                    faces.append(total)
+                sums[k, v, at] = own_sums[k, v, at] = parts[0][k]
             for k in range(3):
-                to_other[k, v, at] = jnp.where(odd, faces[3 + k], faces[k])
-                to_partner[k, v, at] = jnp.where(odd, faces[k], faces[3 + k])
+                to_other[k, v, at] = jnp.where(odd, parts[1][k], parts[2][k])
+                to_partner[k, v, at] = jnp.where(odd, parts[2][k], parts[1][k])
         return 0
 
-    lax.fori_loop(0, 5, second, 0)
+    lax.fori_loop(0, 5, one, 0)
 
 
 def part_kernel(
@@ -424,8 +436,9 @@
     blocks.each(one_row, some)
 
 
-def line_kernel(rho_hbm, mom_hbm, ene_hbm, f_near, part0, part1, *rest):
-    *sums, new_inc_hbm, local = rest[:-9]
+def line_kernel(count, rho_hbm, mom_hbm, ene_hbm, f_near, *rest):
+    parts, rest = rest[:count], rest[count:]
+    *sums, new_inc_hbm, local, edges = rest[:-9]
     rho, mom, ene, new_inc, f_all, q_all, e_all, sems, out_sems = rest[-9:]
     nx, ny, nz = rho.shape
     rows = 16
@@ -446,21 +459,23 @@
                 q_all[v, begin + x] = cells[v] + section_b * part[v, x, at]
             return 0
 
-        cut = part0.shape[1]
-        lax.fori_loop(0, cut, functools.partial(fluxes_at, part0, 0), 0)
-        lax.fori_loop(0, nx - cut, functools.partial(fluxes_at, part1, cut), 0)
-        lines_of = functools.partial(one_line, at, (part0, part1), f_near, sums, new_inc, local, f_all, q_all, e_all)
+        begin = 0
+        for part in parts:
+            lax.fori_loop(0, part.shape[1], functools.partial(fluxes_at, part, begin), 0)
+            begin += part.shape[1]
+        lines_of = functools.partial(one_line, at, parts, f_near, sums, new_inc, local, edges, f_all, q_all, e_all)
         lax.fori_loop(0, 5, lines_of, 0)
 
     write_out(slab, ny // rows, copy_of)
 
 
-def one_line(at, parts, f_near, sums, new_inc, local, f_all, q_all, e_all, v, _):
-    nx, cut = f_all.shape[1], parts[0].shape[1]
+def one_line(at, parts, f_near, sums, new_inc, local, edges, f_all, q_all, e_all, v, _):
+    nx = f_all.shape[1]
+    part_at = [(part, i) for part in parts for i in range(part.shape[1])]
     f = [f_all[v, x] for x in range(nx)]
     q = [q_all[v, x] for x in range(nx)]
-    near, other = f_near[v, at], sums[-1][2, v, at]
-    low, high = jnp.where(is_upper(), near, other), jnp.where(is_upper(), other, near)
+    near = f_near[v, at]
+    low, high = jnp.where(is_upper(), near, 0.0), jnp.where(is_upper(), 0.0, near)
     from_low, from_high = incoming(ROOT_D**nx, sums, v, at)
     forward = ROOT_D * from_low
     for x in range(nx):
@@ -476,7 +491,10 @@
         after = high if x == nx - 1 else f[x + 1]
         e = e_all[x]
         deriv = X["kappa"] * (after - before) + X["deriv"] * e
-        new_inc[v, x, at] = (parts[0][v, x, at] if x < cut else parts[1][v, x - cut, at]) - time_step * deriv
+        value = part_at[x][0][v, part_at[x][1], at] - time_step * deriv
+        new_inc[v, x, at] = value
+        if x in (0, nx - 1):
+            edges[x // (nx - 1), v, at] = value
         total = (1.0 - X["band_q"][0] - X["own"]) * q[x] - X["slow"] * e
         total = total - (section_b * time_step) * deriv
         for n in range(1, 4):
@@ -533,44 +551,66 @@
         lower = jnp.where(odd, came[1, v] + rate * own[1, v], own[1, v] + rate * came[1, v])
         out[0, v] = pair[0, v] = upper
         out[1, v] = pair[1, v] = lower
-        if others:
-            taken, given, near = others
-            near[v] = came[2, v]
-            out[2, v] = came[3, v]
-            for k in range(3):
-                given[k, v] = taken[k, v]
-    beside[0] = came[0]
-    beside[1] = came[1]
-
-
-def inner_kernel(local, *rest):
+    beside[...] = came[...]
+    if others:
+        halos, f_came, d_came, halos_out, f_out, d_out = others
+        halos_out[...] = halos[...]
+        f_out[...] = f_came[...]
+        d_out[...] = d_came[...]
+
+
+def pass_kernel(came, after, near, onward, token):
+    token[...] = jnp.zeros_like(token)
+    near[...] = came[0]
+    onward[...] = came[1]
+
+
+def inner_kernel(local, w_partner, *rest):
     *sums, out_hbm, rim, out, sems = rest
     nx = local.shape[1]
+    odd = is_upper()
 
     def one(v):
         low, high = incoming(ROOT_F**nx, sums, v, slice(None))
         for x in range(nx):
             value = local[v, x] - (ROOT_F ** (x + 1)) * low - (ROOT_F ** (nx - x)) * high
-            if 3 <= x < nx - 3:
+            if x < 3:
+                value = value - jnp.where(odd, w_partner[x, v], 0.0)
+            if x >= nx - 3:
+                value = value - jnp.where(odd, 0.0, w_partner[nx - 1 - x, v])
+            if 4 <= x < nx - 4:
                 out[v, x] = value
             else:
-                rim[x if x < 3 else x - nx + 6, v] = value
-
-    inside = pl.ds(3, nx - 6)
+                rim[x if x < 4 else x - nx + 8, v] = value
+
+    inside = pl.ds(4, nx - 8)
     write_out(one, 5, lambda v: pltpu.make_async_copy(out.at[v, inside], out_hbm.at[v, inside], sems.at[v]))
 
 
-def rim_kernel(before, rim, w_other, w_partner, out_hbm, out, sems):
+def rim_kernel(before, inc_before, rim, edges, f_other, w_other, out_hbm, inc_hbm, out, inc, sems):
     nx = out_hbm.shape[1]
     odd = is_upper()
-    for k in range(3):
-        for v in range(5):
-            other, near = w_other[k, v], w_partner[k, v]
-            out[0, v, k] = rim[k, v] - jnp.where(odd, near, other)
-            out[1, v, 2 - k] = rim[5 - k, v] - jnp.where(odd, other, near)
-    copies = [
-        pltpu.make_async_copy(out.at[side], out_hbm.at[:, pl.ds(side * (nx - 3), 3)], sems.at[side]) for side in range(2)
-    ]
+    step = time_step * X["kappa"]
+    for v in range(5):
+        for side in range(2):
+            others = odd if side else jnp.logical_not(odd)
+            sign = -1.0 if side else 1.0
+            far = sign * jnp.where(others, f_other[v], 0.0)
+            for k in range(4):
+                value = rim[7 - k if side else k, v]
+                if k < 3:
+                    value = value - jnp.where(others, w_other[k, v], 0.0)
+                if k == 0:
+                    value = value + (section_b * step) * far
+                if k == 3:
+                    value = value + X["band_f"][4] * far
+                out[side, v, 3 - k if side else k] = value
+            inc[side, v, 0] = edges[side, v] + step * far
+    copies = []
+    for side in range(2):
+        rows, row = pl.ds(side * (nx - 4), 4), pl.ds(side * (nx - 1), 1)
+        copies.append(pltpu.make_async_copy(out.at[side], out_hbm.at[:, rows], sems.at[0, side]))
+        copies.append(pltpu.make_async_copy(inc.at[side], inc_hbm.at[:, row], sems.at[1, side]))
     for copy in copies:
         copy.start()
     for copy in copies:
@@ -628,66 +668,71 @@
 
     state_room = [vmem(nx, ny, nz), vmem(3, nx, ny, nz), vmem(nx, ny, nz)]
 
-    to_partner, own_d, g_rows, h_rows, z_up, z_down, z_own, y_edge, begun = call(
+    d_out, f_out, own_d, g_rows, h_rows, z_up, z_down, z_own, y_edge, begun = call(
         face_kernel,
         "faces",
         state,
         3,
-        [(4, *face), (2, *face), (8, *face), (8, *face), face, face, (2, *face), (5, nx + 2, 8, nz), (8, nz)],
+        [(2, *face), (2, *face), (2, *face), (8, *face), (8, *face), face, face, (2, *face), (5, nx + 2, 8, nz), (8, nz)],
         state_room + [sems(3, ny // 16)],
     )
     z_low = shifted(z_up, "gz", 1)
     z_high = shifted(z_down, "gz", -1)
     y_halo = shifted(y_edge, "gy", 1)
 
-    base, w_up0, w_down0 = call(
+    base, w_up0, w_down0, based = call(
         base_kernel,
         "base",
         (*state, increment, begun),
         4,
+        [(2, *face), (3, *face), (3, *face), (8, nz)],
+        state_room + [vmem(*whole), sems(4, ny // 16)],
+    )
+    table = jnp.asarray(fix_table(nz), jnp.bfloat16)
+    rate_d, rate_f = ROOT_D**nx, ROOT_F**nx
+    token = based
+    partner = [(i, i ^ 1) for i in range(members)]
+    other = [(i, (i + 1 - 2 * (i % 2 == 0)) % members) for i in range(members)]
+    mixed = [(2, *face), (2, *face), (8, nz)]
+    if members == 4:
+        d_came = lax.ppermute(d_out, "gx", partner)
+        f_came = lax.ppermute(f_out, "gx", partner)
+        group, d_pair, d_beside, token = call(
+            functools.partial(mix_kernel, rate_d), "mixd", (own_d, d_came, based), 0, [(2, *face)] + mixed, []
+        )
+        d_opposite = shifted(group, "gx", 2)
+    sums0, w_up1, w_down1 = call(
+        early_kernel,
+        "early",
+        (base, w_up0, w_down0, g_rows, h_rows, y_halo, token),
+        0,
         [(2, *face), (3, *face), (3, *face)],
-        state_room + [vmem(*whole), sems(4, ny // 16)],
-    )
-    table = jnp.asarray(fix_table(nz), jnp.bfloat16)
+        [vmem(8, 5, ny + 16, nz)],
+    )
     sums, own_sums, w_to_other, w_to_partner, fix, ended = call(
-        end_kernel,
+        functools.partial(end_kernel, nx),
         "ends",
-        (base, w_up0, w_down0, g_rows, h_rows, y_halo, z_low, z_high, z_own, table),
+        (sums0, w_up1, w_down1, z_low, z_high, z_own, table),
         0,
         [(2, *face), (2, *face), (3, *face), (3, *face), (2, *face), (8, nz)],
-        [vmem(8, 5, ny + 16, nz), vmem(8, *face)],
-    )
-    rate_d, rate_f = ROOT_D**nx, ROOT_F**nx
+        [],
+    )
     token = ended
     if members == 4:
-        partner = [(i, i ^ 1) for i in range(members)]
-        other = [(i, (i + 1 - 2 * (i % 2 == 0)) % members) for i in range(members)]
-        mixed = [(2, *face), (2, *face), (8, nz)]
-        d_came = lax.ppermute(to_partner, "gx", partner)
-        f_came = lax.ppermute(sums, "gx", partner)
+        sums_came = lax.ppermute(sums, "gx", partner)
         w_partner = lax.ppermute(w_to_partner, "gx", partner)
-        w_to_other, f_near, group, d_pair, d_beside, token = call(
-            functools.partial(mix_kernel, rate_d),
-            "mixd",
-            (own_d, d_came, ended, w_to_other),
-            0,
-            [(3, *face), face, (3, *face)] + mixed,
-            [],
-        )
-        w_other = lax.ppermute(w_to_other, "gx", other)
-        far = (d_beside, d_pair, shifted(group, "gx", 2))
     else:
         odd = lax.axis_index("gx") % 2 == 1
-        f_low = shifted(jnp.where(odd, to_partner[3], to_partner[2]), "gx", 1)
-        f_high = shifted(jnp.where(odd, to_partner[2], to_partner[3]), "gx", -1)
+        f_low = shifted(jnp.where(odd, f_out[1], f_out[0]), "gx", 1)
+        f_high = shifted(jnp.where(odd, f_out[0], f_out[1]), "gx", -1)
         f_near, f_other = jnp.where(odd, f_low, f_high), jnp.where(odd, f_high, f_low)
-        far = (jnp.concatenate([ring_sums(own_d, rate_d), f_other[None]]),)
+        far = (ring_sums(own_d, rate_d),)
         w_low = shifted(jnp.where(odd, w_to_other, w_to_partner), "gx", 1)
         w_high = shifted(jnp.where(odd, w_to_partner, w_to_other), "gx", -1)
         w_other, w_partner = jnp.where(odd, w_high, w_low), jnp.where(odd, w_low, w_high)
-    cut = FIRST_ROWS
     parts = []
-    for begin, rows in ((0, cut), (cut, nx - cut)):
+    for begin, end in zip(CUTS, CUTS[1:] + (nx,), strict=True):
+        rows = end - begin
         some_part, token = call(
             functools.partial(part_kernel, begin),
             "part%d" % begin,
@@ -698,19 +743,29 @@
             + [vmem(5, ny + 16, nz), sems(4, rows // 4)],
         )
         parts.append(some_part)
-        if begin == 0 and members == 4:
-            group, f_pair, f_beside, token = call(
-                functools.partial(mix_kernel, rate_f), "mixf", (own_sums, f_came, token), 0, [(2, *face)] + mixed, []
+        if len(parts) == 1 and members == 4:
+            f_near, onward, token = call(pass_kernel, "pass", (f_came, token), 0, [face, face, (8, nz)], [])
+            f_passed = shifted(onward, "gx", 2)
+        if len(parts) == 2 and members == 4:
+            w_to_other, f_other, d_opposite, group, f_pair, f_beside, token = call(
+                functools.partial(mix_kernel, rate_f),
+                "mixf",
+                (own_sums, sums_came, token, w_to_other, f_passed, d_opposite),
+                0,
+                [(3, *face), face, (2, *face), (2, *face)] + mixed,
+                [],
             )
+            far = (d_beside, d_pair, d_opposite)
+            w_other = lax.ppermute(w_to_other, "gx", other)
             from_others = (f_beside, f_pair, shifted(group, "gx", 2))
     if members != 4:
         from_others = (ring_sums(own_sums, rate_f),)
-    new_increment, local = call(
-        line_kernel,
+    new_inc, local, edges = call(
+        functools.partial(line_kernel, len(parts)),
         "lines",
         (*state, f_near, *parts, *far),
         3,
-        [("hbm", whole), whole],
+        [("hbm", whole), whole, (2, *face)],
         state_room
         + [vmem(*whole), vmem(5, nx, 16, nz), vmem(5, nx, 16, nz), vmem(nx, 16, nz)]
         + [sems(3, ny // 16), sems(ny // 16)],
@@ -718,19 +773,19 @@
     inner, rim = call(
         inner_kernel,
         "inner",
-        (local, *from_others),
+        (local, w_partner, *from_others),
         0,
-        [("hbm", whole), (6, *face)],
+        [("hbm", whole), (8, *face)],
         [vmem(*whole), sems(5)],
     )
-    (new_state,) = call(
+    new_state, new_increment = call(
         rim_kernel,
         "rim",
-        (inner, rim, w_other, w_partner),
-        1,
-        [("hbm", whole)],
-        [vmem(2, 5, 3, ny, nz), sems(2)],
-        {0: 0},
+        (inner, new_inc, rim, edges, f_other, w_other),
+        2,
+        [("hbm", whole), ("hbm", whole)],
+        [vmem(2, 5, 4, ny, nz), vmem(2, 5, 1, ny, nz), sems(2, 2)],
+        {0: 0, 1: 1},
     )
     return (new_state, new_increment)
 

time: 57.4 us -> 57.1 us (level)
  waiting for transfers between devices: 4.76 us -> 1.73 us
  starting transfers between devices: 12.6 us -> 14.7 us
    ppermute x5 -> x6, waiting for transfers between devices: 3.93 us -> 0.36 us  [shifted(): lax.ppermute(value, axis, [(i, (i + by) % size) for i in range(size)])]
    ppermute x2 -> x3, starting transfers between devices: 3.15 us -> 4.44 us  [the longest x1 2.56 us: on_device(): d_came = lax.ppermute(d_out, 'gx', partner)]
    ppermute x1, starting transfers between devices: 1.52 us -> 0.33 us  [on_device(): w_partner = lax.ppermute(w_to_partner, 'gx', partner)]
    ppermute x1, starting transfers between devices: 0.45 us -> 1.5 us  [on_device(): w_other = lax.ppermute(w_to_other, 'gx', other)]
    ppermute x5 -> x6, starting transfers between devices: 7.53 us -> 8.48 us  [shifted(): lax.ppermute(value, axis, [(i, (i + by) % size) for i in range(size)])]
    pallas_call x10 -> x13, Pallas kernels: 39.1 us -> 39.6 us  [call(): pl.pallas_call(kernel, in_specs=[place[i < hbm] for i in range(len(inputs...]
    ppermute x2 -> x3, waiting for transfers between devices: 0.83 us -> 1.36 us  [the longest x1 1.01 us: on_device(): sums_came = lax.ppermute(sums, 'gx', partner)]
  transfers between devices with their start and end apart: 9 -> 11, of which waited for: 4 -> 3; matrix products, arithmetic and copies ran while one was open for 0% -> 0% of each run, Pallas kernels for 57% -> 58%
where the time goes in v3:
time: 57.1 us; the launch traced here: 56.9 us
  Pallas kernels  39.6 us (69%)
  starting transfers between devices  14.7 us (26%)
  waiting for transfers between devices  1.73 us (3%)
  between operations  0.79 us (1%)
    pallas_call x13, Pallas kernels, call(): pl.pallas_call(kernel, in_specs=[place[i < hbm] for i in range(len(inputs...  39.6 us
    ppermute x6, starting transfers between devices, shifted(): lax.ppermute(value, axis, [(i, (i + by) % size) for i in range(size)])  8.48 us
    ppermute x1, starting transfers between devices, on_device(): d_came = lax.ppermute(d_out, 'gx', partner)  2.56 us
    ppermute x1, starting transfers between devices, on_device(): sums_came = lax.ppermute(sums, 'gx', partner)  1.56 us
    ppermute x1, starting transfers between devices, on_device(): w_other = lax.ppermute(w_to_other, 'gx', other)  1.5 us
  transfers between devices with their start and end apart: 11, of which 3 were waited for; matrix products, arithmetic and copies ran while one was open for 0% of the time, Pallas kernels for 58%

profile of v3, /device:TPU:0, one launch (start us, length us, event | category | flops | bytes accessed | tf_op | source)
XLA Modules:
  0.0 56.9 jit_solution(3563427904252043794)
XLA Ops:
  0.6 5.5 %faces.1 = (f32[2,5,64,128]{3,2,1,0:T(8,128)S(1)}, f32[2,5,64,128]{3,2,1,0:T(8,128)S(1)}, f32[2,5,64,128]{3,2,1,0:T(8,128)S(1)}, f32[8,5,64,128]{3,2,1,0:T(8,128...) custom-call(f32[24,64,128]{2,1,0:T(8,128)} %rho_hbm.11, ...), custom_call_target="tpu_custom_call" | custom-call | flops 1000 | bytes 1000 | tf_op jit(solution)/shard_map/faces/pallas_call | solution.py:642
  6.1 0.5 collective-permute-start.1
  6.7 2.6 %collective-permute-start.2 = (f32[2,5,64,128]{3,2,1,0:T(8,128)S(1)}, f32[2,5,64,128]{3,2,1,0:T(8,128)S(1)}, u32[]{:S(2)}, u32[]{:S(2)}) collective-permute-start(f32[2,5,64,128]{3,2,1,0:T(8,128)S(1)} %get-tuple-element.58), channel_id=1, source_target_pairs={{0,8},{8,0},{16,24},{24,16},{1,9},{9,1},{17,25},{25,17},{2,10},{10... | collective-permute-start | bytes 983048 | tf_op jit(solution)/shard_map/ppermute | solution.py:698
  9.2 1.6 %collective-permute-start.3 = (f32[5,64,128]{2,1,0:T(8,128)S(1)}, f32[5,64,128]{2,1,0:T(8,128)S(1)}, u32[]{:S(2)}, u32[]{:S(2)}) collective-permute-start(f32[5,64,128]{2,1,0:T(8,128)S(1)} %get-tuple-element.64), channel_id=1, source_target_pairs={{0,1},{1,2},{2,3},{3,0},{4,5},{5,6},{6,7},{7,4},{8,9},{9,10},{10,1... | collective-permute-start | bytes 491528 | tf_op jit(solution)/shard_map/ppermute | solution.py:622
  10.8 2.2 %collective-permute-start.4 = (f32[5,64,128]{2,1,0:T(8,128)S(1)}, f32[5,64,128]{2,1,0:T(8,128)S(1)}, u32[]{:S(2)}, u32[]{:S(2)}) collective-permute-start(f32[5,64,128]{2,1,0:T(8,128)S(1)} %get-tuple-element.65), channel_id=1, source_target_pairs={{0,3},{1,0},{2,1},{3,2},{4,7},{5,4},{6,5},{7,6},{8,11},{9,8},{10,9... | collective-permute-start | bytes 491528 | tf_op jit(solution)/shard_map/ppermute | solution.py:622
  13.0 0.3 collective-permute-start
  13.4 4.1 %base.1 = (f32[2,5,64,128]{3,2,1,0:T(8,128)S(1)}, f32[3,5,64,128]{3,2,1,0:T(8,128)S(1)}, f32[3,5,64,128]{3,2,1,0:T(8,128)S(1)}, f32[8,128]{1,0:T(8,128)S(1)}) custom-call(f32[24,64,128]{2,1,0:T(8,128)} %rho_hbm.11, f32[3,24,64,128]{3,2,1,0:T(8,128)} %mom_hbm.11, f32[24,64,128]{2,1,0:T(8,128)} %ene_hbm.11, f32[5,24,64,128]{3,2,1,0:T(8,128)} %inc_hbm.7, ...), custom_call_target="tpu_custom_call" | custom-call | flops 1000 | bytes 1000 | tf_op jit(solution)/shard_map/base/pallas_call | solution.py:642
  17.4 0.3 collective-permute-done.2.came
  17.9 2.0 %collective-permute-start.7 = (f32[2,5,64,128]{3,2,1,0:T(8,128)S(1)}, f32[2,5,64,128]{3,2,1,0:T(8,128)S(1)}, u32[]{:S(2)}, u32[]{:S(2)}) collective-permute-start(f32[2,5,64,128]{3,2,1,0:T(8,128)S(1)} %get-tuple-element.79), channel_id=1, source_target_pairs={{0,16},{8,24},{16,0},{24,8},{1,17},{9,25},{17,1},{25,9},{2,18},{10... | collective-permute-start | bytes 983048 | tf_op jit(solution)/shard_map/ppermute | solution.py:622
  19.9 2.2 %early.1 = (f32[2,5,64,128]{3,2,1,0:T(8,128)S(1)}, f32[3,5,64,128]{3,2,1,0:T(8,128)S(1)}, f32[3,5,64,128]{3,2,1,0:T(8,128)S(1)}) custom-call(f32[2,5,64,128]{3,2,1,0:T(8,128)S(1)} %get-tuple-element.52.base, f32[3,5,64,128]{3,2,1,0:T(8,128)S(1)} %get-tuple-element.53.w_up0, f32[3,5,64,128]{3,2,1,0:T(8,128)S(1)} %get-tuple-element.54.w_down0, ...), custom_call_target="tpu_custom_call" | custom-call | flops 1000 | bytes 1000 | tf_op jit(solution)/shard_map/early/pallas_call | solution.py:642
  22.1 1.0 %ends.1 = (f32[2,5,64,128]{3,2,1,0:T(8,128)S(1)}, f32[2,5,64,128]{3,2,1,0:T(8,128)S(1)}, f32[3,5,64,128]{3,2,1,0:T(8,128)S(1)}, f32[3,5,64,128]{3,2,1,0:T(8,128)...) custom-call(f32[2,5,64,128]{3,2,1,0:T(8,128)S(1)} %get-tuple-element.61.sums0, ...), custom_call_target="tpu_custom_call" | custom-call | flops 1000 | bytes 1000 | tf_op jit(solution)/shard_map/ends/pallas_call | solution.py:642
  23.1 1.6 %collective-permute-start.5 = (f32[2,5,64,128]{3,2,1,0:T(8,128)S(1)}, f32[2,5,64,128]{3,2,1,0:T(8,128)S(1)}, u32[]{:S(2)}, u32[]{:S(2)}) collective-permute-start(f32[2,5,64,128]{3,2,1,0:T(8,128)S(1)} %get-tuple-element.75), channel_id=1, source_target_pairs={{0,8},{8,0},{16,24},{24,16},{1,9},{9,1},{17,25},{25,17},{2,10},{10... | collective-permute-start | bytes 983048 | tf_op jit(solution)/shard_map/ppermute | solution.py:722
  24.7 2.7 %part0.1 = (f32[5,4,64,128]{3,2,1,0:T(8,128)S(1)}, f32[8,128]{1,0:T(8,128)S(1)}) custom-call(f32[24,64,128]{2,1,0:T(8,128)} %rho_hbm.11, f32[3,24,64,128]{3,2,1,0:T(8,128)} %mom_hbm.11, f32[24,64,128]{2,1,0:T(8,128)} %ene_hbm.11, f32[5,24,64,128]{3,2,1,0:T(8,128)} %inc_hbm.7, f32[5,26,8,128]{3,2,1,0:T(8,128)S(1)} %collective-permute-done.1.y_halo, ...), custom_call_target="tpu_custom_call" | custom-call | flops 1000 | bytes 1000 | tf_op jit(solution)/shard_map/part0/pallas_call | solution.py:642
  27.5 0.6 %collective-permute-start.6 = (f32[5,64,128]{2,1,0:T(8,128)S(1)}, f32[5,64,128]{2,1,0:T(8,128)S(1)}, u32[]{:S(2)}, u32[]{:S(2)}) collective-permute-start(f32[5,64,128]{2,1,0:T(8,128)S(1)} %get-tuple-element.78), channel_id=1, source_target_pairs={{0,16},{8,24},{16,0},{24,8},{1,17},{9,25},{17,1},{25,9},{2,18},{10... | collective-permute-start | bytes 491528 | tf_op jit(solution)/shard_map/ppermute | solution.py:622
  28.0 0.3 collective-permute-start.8
  28.4 4.1 %part4.1 = (f32[5,8,64,128]{3,2,1,0:T(8,128)S(1)}, f32[8,128]{1,0:T(8,128)S(1)}) custom-call(f32[24,64,128]{2,1,0:T(8,128)} %rho_hbm.11, f32[3,24,64,128]{3,2,1,0:T(8,128)} %mom_hbm.11, f32[24,64,128]{2,1,0:T(8,128)} %ene_hbm.11, f32[5,24,64,128]{3,2,1,0:T(8,128)} %inc_hbm.7, f32[5,26,8,128]{3,2,1,0:T(8,128)S(1)} %collective-permute-done.1.y_halo, ...), custom_call_target="tpu_custom_call" | custom-call | flops 1000 | bytes 1000 | tf_op jit(solution)/shard_map/part4/pallas_call | solution.py:642
  32.5 0.4 collective-permute-done.6.rest_1_
  32.8 1.0 %collective-permute-done.5.came = f32[2,5,64,128]{3,2,1,0:T(8,128)S(1)} collective-permute-done((f32[2,5,64,128]{3,2,1,0:T(8,128)S(1)}, f32[2,5,64,128]{3,2,1,0:T(8,128)S(1)}, u32[]{:S(2)}, u32[]{:S(2)}) %collective-permute-start.5) | collective-permute-done | bytes 327712 | tf_op jit(solution)/shard_map/ppermute | solution.py:722
  34.0 1.5 %collective-permute-start.10 = (f32[3,5,64,128]{3,2,1,0:T(8,128)S(1)}, f32[3,5,64,128]{3,2,1,0:T(8,128)S(1)}, u32[]{:S(2)}, u32[]{:S(2)}) collective-permute-start(f32[3,5,64,128]{3,2,1,0:T(8,128)S(1)} %get-tuple-element.95), channel_id=1, source_target_pairs={{0,24},{8,16},{16,8},{24,0},{1,25},{9,17},{17,9},{25,1},{2,26},{10... | collective-permute-start | bytes 1474568 | tf_op jit(solution)/shard_map/ppermute | solution.py:759
  35.5 1.5 %collective-permute-start.9 = (f32[2,5,64,128]{3,2,1,0:T(8,128)S(1)}, f32[2,5,64,128]{3,2,1,0:T(8,128)S(1)}, u32[]{:S(2)}, u32[]{:S(2)}) collective-permute-start(f32[2,5,64,128]{3,2,1,0:T(8,128)S(1)} %get-tuple-element.89), channel_id=1, source_target_pairs={{0,16},{8,24},{16,0},{24,8},{1,17},{9,25},{17,1},{25,9},{2,18},{10... | collective-permute-start | bytes 983048 | tf_op jit(solution)/shard_map/ppermute | solution.py:622
  37.0 6.1 %part12.1 = (f32[5,12,64,128]{3,2,1,0:T(8,128)S(1)}, f32[8,128]{1,0:T(8,128)}) custom-call(f32[24,64,128]{2,1,0:T(8,128)} %rho_hbm.11, f32[3,24,64,128]{3,2,1,0:T(8,128)} %mom_hbm.11, f32[24,64,128]{2,1,0:T(8,128)} %ene_hbm.11, f32[5,24,64,128]{3,2,1,0:T(8,128)} %inc_hbm.7, f32[5,26,8,128]{3,2,1,0:T(8,128)S(1)} %collective-permute-done.1.y_halo, ...), custom_call_target="tpu_custom_call" | custom-call | flops 1000 | bytes 1000 | tf_op jit(solution)/shard_map/part12/pallas_call | solution.py:642
  43.1 10.7 %lines.1 = (f32[5,24,64,128]{3,2,1,0:T(8,128)}, f32[5,24,64,128]{3,2,1,0:T(8,128)S(1)}, f32[2,5,64,128]{3,2,1,0:T(8,128)S(1)}) custom-call(f32[24,64,128]{2,1,0:T(8,128)} %rho_hbm.11, f32[3,24,64,128]{3,2,1,0:T(8,128)} %mom_hbm.11, f32[24,64,128]{2,1,0:T(8,128)} %ene_hbm.11, f32[5,64,128]{2,1,0:T(8,128)S(1)} %get-tuple-element.70.f_near, ...), custom_call_target="tpu_custom_call" | custom-call | flops 1000 | bytes 1000 | tf_op jit(solution)/shard_map/lines/pallas_call | solution.py:642
  53.9 1.6 %inner.1 = (f32[5,24,64,128]{3,2,1,0:T(8,128)}, f32[8,5,64,128]{3,2,1,0:T(8,128)S(1)}) custom-call(f32[5,24,64,128]{3,2,1,0:T(8,128)S(1)} %get-tuple-element.85.local, f32[3,5,64,128]{3,2,1,0:T(8,128)S(1)} %collective-permute-done.8.w_partner, f32[2,5,64,128]{3,2,1,0:T(8,128)S(1)} %get-tuple-element.87.rest_0_, ...), custom_call_target="tpu_custom_call" | custom-call | flops 1000 | bytes 1000 | tf_op jit(solution)/shard_map/inner/pallas_call | solution.py:642
  55.6 1.4 %rim.1 = (f32[5,24,64,128]{3,2,1,0:T(8,128)}, f32[5,24,64,128]{3,2,1,0:T(8,128)}) custom-call(f32[5,24,64,128]{3,2,1,0:T(8,128)} %get-tuple-element.90.before, f32[5,24,64,128]{3,2,1,0:T(8,128)} %get-tuple-element.91.inc_before, f32[8,5,64,128]{3,2,1,0:T(8,128)S(1)} %get-tuple-element.92.rim, ...), custom_call_target="tpu_custom_call", output_to_operand_aliasing={{0}: (0, {}), {1}: (1, {})} | custom-call | flops 1000 | bytes 1000 | tf_op jit(solution)/shard_map/rim/pallas_call | solution.py:642
  (13 shorter events, 0.3 us)
Async XLA Ops:
  6.1 13.8 %collective-permute-start.1 = (f32[5,26,8,128]{3,2,1,0:T(8,128)S(1)}, f32[5,26,8,128]{3,2,1,0:T(8,128)S(1)}, u32[]{:S(2)}, u32[]{:S(2)}) collective-permute-start(f32[5,26,8,128]{3,2,1,0:T(8,128)S(1)} %get-tuple-element.50), channel_id=1, source_target_pairs={{0,4},{4,0},{1,5},{5,1},{2,6},{6,2},{3,7},{7,3},{8,12},{12,8},{9,1... | collective-permute-start | bytes 1597448 | tf_op jit(solution)/shard_map/ppermute | solution.py:622
  6.7 11.1 %collective-permute-start.2 = (f32[2,5,64,128]{3,2,1,0:T(8,128)S(1)}, f32[2,5,64,128]{3,2,1,0:T(8,128)S(1)}, u32[]{:S(2)}, u32[]{:S(2)}) collective-permute-start(f32[2,5,64,128]{3,2,1,0:T(8,128)S(1)} %get-tuple-element.58), channel_id=1, source_target_pairs={{0,8},{8,0},{16,24},{24,16},{1,9},{9,1},{17,25},{25,17},{2,10},{10... | collective-permute-start | bytes 983048 | tf_op jit(solution)/shard_map/ppermute | solution.py:698
  9.2 12.9 %collective-permute-start.3 = (f32[5,64,128]{2,1,0:T(8,128)S(1)}, f32[5,64,128]{2,1,0:T(8,128)S(1)}, u32[]{:S(2)}, u32[]{:S(2)}) collective-permute-start(f32[5,64,128]{2,1,0:T(8,128)S(1)} %get-tuple-element.64), channel_id=1, source_target_pairs={{0,1},{1,2},{2,3},{3,0},{4,5},{5,6},{6,7},{7,4},{8,9},{9,10},{10,1... | collective-permute-start | bytes 491528 | tf_op jit(solution)/shard_map/ppermute | solution.py:622
  10.8 11.3 %collective-permute-start.4 = (f32[5,64,128]{2,1,0:T(8,128)S(1)}, f32[5,64,128]{2,1,0:T(8,128)S(1)}, u32[]{:S(2)}, u32[]{:S(2)}) collective-permute-start(f32[5,64,128]{2,1,0:T(8,128)S(1)} %get-tuple-element.65), channel_id=1, source_target_pairs={{0,3},{1,0},{2,1},{3,2},{4,7},{5,4},{6,5},{7,6},{8,11},{9,8},{10,9... | collective-permute-start | bytes 491528 | tf_op jit(solution)/shard_map/ppermute | solution.py:622
  13.0 14.4 %collective-permute-start = (f32[2,5,64,128]{3,2,1,0:T(8,128)S(1)}, f32[2,5,64,128]{3,2,1,0:T(8,128)S(1)}, u32[]{:S(2)}, u32[]{:S(2)}) collective-permute-start(f32[2,5,64,128]{3,2,1,0:T(8,128)S(1)} %get-tuple-element.49), channel_id=1, source_target_pairs={{0,8},{8,0},{16,24},{24,16},{1,9},{9,1},{17,25},{25,17},{2,10},{10... | collective-permute-start | bytes 983048 | tf_op jit(solution)/shard_map/ppermute | solution.py:699
  17.4 4.7 %copy-start = (bf16[512,256]{1,0:T(8,128)(2,1)S(1)}, bf16[512,256]{1,0:T(8,128)(2,1)}, u32[]{:S(2)}) copy-start(bf16[512,256]{1,0:T(8,128)(2,1)} %constant.2.clone.table) | copy-start | bytes 786436
  17.9 14.6 %collective-permute-start.7 = (f32[2,5,64,128]{3,2,1,0:T(8,128)S(1)}, f32[2,5,64,128]{3,2,1,0:T(8,128)S(1)}, u32[]{:S(2)}, u32[]{:S(2)}) collective-permute-start(f32[2,5,64,128]{3,2,1,0:T(8,128)S(1)} %get-tuple-element.79), channel_id=1, source_target_pairs={{0,16},{8,24},{16,0},{24,8},{1,17},{9,25},{17,1},{25,9},{2,18},{10... | collective-permute-start | bytes 983048 | tf_op jit(solution)/shard_map/ppermute | solution.py:622
  23.1 10.7 %collective-permute-start.5 = (f32[2,5,64,128]{3,2,1,0:T(8,128)S(1)}, f32[2,5,64,128]{3,2,1,0:T(8,128)S(1)}, u32[]{:S(2)}, u32[]{:S(2)}) collective-permute-start(f32[2,5,64,128]{3,2,1,0:T(8,128)S(1)} %get-tuple-element.75), channel_id=1, source_target_pairs={{0,8},{8,0},{16,24},{24,16},{1,9},{9,1},{17,25},{25,17},{2,10},{10... | collective-permute-start | bytes 983048 | tf_op jit(solution)/shard_map/ppermute | solution.py:722
  27.5 5.4 %collective-permute-start.6 = (f32[5,64,128]{2,1,0:T(8,128)S(1)}, f32[5,64,128]{2,1,0:T(8,128)S(1)}, u32[]{:S(2)}, u32[]{:S(2)}) collective-permute-start(f32[5,64,128]{2,1,0:T(8,128)S(1)} %get-tuple-element.78), channel_id=1, source_target_pairs={{0,16},{8,24},{16,0},{24,8},{1,17},{9,25},{17,1},{25,9},{2,18},{10... | collective-permute-start | bytes 491528 | tf_op jit(solution)/shard_map/ppermute | solution.py:622
  28.0 25.9 %collective-permute-start.8 = (f32[3,5,64,128]{3,2,1,0:T(8,128)S(1)}, f32[3,5,64,128]{3,2,1,0:T(8,128)S(1)}, u32[]{:S(2)}, u32[]{:S(2)}) collective-permute-start(f32[3,5,64,128]{3,2,1,0:T(8,128)S(1)} %get-tuple-element.86), channel_id=1, source_target_pairs={{0,8},{8,0},{16,24},{24,16},{1,9},{9,1},{17,25},{25,17},{2,10},{10... | collective-permute-start | bytes 1474568 | tf_op jit(solution)/shard_map/ppermute | solution.py:723
  34.0 21.5 %collective-permute-start.10 = (f32[3,5,64,128]{3,2,1,0:T(8,128)S(1)}, f32[3,5,64,128]{3,2,1,0:T(8,128)S(1)}, u32[]{:S(2)}, u32[]{:S(2)}) collective-permute-start(f32[3,5,64,128]{3,2,1,0:T(8,128)S(1)} %get-tuple-element.95), channel_id=1, source_target_pairs={{0,24},{8,16},{16,8},{24,0},{1,25},{9,17},{17,9},{25,1},{2,26},{10... | collective-permute-start | bytes 1474568 | tf_op jit(solution)/shard_map/ppermute | solution.py:759
  35.5 18.4 %collective-permute-start.9 = (f32[2,5,64,128]{3,2,1,0:T(8,128)S(1)}, f32[2,5,64,128]{3,2,1,0:T(8,128)S(1)}, u32[]{:S(2)}, u32[]{:S(2)}) collective-permute-start(f32[2,5,64,128]{3,2,1,0:T(8,128)S(1)} %get-tuple-element.89), channel_id=1, source_target_pairs={{0,16},{8,24},{16,0},{24,8},{1,17},{9,25},{17,1},{25,9},{2,18},{10... | collective-permute-start | bytes 983048 | tf_op jit(solution)/shard_map/ppermute | solution.py:622

commit v4 on v3

--- a/solution.py
+++ b/solution.py
@@ -425,12 +425,12 @@
                 pad[v, 8 + 8 * t : 16 + 8 * t] = g[v]
                 dz = along_lanes(h[v])
                 dz = dz + jnp.where(edge_lane, roll(fix[group, v, at], turn), 0.0)
-                part[v, x, at] = section_a * inc[v, x, at] + scale * dz
+                part[v, x, at] = dz
         for t in range(ny // 8):
             at = slice(8 * t, 8 * t + 8)
             for v in range(5):
                 dy = around(lambda n, v=v, t=t: pad[v, 8 + 8 * t + n : 16 + 8 * t + n])
-                part[v, x, at] = part[v, x, at] + scale * dy
+                part[v, x, at] = section_a * inc[v, x, at] + scale * (part[v, x, at] + dy)
         return 0
 
     blocks.each(one_row, some)
@@ -490,13 +490,13 @@
         before = low if x == 0 else f[x - 1]
         after = high if x == nx - 1 else f[x + 1]
         e = e_all[x]
-        deriv = X["kappa"] * (after - before) + X["deriv"] * e
-        value = part_at[x][0][v, part_at[x][1], at] - time_step * deriv
+        deriv = (time_step * X["kappa"]) * (after - before) + (time_step * X["deriv"]) * e
+        value = part_at[x][0][v, part_at[x][1], at] - deriv
         new_inc[v, x, at] = value
         if x in (0, nx - 1):
             edges[x // (nx - 1), v, at] = value
         total = (1.0 - X["band_q"][0] - X["own"]) * q[x] - X["slow"] * e
-        total = total - (section_b * time_step) * deriv
+        total = total - section_b * deriv
         for n in range(1, 4):
             near = [q[i] for i in (x - n, x + n) if 0 <= i < nx]
             total = total - X["band_q"][n] * (near[0] if len(near) == 1 else near[0] + near[1])

time: 57.1 us -> 57.1 us (level)
  no operation moved by 1% of the time
where the time goes in v4:
time: 57.1 us; the launch traced here: 56.9 us
  Pallas kernels  39.6 us (69%)
  starting transfers between devices  14.7 us (26%)
  waiting for transfers between devices  1.73 us (3%)
  between operations  0.79 us (1%)
    pallas_call x13, Pallas kernels, call(): pl.pallas_call(kernel, in_specs=[place[i < hbm] for i in range(len(inputs...  39.6 us
    ppermute x6, starting transfers between devices, shifted(): lax.ppermute(value, axis, [(i, (i + by) % size) for i in range(size)])  8.48 us
    ppermute x1, starting transfers between devices, on_device(): d_came = lax.ppermute(d_out, 'gx', partner)  2.56 us
    ppermute x1, starting transfers between devices, on_device(): sums_came = lax.ppermute(sums, 'gx', partner)  1.56 us
    ppermute x1, starting transfers between devices, on_device(): w_other = lax.ppermute(w_to_other, 'gx', other)  1.5 us
  transfers between devices with their start and end apart: 11, of which 3 were waited for; matrix products, arithmetic and copies ran while one was open for 0% of the time, Pallas kernels for 58%

profile of v4, /device:TPU:0, one launch (start us, length us, event | category | flops | bytes accessed | tf_op | source)
XLA Modules:
  0.0 56.9 jit_solution(7851525005919808963)
XLA Ops:
  0.6 5.5 %faces.1 = (f32[2,5,64,128]{3,2,1,0:T(8,128)S(1)}, f32[2,5,64,128]{3,2,1,0:T(8,128)S(1)}, f32[2,5,64,128]{3,2,1,0:T(8,128)S(1)}, f32[8,5,64,128]{3,2,1,0:T(8,128...) custom-call(f32[24,64,128]{2,1,0:T(8,128)} %rho_hbm.11, ...), custom_call_target="tpu_custom_call" | custom-call | flops 1000 | bytes 1000 | tf_op jit(solution)/shard_map/faces/pallas_call | solution.py:642
  6.1 0.5 collective-permute-start.1
  6.7 2.6 %collective-permute-start.2 = (f32[2,5,64,128]{3,2,1,0:T(8,128)S(1)}, f32[2,5,64,128]{3,2,1,0:T(8,128)S(1)}, u32[]{:S(2)}, u32[]{:S(2)}) collective-permute-start(f32[2,5,64,128]{3,2,1,0:T(8,128)S(1)} %get-tuple-element.58), channel_id=1, source_target_pairs={{0,8},{8,0},{16,24},{24,16},{1,9},{9,1},{17,25},{25,17},{2,10},{10... | collective-permute-start | bytes 983048 | tf_op jit(solution)/shard_map/ppermute | solution.py:698
  9.2 1.6 %collective-permute-start.3 = (f32[5,64,128]{2,1,0:T(8,128)S(1)}, f32[5,64,128]{2,1,0:T(8,128)S(1)}, u32[]{:S(2)}, u32[]{:S(2)}) collective-permute-start(f32[5,64,128]{2,1,0:T(8,128)S(1)} %get-tuple-element.64), channel_id=1, source_target_pairs={{0,1},{1,2},{2,3},{3,0},{4,5},{5,6},{6,7},{7,4},{8,9},{9,10},{10,1... | collective-permute-start | bytes 491528 | tf_op jit(solution)/shard_map/ppermute | solution.py:622
  10.8 2.2 %collective-permute-start.4 = (f32[5,64,128]{2,1,0:T(8,128)S(1)}, f32[5,64,128]{2,1,0:T(8,128)S(1)}, u32[]{:S(2)}, u32[]{:S(2)}) collective-permute-start(f32[5,64,128]{2,1,0:T(8,128)S(1)} %get-tuple-element.65), channel_id=1, source_target_pairs={{0,3},{1,0},{2,1},{3,2},{4,7},{5,4},{6,5},{7,6},{8,11},{9,8},{10,9... | collective-permute-start | bytes 491528 | tf_op jit(solution)/shard_map/ppermute | solution.py:622
  13.0 0.3 collective-permute-start
  13.4 4.1 %base.1 = (f32[2,5,64,128]{3,2,1,0:T(8,128)S(1)}, f32[3,5,64,128]{3,2,1,0:T(8,128)S(1)}, f32[3,5,64,128]{3,2,1,0:T(8,128)S(1)}, f32[8,128]{1,0:T(8,128)S(1)}) custom-call(f32[24,64,128]{2,1,0:T(8,128)} %rho_hbm.11, f32[3,24,64,128]{3,2,1,0:T(8,128)} %mom_hbm.11, f32[24,64,128]{2,1,0:T(8,128)} %ene_hbm.11, f32[5,24,64,128]{3,2,1,0:T(8,128)} %inc_hbm.7, ...), custom_call_target="tpu_custom_call" | custom-call | flops 1000 | bytes 1000 | tf_op jit(solution)/shard_map/base/pallas_call | solution.py:642
  17.4 0.3 collective-permute-done.2.came
  17.9 2.0 %collective-permute-start.7 = (f32[2,5,64,128]{3,2,1,0:T(8,128)S(1)}, f32[2,5,64,128]{3,2,1,0:T(8,128)S(1)}, u32[]{:S(2)}, u32[]{:S(2)}) collective-permute-start(f32[2,5,64,128]{3,2,1,0:T(8,128)S(1)} %get-tuple-element.79), channel_id=1, source_target_pairs={{0,16},{8,24},{16,0},{24,8},{1,17},{9,25},{17,1},{25,9},{2,18},{10... | collective-permute-start | bytes 983048 | tf_op jit(solution)/shard_map/ppermute | solution.py:622
  19.9 2.2 %early.1 = (f32[2,5,64,128]{3,2,1,0:T(8,128)S(1)}, f32[3,5,64,128]{3,2,1,0:T(8,128)S(1)}, f32[3,5,64,128]{3,2,1,0:T(8,128)S(1)}) custom-call(f32[2,5,64,128]{3,2,1,0:T(8,128)S(1)} %get-tuple-element.52.base, f32[3,5,64,128]{3,2,1,0:T(8,128)S(1)} %get-tuple-element.53.w_up0, f32[3,5,64,128]{3,2,1,0:T(8,128)S(1)} %get-tuple-element.54.w_down0, ...), custom_call_target="tpu_custom_call" | custom-call | flops 1000 | bytes 1000 | tf_op jit(solution)/shard_map/early/pallas_call | solution.py:642
  22.1 1.0 %ends.1 = (f32[2,5,64,128]{3,2,1,0:T(8,128)S(1)}, f32[2,5,64,128]{3,2,1,0:T(8,128)S(1)}, f32[3,5,64,128]{3,2,1,0:T(8,128)S(1)}, f32[3,5,64,128]{3,2,1,0:T(8,128)...) custom-call(f32[2,5,64,128]{3,2,1,0:T(8,128)S(1)} %get-tuple-element.61.sums0, ...), custom_call_target="tpu_custom_call" | custom-call | flops 1000 | bytes 1000 | tf_op jit(solution)/shard_map/ends/pallas_call | solution.py:642
  23.1 1.6 %collective-permute-start.5 = (f32[2,5,64,128]{3,2,1,0:T(8,128)S(1)}, f32[2,5,64,128]{3,2,1,0:T(8,128)S(1)}, u32[]{:S(2)}, u32[]{:S(2)}) collective-permute-start(f32[2,5,64,128]{3,2,1,0:T(8,128)S(1)} %get-tuple-element.75), channel_id=1, source_target_pairs={{0,8},{8,0},{16,24},{24,16},{1,9},{9,1},{17,25},{25,17},{2,10},{10... | collective-permute-start | bytes 983048 | tf_op jit(solution)/shard_map/ppermute | solution.py:722
  24.7 2.7 %part0.1 = (f32[5,4,64,128]{3,2,1,0:T(8,128)S(1)}, f32[8,128]{1,0:T(8,128)S(1)}) custom-call(f32[24,64,128]{2,1,0:T(8,128)} %rho_hbm.11, f32[3,24,64,128]{3,2,1,0:T(8,128)} %mom_hbm.11, f32[24,64,128]{2,1,0:T(8,128)} %ene_hbm.11, f32[5,24,64,128]{3,2,1,0:T(8,128)} %inc_hbm.7, f32[5,26,8,128]{3,2,1,0:T(8,128)S(1)} %collective-permute-done.1.y_halo, ...), custom_call_target="tpu_custom_call" | custom-call | flops 1000 | bytes 1000 | tf_op jit(solution)/shard_map/part0/pallas_call | solution.py:642
  27.5 0.6 %collective-permute-start.6 = (f32[5,64,128]{2,1,0:T(8,128)S(1)}, f32[5,64,128]{2,1,0:T(8,128)S(1)}, u32[]{:S(2)}, u32[]{:S(2)}) collective-permute-start(f32[5,64,128]{2,1,0:T(8,128)S(1)} %get-tuple-element.78), channel_id=1, source_target_pairs={{0,16},{8,24},{16,0},{24,8},{1,17},{9,25},{17,1},{25,9},{2,18},{10... | collective-permute-start | bytes 491528 | tf_op jit(solution)/shard_map/ppermute | solution.py:622
  28.0 0.3 collective-permute-start.8
  28.4 4.1 %part4.1 = (f32[5,8,64,128]{3,2,1,0:T(8,128)S(1)}, f32[8,128]{1,0:T(8,128)S(1)}) custom-call(f32[24,64,128]{2,1,0:T(8,128)} %rho_hbm.11, f32[3,24,64,128]{3,2,1,0:T(8,128)} %mom_hbm.11, f32[24,64,128]{2,1,0:T(8,128)} %ene_hbm.11, f32[5,24,64,128]{3,2,1,0:T(8,128)} %inc_hbm.7, f32[5,26,8,128]{3,2,1,0:T(8,128)S(1)} %collective-permute-done.1.y_halo, ...), custom_call_target="tpu_custom_call" | custom-call | flops 1000 | bytes 1000 | tf_op jit(solution)/shard_map/part4/pallas_call | solution.py:642
  32.5 0.4 collective-permute-done.6.rest_1_
  32.8 1.0 %collective-permute-done.5.came = f32[2,5,64,128]{3,2,1,0:T(8,128)S(1)} collective-permute-done((f32[2,5,64,128]{3,2,1,0:T(8,128)S(1)}, f32[2,5,64,128]{3,2,1,0:T(8,128)S(1)}, u32[]{:S(2)}, u32[]{:S(2)}) %collective-permute-start.5) | collective-permute-done | bytes 327712 | tf_op jit(solution)/shard_map/ppermute | solution.py:722
  34.0 1.5 %collective-permute-start.10 = (f32[3,5,64,128]{3,2,1,0:T(8,128)S(1)}, f32[3,5,64,128]{3,2,1,0:T(8,128)S(1)}, u32[]{:S(2)}, u32[]{:S(2)}) collective-permute-start(f32[3,5,64,128]{3,2,1,0:T(8,128)S(1)} %get-tuple-element.95), channel_id=1, source_target_pairs={{0,24},{8,16},{16,8},{24,0},{1,25},{9,17},{17,9},{25,1},{2,26},{10... | collective-permute-start | bytes 1474568 | tf_op jit(solution)/shard_map/ppermute | solution.py:759
  35.5 1.5 %collective-permute-start.9 = (f32[2,5,64,128]{3,2,1,0:T(8,128)S(1)}, f32[2,5,64,128]{3,2,1,0:T(8,128)S(1)}, u32[]{:S(2)}, u32[]{:S(2)}) collective-permute-start(f32[2,5,64,128]{3,2,1,0:T(8,128)S(1)} %get-tuple-element.89), channel_id=1, source_target_pairs={{0,16},{8,24},{16,0},{24,8},{1,17},{9,25},{17,1},{25,9},{2,18},{10... | collective-permute-start | bytes 983048 | tf_op jit(solution)/shard_map/ppermute | solution.py:622
  37.0 6.1 %part12.1 = (f32[5,12,64,128]{3,2,1,0:T(8,128)S(1)}, f32[8,128]{1,0:T(8,128)}) custom-call(f32[24,64,128]{2,1,0:T(8,128)} %rho_hbm.11, f32[3,24,64,128]{3,2,1,0:T(8,128)} %mom_hbm.11, f32[24,64,128]{2,1,0:T(8,128)} %ene_hbm.11, f32[5,24,64,128]{3,2,1,0:T(8,128)} %inc_hbm.7, f32[5,26,8,128]{3,2,1,0:T(8,128)S(1)} %collective-permute-done.1.y_halo, ...), custom_call_target="tpu_custom_call" | custom-call | flops 1000 | bytes 1000 | tf_op jit(solution)/shard_map/part12/pallas_call | solution.py:642
  43.2 10.7 %lines.1 = (f32[5,24,64,128]{3,2,1,0:T(8,128)}, f32[5,24,64,128]{3,2,1,0:T(8,128)S(1)}, f32[2,5,64,128]{3,2,1,0:T(8,128)S(1)}) custom-call(f32[24,64,128]{2,1,0:T(8,128)} %rho_hbm.11, f32[3,24,64,128]{3,2,1,0:T(8,128)} %mom_hbm.11, f32[24,64,128]{2,1,0:T(8,128)} %ene_hbm.11, f32[5,64,128]{2,1,0:T(8,128)S(1)} %get-tuple-element.70.f_near, ...), custom_call_target="tpu_custom_call" | custom-call | flops 1000 | bytes 1000 | tf_op jit(solution)/shard_map/lines/pallas_call | solution.py:642
  53.9 1.6 %inner.1 = (f32[5,24,64,128]{3,2,1,0:T(8,128)}, f32[8,5,64,128]{3,2,1,0:T(8,128)S(1)}) custom-call(f32[5,24,64,128]{3,2,1,0:T(8,128)S(1)} %get-tuple-element.85.local, f32[3,5,64,128]{3,2,1,0:T(8,128)S(1)} %collective-permute-done.8.w_partner, f32[2,5,64,128]{3,2,1,0:T(8,128)S(1)} %get-tuple-element.87.rest_0_, ...), custom_call_target="tpu_custom_call" | custom-call | flops 1000 | bytes 1000 | tf_op jit(solution)/shard_map/inner/pallas_call | solution.py:642
  55.5 1.4 %rim.1 = (f32[5,24,64,128]{3,2,1,0:T(8,128)}, f32[5,24,64,128]{3,2,1,0:T(8,128)}) custom-call(f32[5,24,64,128]{3,2,1,0:T(8,128)} %get-tuple-element.90.before, f32[5,24,64,128]{3,2,1,0:T(8,128)} %get-tuple-element.91.inc_before, f32[8,5,64,128]{3,2,1,0:T(8,128)S(1)} %get-tuple-element.92.rim, ...), custom_call_target="tpu_custom_call", output_to_operand_aliasing={{0}: (0, {}), {1}: (1, {})} | custom-call | flops 1000 | bytes 1000 | tf_op jit(solution)/shard_map/rim/pallas_call | solution.py:642
  (13 shorter events, 0.3 us)
Async XLA Ops:
  6.1 13.8 %collective-permute-start.1 = (f32[5,26,8,128]{3,2,1,0:T(8,128)S(1)}, f32[5,26,8,128]{3,2,1,0:T(8,128)S(1)}, u32[]{:S(2)}, u32[]{:S(2)}) collective-permute-start(f32[5,26,8,128]{3,2,1,0:T(8,128)S(1)} %get-tuple-element.50), channel_id=1, source_target_pairs={{0,4},{4,0},{1,5},{5,1},{2,6},{6,2},{3,7},{7,3},{8,12},{12,8},{9,1... | collective-permute-start | bytes 1597448 | tf_op jit(solution)/shard_map/ppermute | solution.py:622
  6.7 11.1 %collective-permute-start.2 = (f32[2,5,64,128]{3,2,1,0:T(8,128)S(1)}, f32[2,5,64,128]{3,2,1,0:T(8,128)S(1)}, u32[]{:S(2)}, u32[]{:S(2)}) collective-permute-start(f32[2,5,64,128]{3,2,1,0:T(8,128)S(1)} %get-tuple-element.58), channel_id=1, source_target_pairs={{0,8},{8,0},{16,24},{24,16},{1,9},{9,1},{17,25},{25,17},{2,10},{10... | collective-permute-start | bytes 983048 | tf_op jit(solution)/shard_map/ppermute | solution.py:698
  9.2 12.9 %collective-permute-start.3 = (f32[5,64,128]{2,1,0:T(8,128)S(1)}, f32[5,64,128]{2,1,0:T(8,128)S(1)}, u32[]{:S(2)}, u32[]{:S(2)}) collective-permute-start(f32[5,64,128]{2,1,0:T(8,128)S(1)} %get-tuple-element.64), channel_id=1, source_target_pairs={{0,1},{1,2},{2,3},{3,0},{4,5},{5,6},{6,7},{7,4},{8,9},{9,10},{10,1... | collective-permute-start | bytes 491528 | tf_op jit(solution)/shard_map/ppermute | solution.py:622
  10.8 11.3 %collective-permute-start.4 = (f32[5,64,128]{2,1,0:T(8,128)S(1)}, f32[5,64,128]{2,1,0:T(8,128)S(1)}, u32[]{:S(2)}, u32[]{:S(2)}) collective-permute-start(f32[5,64,128]{2,1,0:T(8,128)S(1)} %get-tuple-element.65), channel_id=1, source_target_pairs={{0,3},{1,0},{2,1},{3,2},{4,7},{5,4},{6,5},{7,6},{8,11},{9,8},{10,9... | collective-permute-start | bytes 491528 | tf_op jit(solution)/shard_map/ppermute | solution.py:622
  13.0 14.4 %collective-permute-start = (f32[2,5,64,128]{3,2,1,0:T(8,128)S(1)}, f32[2,5,64,128]{3,2,1,0:T(8,128)S(1)}, u32[]{:S(2)}, u32[]{:S(2)}) collective-permute-start(f32[2,5,64,128]{3,2,1,0:T(8,128)S(1)} %get-tuple-element.49), channel_id=1, source_target_pairs={{0,8},{8,0},{16,24},{24,16},{1,9},{9,1},{17,25},{25,17},{2,10},{10... | collective-permute-start | bytes 983048 | tf_op jit(solution)/shard_map/ppermute | solution.py:699
  17.4 4.7 %copy-start = (bf16[512,256]{1,0:T(8,128)(2,1)S(1)}, bf16[512,256]{1,0:T(8,128)(2,1)}, u32[]{:S(2)}) copy-start(bf16[512,256]{1,0:T(8,128)(2,1)} %constant.2.clone.table) | copy-start | bytes 786436
  17.9 14.6 %collective-permute-start.7 = (f32[2,5,64,128]{3,2,1,0:T(8,128)S(1)}, f32[2,5,64,128]{3,2,1,0:T(8,128)S(1)}, u32[]{:S(2)}, u32[]{:S(2)}) collective-permute-start(f32[2,5,64,128]{3,2,1,0:T(8,128)S(1)} %get-tuple-element.79), channel_id=1, source_target_pairs={{0,16},{8,24},{16,0},{24,8},{1,17},{9,25},{17,1},{25,9},{2,18},{10... | collective-permute-start | bytes 983048 | tf_op jit(solution)/shard_map/ppermute | solution.py:622
  23.1 10.7 %collective-permute-start.5 = (f32[2,5,64,128]{3,2,1,0:T(8,128)S(1)}, f32[2,5,64,128]{3,2,1,0:T(8,128)S(1)}, u32[]{:S(2)}, u32[]{:S(2)}) collective-permute-start(f32[2,5,64,128]{3,2,1,0:T(8,128)S(1)} %get-tuple-element.75), channel_id=1, source_target_pairs={{0,8},{8,0},{16,24},{24,16},{1,9},{9,1},{17,25},{25,17},{2,10},{10... | collective-permute-start | bytes 983048 | tf_op jit(solution)/shard_map/ppermute | solution.py:722
  27.5 5.4 %collective-permute-start.6 = (f32[5,64,128]{2,1,0:T(8,128)S(1)}, f32[5,64,128]{2,1,0:T(8,128)S(1)}, u32[]{:S(2)}, u32[]{:S(2)}) collective-permute-start(f32[5,64,128]{2,1,0:T(8,128)S(1)} %get-tuple-element.78), channel_id=1, source_target_pairs={{0,16},{8,24},{16,0},{24,8},{1,17},{9,25},{17,1},{25,9},{2,18},{10... | collective-permute-start | bytes 491528 | tf_op jit(solution)/shard_map/ppermute | solution.py:622
  28.0 25.8 %collective-permute-start.8 = (f32[3,5,64,128]{3,2,1,0:T(8,128)S(1)}, f32[3,5,64,128]{3,2,1,0:T(8,128)S(1)}, u32[]{:S(2)}, u32[]{:S(2)}) collective-permute-start(f32[3,5,64,128]{3,2,1,0:T(8,128)S(1)} %get-tuple-element.86), channel_id=1, source_target_pairs={{0,8},{8,0},{16,24},{24,16},{1,9},{9,1},{17,25},{25,17},{2,10},{10... | collective-permute-start | bytes 1474568 | tf_op jit(solution)/shard_map/ppermute | solution.py:723
  34.0 21.5 %collective-permute-start.10 = (f32[3,5,64,128]{3,2,1,0:T(8,128)S(1)}, f32[3,5,64,128]{3,2,1,0:T(8,128)S(1)}, u32[]{:S(2)}, u32[]{:S(2)}) collective-permute-start(f32[3,5,64,128]{3,2,1,0:T(8,128)S(1)} %get-tuple-element.95), channel_id=1, source_target_pairs={{0,24},{8,16},{16,8},{24,0},{1,25},{9,17},{17,9},{25,1},{2,26},{10... | collective-permute-start | bytes 1474568 | tf_op jit(solution)/shard_map/ppermute | solution.py:759
  35.5 18.4 %collective-permute-start.9 = (f32[2,5,64,128]{3,2,1,0:T(8,128)S(1)}, f32[2,5,64,128]{3,2,1,0:T(8,128)S(1)}, u32[]{:S(2)}, u32[]{:S(2)}) collective-permute-start(f32[2,5,64,128]{3,2,1,0:T(8,128)S(1)} %get-tuple-element.89), channel_id=1, source_target_pairs={{0,16},{8,24},{16,0},{24,8},{1,17},{9,25},{17,1},{25,9},{2,18},{10... | collective-permute-start | bytes 983048 | tf_op jit(solution)/shard_map/ppermute | solution.py:622
